TPU v7x, 32 devices: a whole 2x2x4 slice. The times are simulated.
32 devices in a mesh: req: 8 (over y, x, core), head: 4 (over z).
Axes of the slice: x: 2, y: 2, z: 4, core: 2. Of those that a mesh axis runs over, the one named last changes fastest.
Arguments:
- queries: bfloat16 [256, 8192], P('req', 'head'), may hold values from -64 to 64
- key_new: bfloat16 [256, 1024], P('req', 'head'), may hold values from -6 to 6
- value_new: bfloat16 [256, 1024], P('req', 'head'), may hold values from -6 to 6
- key_pool: bfloat16 [1536, 128, 1024], P('req', None, 'head'), may hold values from -10 to 10
- value_pool: bfloat16 [1536, 128, 1024], P('req', None, 'head'), may hold values from -6 to 6
- page_table: int32 [256, 64], P('req'), may hold values from -1 to 1535, as said below
- lengths: int32 [256], P('req'), may hold values from 1 to 8192, as said below
- residual_in: bfloat16 [256, 8192], P('head', 'req'), may hold values from -3 to 3
- w_out: bfloat16 [8192, 8192], P('head', 'req'), may hold values from -0.5 to 0.5
- norm_gain: bfloat16 [8192], replicated, may hold values from 0.25 to 1.75
- w_gate: bfloat16 [8192, 29568], P(None, ('req', 'head')), may hold values from -0.0625 to 0.0625
- w_up: bfloat16 [8192, 29568], P(None, ('req', 'head')), may hold values from -0.0625 to 0.0625
- w_down: bfloat16 [29568, 8192], P(('req', 'head')), may hold values from -0.0625 to 0.0625
Outputs:
- output: bfloat16 [256, 8192], P('head', 'req')
Inputs may be any that keep to these rules, and one draw needn't show every extreme that they name: `page_table`: entry k of request b is a pool page for k < ceil(lengths[b] / 128) and -1 otherwise; no pool page appears twice in the table. `lengths`: one request holds exactly 8192 cached tokens.
All inputs are finite; a program needn't handle non-finite values.
Results may differ from a plain program's by a relative error of at most 0.009.
Values may be sent and summed in bfloat16 or wider, within the bound.
No kernel may reach another device: no remote copies, remote signals or barrier semaphores. Data moves between devices by JAX's collectives and lax.ppermute only.
A program may use at most 128 MiB of HBM per device.

v0:
```python
import math

import jax
import jax.numpy as jnp
from jax import lax
from jax.sharding import PartitionSpec as P

HEAD_DIM = 128


NEGATIVE_FILL = -1e30
NORM_EPS = 1e-06


def page_partials(all_queries, all_tables, all_lengths, key_pool, value_pool, first_page):
    page_count = key_pool.shape[0]
    page_len = key_pool.shape[1]
    request_count, max_slots = all_tables.shape
    kv_local = key_pool.shape[2] // HEAD_DIM
    heads_local = all_queries.shape[1] // HEAD_DIM
    group_size = heads_local // kv_local
    score_scale = 1.0 / math.sqrt(HEAD_DIM)
    local_ids = all_tables - first_page
    page_index = jnp.arange(page_count, dtype=jnp.int32)
    entry_hits = local_ids[None, :, :] == page_index[:, None, None]
    page_hits = jnp.any(entry_hits, axis=2)
    req_index = jnp.arange(request_count, dtype=jnp.int32)
    slot_index = jnp.arange(max_slots, dtype=jnp.int32)
    page_owner = jnp.max(jnp.where(page_hits, req_index[None, :], -1), axis=1)
    page_slot = jnp.sum(jnp.where(entry_hits, slot_index[None, None, :], 0), axis=(1, 2))
    safe_owner = jnp.maximum(page_owner, 0)
    q_heads = all_queries[safe_owner].reshape(page_count, kv_local, group_size, HEAD_DIM)
    page_keys = key_pool.reshape(page_count, page_len, kv_local, HEAD_DIM)
    page_values = value_pool.reshape(page_count, page_len, kv_local, HEAD_DIM)
    scores = (
        jnp.einsum("pkgd,pskd->pkgs", q_heads, page_keys, preferred_element_type=jnp.float32)
        * score_scale
    )
    token_pos = page_slot[:, None] * page_len + jnp.arange(page_len, dtype=jnp.int32)[None, :]
    is_valid = (page_owner[:, None] >= 0) & (token_pos < all_lengths[safe_owner][:, None])
    is_valid = is_valid[:, None, None, :]
    masked = jnp.where(is_valid, scores, NEGATIVE_FILL)
    page_max = jnp.max(masked, axis=3)
    weights = jnp.where(is_valid, jnp.exp(masked - page_max[..., None]), 0.0).astype(jnp.bfloat16)
    page_sum = jnp.sum(weights.astype(jnp.float32), axis=3).reshape(page_count, heads_local)
    page_acc = jnp.einsum(
        "pkgs,pskd->pkgd", weights, page_values, preferred_element_type=jnp.float32
    )
    page_acc = page_acc.reshape(page_count, heads_local, HEAD_DIM)
    page_max = page_max.reshape(page_count, heads_local)
    req_max = jnp.max(jnp.where(page_hits[:, :, None], page_max[:, None, :], NEGATIVE_FILL), axis=0)
    factor = jnp.exp(page_max - req_max[safe_owner])
    one_hot = page_hits.astype(jnp.float32)
    req_sum = jnp.dot(one_hot.T, factor * page_sum, precision=lax.Precision.HIGHEST)
    scaled_acc = (factor[..., None] * page_acc).reshape(page_count, heads_local * HEAD_DIM)
    req_acc = jnp.dot(one_hot.T, scaled_acc, precision=lax.Precision.HIGHEST)
    return (req_max, req_sum, req_acc)


def shards(
    queries,
    key_new,
    value_new,
    key_pool,
    value_pool,
    page_table,
    lengths,
    residual_in,
    w_out,
    norm_gain,
    w_gate,
    w_up,
    w_down,
):
    req_devices = lax.axis_size("req")
    local_reqs = queries.shape[0]
    heads_local = queries.shape[1] // HEAD_DIM
    kv_local = key_new.shape[1] // HEAD_DIM
    group_size = heads_local // kv_local
    score_scale = 1.0 / math.sqrt(HEAD_DIM)
    all_queries, all_tables, all_lengths = (
        lax.all_gather(queries, "req", axis=0, tiled=True),
        lax.all_gather(page_table, "req", axis=0, tiled=True),
        lax.all_gather(lengths, "req", axis=0, tiled=True),
    )
    first_page = lax.axis_index("req") * key_pool.shape[0]
    req_max, req_sum, req_acc = page_partials(
        all_queries, all_tables, all_lengths, key_pool, value_pool, first_page
    )
    got_max, got_sum, got_acc = (
        lax.all_to_all(req_max, "req", split_axis=0, concat_axis=0, tiled=True),
        lax.all_to_all(req_sum, "req", split_axis=0, concat_axis=0, tiled=True),
        lax.all_to_all(req_acc, "req", split_axis=0, concat_axis=0, tiled=True),
    )
    got_max = got_max.reshape(req_devices, local_reqs, heads_local)
    got_sum = got_sum.reshape(req_devices, local_reqs, heads_local)
    got_acc = got_acc.reshape(req_devices, local_reqs, heads_local, HEAD_DIM)
    q_heads = queries.reshape(local_reqs, kv_local, group_size, HEAD_DIM)
    own_score = jnp.einsum(
        "rkgd,rkd->rkg",
        q_heads,
        key_new.reshape(local_reqs, kv_local, HEAD_DIM),
        preferred_element_type=jnp.float32,
    )
    own_score = own_score.reshape(local_reqs, heads_local) * score_scale
    top_score = jnp.maximum(jnp.max(got_max, axis=0), own_score)
    source_factor = jnp.exp(got_max - top_score[None])
    own_factor = jnp.exp(own_score - top_score)
    weight_total = jnp.sum(source_factor * got_sum, axis=0) + own_factor
    own_values = jnp.broadcast_to(
        value_new.reshape(local_reqs, kv_local, 1, HEAD_DIM).astype(jnp.float32),
        (local_reqs, kv_local, group_size, HEAD_DIM),
    )
    own_values = own_values.reshape(local_reqs, heads_local, HEAD_DIM)
    accum = jnp.sum(source_factor[..., None] * got_acc, axis=0) + own_factor[..., None] * own_values
    attention = (
        (accum / weight_total[..., None])
        .reshape(local_reqs, heads_local * HEAD_DIM)
        .astype(jnp.bfloat16)
    )
    projected = jnp.dot(
        lax.all_gather(attention, "req", axis=0, tiled=True),
        w_out,
        preferred_element_type=jnp.float32,
    )
    head_total = lax.psum_scatter(projected, "head", scatter_dimension=0, tiled=True)
    state = (residual_in.astype(jnp.float32) + head_total).astype(jnp.bfloat16)
    full_state = lax.all_gather(state, "req", axis=1, tiled=True)
    state_wide = full_state.astype(jnp.float32)
    mean_square = jnp.mean(state_wide * state_wide, axis=1, keepdims=True)
    normed = (
        state_wide * lax.rsqrt(mean_square + NORM_EPS) * norm_gain.astype(jnp.float32)[None, :]
    ).astype(jnp.bfloat16)
    row_piece = lax.all_gather(normed, "head", axis=0, tiled=True)
    gate_proj = jnp.dot(row_piece, w_gate, preferred_element_type=jnp.float32)
    up_proj = jnp.dot(row_piece, w_up, preferred_element_type=jnp.float32)
    hidden = (jax.nn.silu(gate_proj) * up_proj).astype(jnp.bfloat16)
    row_total = lax.psum_scatter(
        jnp.dot(hidden, w_down, preferred_element_type=jnp.float32),
        "head",
        scatter_dimension=0,
        tiled=True,
    )
    down_sum = lax.psum_scatter(row_total, "req", scatter_dimension=1, tiled=True)
    return (state.astype(jnp.float32) + down_sum).astype(jnp.bfloat16)


def solution(mesh):
    return jax.shard_map(
        shards,
        mesh=mesh,
        in_specs=(
            P("req", "head"),
            P("req", "head"),
            P("req", "head"),
            P("req", None, "head"),
            P("req", None, "head"),
            P("req", None),
            P("req"),
            P("head", "req"),
            P("head", "req"),
            P(),
            P(None, ("req", "head")),
            P(None, ("req", "head")),
            P(("req", "head"), None),
        ),
        out_specs=P("head", "req"),
        check_vma=False,
    )
```

profile of v0, /device:TPU:0, one launch (start us, length us, event | category | flops | bytes accessed | tf_op | source)
XLA Modules:
  0.0 509.2 jit_solution(5940896341228771041)
XLA Ops:
  7.3 10.8 %all_gather.18 = s32[256,64]{1,0:T(8,128)S(1)} all-gather(s32[32,64]{1,0:T(8,128)} %param.18), channel_id=1, replica_groups=mesh['req'=8,'head'=4] {'req'}, dimensions={0}, use_global_device_ids=true | all-gather | bytes 73728 | tf_op jit(solution)/shard_map/all_gather | solution.py:83
  18.2 3.8 fusion.6
  24.9 7.2 %all-reduce = s32[256]{0:T(256)S(1)} all-reduce(s32[256]{0:T(256)S(1)} %dynamic-update-slice), channel_id=1, replica_groups=mesh['req'=8,'head'=4] {'req'}, use_global_device_ids=true, to_apply=%add | all-reduce | flops 256 | bytes 2048
  33.9 3.5 select_reduce_fusion
  37.6 3.3 gather_fusion.1
  41.0 9.4 %fusion.27 = (f32[192,2,8]{2,1,0:T(2,128)S(1)}, f32[192,2,8,128]{3,2,1,0:T(8,128)S(1)}) fusion(bf16[192,2,8,128]{3,2,1,0:T(8,128)(2,1)S(1)} %bitcast.120, pred[192,128]{1,0:T(8,128)(4,1)S(1)} %fusion.17, bf16[192,128,256]{2,1,0:T(8,128)(2,1)} %param.16), kind=kOutput, calls=%fused_computation.54 | convolution fusion | flops 101839872 | bytes 14979072 | tf_op jit(solution)/shard_map/pkgd,pskd->pkgs/dot_general | solution.py:36
  52.0 4.0 all-to-all-start
  58.1 6.9 %bitcast_multiply_fusion = f32[192,16,128]{2,1,0:T(8,128)S(1)} fusion(f32[192,16]{1,0:T(8,128)S(1)} %copy.117, f32[192,2,8,128]{3,2,1,0:T(8,128)S(1)} %get-tuple-element.10, f32[192,2,8]{2,1,0:T(2,128)S(1)} %get-tuple-element.9, pred[192,128]{1,0:T(8,128)(4,1)} %copy-done.2, bf16[192,128,256]{2,1,0:T(8,128)(2,1)} %param.17), kind=kOutput, calls=%fused_computation.19 | convolution fusion | flops 102236160 | bytes 15777792 | tf_op jit(solution)/shard_map/pkgs,pskd->pkgd/dot_general | solution.py:46
  66.4 4.1 all-to-all-start.2
  70.5 2.4 fusion.32
  73.0 2.3 all-to-all-done.2
  75.3 3.6 all-to-all-start.1
  84.6 2.7 mul.130
  87.3 18.2 %all-to-all-done.1 = f32[8,32,2048]{2,1,0:T(8,128)S(1)} async-done(((f32[8,32,2048]{2,1,0:T(8,128)}), f32[8,32,2048]{2,1,0:T(8,128)S(1)}, u32[]{:S(2)}, u32[]{:S(2)}) %all-to-all-start.1) | async-done | bytes 2097184 | tf_op jit(solution)/shard_map/all_to_all | solution.py:93
  108.6 23.0 %all-gather.7.cloned.1.call-done = bf16[256,2048]{1,0:T(8,128)(2,1)} async-done(((bf16[32,2048]{1,0:T(8,128)(2,1)}), bf16[256,2048]{1,0:T(8,128)(2,1)}) %all-gather.7.cloned.1.call-update) | async-done | bytes 1048592 | tf_op jit(solution)/shard_map/all_gather | solution.py:122
  131.6 4.8 fusion.33
  136.4 27.2 %reduce-scatter.4.cloned.1.call-done = f32[64,1024]{1,0:T(8,128)} async-done(((f32[256,1024]{1,0:T(8,128)}), f32[64,1024]{1,0:T(8,128)}) %reduce-scatter.4.cloned.1.call-update) | async-done | bytes 262160 | tf_op jit(solution)/shard_map/reduce_scatter | solution.py:126
  165.4 22.4 %all-gather.9.cloned.1.call-done = bf16[64,8192]{1,0:T(8,128)(2,1)} async-done(((bf16[64,1024]{1,0:T(8,128)(2,1)}), bf16[64,8192]{1,0:T(8,128)(2,1)}) %all-gather.9.cloned.1.call-update) | async-done | bytes 1048592 | tf_op jit(solution)/shard_map/all_gather | solution.py:128
  189.3 2.5 fusion.9
  191.9 80.9 %all-gather.11.cloned.1.call-done = bf16[256,8192]{1,0:T(8,128)(2,1)} async-done(((bf16[64,8192]{1,0:T(8,128)(2,1)}), bf16[256,8192]{1,0:T(8,128)(2,1)}) %all-gather.11.cloned.1.call-update) | async-done | bytes 4194320 | tf_op jit(solution)/shard_map/all_gather | solution.py:134
  272.8 8.7 %fusion.34 = f32[256,924]{0,1:T(8,128)S(1)} fusion(bf16[256,8192]{1,0:T(8,128)(2,1)} %all-gather.11.cloned.1.call-done, bf16[8192,924]{0,1:T(8,128)(2,1)} %param.23), kind=kOutput, calls=%fused_computation.61 | convolution fusion | flops 3875536896 | bytes 20279296 | tf_op jit(solution)/shard_map/dot_general | solution.py:135
  281.5 30.4 %fusion.35 = f32[256,8192]{1,0:T(8,128)} fusion(bf16[924,8192]{1,0:T(8,128)(2,1)} %param.25, bf16[256,8192]{1,0:T(8,128)(2,1)} %all-gather.11.cloned.1.call-done, bf16[8192,924]{0,1:T(8,128)(2,1)} %param.24, f32[256,924]{0,1:T(8,128)S(1)} %fusion.34), kind=kOutput, calls=%fused_computation.62 | convolution fusion | flops 7752493056 | bytes 43806720 | tf_op jit(solution)/shard_map/dot_general | solution.py:139
  311.9 143.1 %reduce-scatter.6.cloned.1.call-done = f32[64,8192]{1,0:T(8,128)} async-done(((f32[256,8192]{1,0:T(8,128)}), f32[64,8192]{1,0:T(8,128)}) %reduce-scatter.6.cloned.1.call-update) | async-done | bytes 2097168 | tf_op jit(solution)/shard_map/reduce_scatter | solution.py:138
  455.1 45.6 %reduce-scatter.8.cloned.1.call-done = f32[64,1024]{1,0:T(8,128)} async-done(((f32[64,8192]{1,0:T(8,128)}), f32[64,1024]{1,0:T(8,128)}) %reduce-scatter.8.cloned.1.call-update) | async-done | bytes 262160 | tf_op jit(solution)/shard_map/reduce_scatter | solution.py:144
  (88 shorter events, 23.9 us)
Async XLA Ops:
  6.5 31.0 %all-gather.5.cloned.1.call-start = ((), (), s32[]{:S(2)}) async-start(), calls=%async_computation.6 | async-start | bytes 1179648 | tf_op jit(solution)/shard_map/all_gather | solution.py:82
  37.5 19.4 %copy-start.2 = (pred[192,128]{1,0:T(8,128)(4,1)}, pred[192,128]{1,0:T(8,128)(4,1)S(1)}, u32[]{:S(2)}) copy-start(pred[192,128]{1,0:T(8,128)(4,1)S(1)} %fusion.17) | copy-start | bytes 73732
  52.0 14.4 %all-to-all-start = ((f32[8,1,512]{2,1,0:T(1,128)}), f32[8,1,512]{2,1,0:T(1,128)}, u32[]{:S(2)}, u32[]{:S(2)}) async-start(f32[8,1,512]{2,1,0:T(1,128)} %reshape.246), calls=%async_computation | async-start | bytes 32768 | tf_op jit(solution)/shard_map/all_to_all | solution.py:91
  66.4 8.9 %all-to-all-start.2 = ((f32[8,1,512]{2,1,0:T(1,128)}), f32[8,1,512]{2,1,0:T(1,128)S(1)}, u32[]{:S(2)}, u32[]{:S(2)}) async-start(f32[8,1,512]{2,1,0:T(1,128)} %reshape.248), calls=%async_computation.2 | async-start | bytes 32768 | tf_op jit(solution)/shard_map/all_to_all | solution.py:92
  70.5 8.6 %copy-start.4 = (bf16[32,256]{1,0:T(8,128)(2,1)S(1)}, bf16[32,256]{1,0:T(8,128)(2,1)}, u32[]{:S(2)}) copy-start(bf16[32,256]{1,0:T(8,128)(2,1)} %param.14) | copy-start | bytes 49156
  70.5 8.7 %copy-start.5 = (bf16[32,256]{1,0:T(8,128)(2,1)S(1)}, bf16[32,256]{1,0:T(8,128)(2,1)}, u32[]{:S(2)}) copy-start(bf16[32,256]{1,0:T(8,128)(2,1)} %param.15) | copy-start | bytes 49156
  70.5 8.7 %copy-start.1 = (bf16[32,2048]{1,0:T(8,128)(2,1)S(1)}, bf16[32,2048]{1,0:T(8,128)(2,1)}, u32[]{:S(2)}) copy-start(bf16[32,2048]{1,0:T(8,128)(2,1)} %param.13) | copy-start | bytes 393220
  75.3 30.2 %all-to-all-start.1 = ((f32[8,32,2048]{2,1,0:T(8,128)}), f32[8,32,2048]{2,1,0:T(8,128)S(1)}, u32[]{:S(2)}, u32[]{:S(2)}) async-start(f32[8,32,2048]{2,1,0:T(8,128)} %fusion.32), calls=%async_computation.1 | async-start | bytes 4194304 | tf_op jit(solution)/shard_map/all_to_all | solution.py:93
  78.9 52.7 %all-gather.7.cloned.1.call-start = ((), (), s32[]{:S(2)}) async-start(), calls=%async_computation.7 | async-start | bytes 1179648 | tf_op jit(solution)/shard_map/all_gather | solution.py:122
  108.5 55.1 %copy-start.3 = (bf16[64,1024]{1,0:T(8,128)(2,1)S(1)}, bf16[64,1024]{1,0:T(8,128)(2,1)}, u32[]{:S(2)}) copy-start(bf16[64,1024]{1,0:T(8,128)(2,1)} %param.20) | copy-start | bytes 393220
  108.5 56.8 %copy-start.6 = (bf16[8192]{0:T(1024)(128)(2,1)S(1)}, bf16[8192]{0:T(1024)(128)(2,1)}, u32[]{:S(2)}) copy-start(bf16[8192]{0:T(1024)(128)(2,1)} %param.22) | copy-start | bytes 49156
  108.6 55.1 %reduce-scatter.4.cloned.1.call-start = ((), (), s32[]{:S(2)}) async-start(), calls=%async_computation.8 | async-start | bytes 1310720 | tf_op jit(solution)/shard_map/reduce_scatter | solution.py:126
  136.3 51.4 %all-gather.9.cloned.1.call-start = ((), (), s32[]{:S(2)}) async-start(), calls=%async_computation.9 | async-start | bytes 1179648 | tf_op jit(solution)/shard_map/all_gather | solution.py:128
  165.3 107.5 %all-gather.11.cloned.1.call-start = ((), (), s32[]{:S(2)}) async-start(), calls=%async_computation.10 | async-start | bytes 5242880 | tf_op jit(solution)/shard_map/all_gather | solution.py:134
  191.9 263.2 %reduce-scatter.6.cloned.1.call-start = ((), (), s32[]{:S(2)}) async-start(), calls=%async_computation.11 | async-start | bytes 10485760 | tf_op jit(solution)/shard_map/reduce_scatter | solution.py:138
  311.9 188.8 %copy-start = (bf16[64,1024]{1,0:T(8,128)(2,1)S(1)}, bf16[64,1024]{1,0:T(8,128)(2,1)}, u32[]{:S(2)}) copy-start(bf16[64,1024]{1,0:T(8,128)(2,1)} %add_convert_fusion.1) | copy-start | bytes 393220
  311.9 188.8 %reduce-scatter.8.cloned.1.call-start = ((), (), s32[]{:S(2)}) async-start(), calls=%async_computation.12 | async-start | bytes 2359296 | tf_op jit(solution)/shard_map/reduce_scatter | solution.py:144
Sparse Core Ops, SparseCore 0:
  9.2 26.2 all-gather.4
  108.6 22.8 all-gather.6
  136.5 27.1 reduce-scatter.3
  165.6 22.1 all-gather.8
  192.0 80.7 all-gather.10
  312.0 142.9 reduce-scatter.5
  458.7 41.9 reduce-scatter.7
where the time goes:
time: 510 us; the launch traced here: 509 us
  waiting for transfers between devices  363 us (71%)
  matrix products  63.2 us (12%)
  other arithmetic  21.5 us (4%)
  blocking collectives  18 us (4%)
  local copies, waits for them, and re-layouts  16.3 us (3%)
  between operations  14.5 us (3%)
  starting transfers between devices  12.1 us (2%)
    reduce_scatter x1, waiting for transfers between devices, shards(): lax.psum_scatter(jnp.dot(hidden, w_down, preferred_element_type=jnp.float...  143 us
    all_gather x1, waiting for transfers between devices, shards(): row_piece = lax.all_gather(normed, 'head', axis=0, tiled=True)  80.9 us
    reduce_scatter x1, waiting for transfers between devices, shards(): lax.psum_scatter(row_total, 'req', scatter_dimension=1, tiled=True)  45.6 us
    dot_general x1, matrix products, shards(): jnp.dot(hidden, w_down, preferred_element_type=jnp.float32)  30.4 us
    reduce_scatter x1, waiting for transfers between devices, shards(): lax.psum_scatter(projected, 'head', scatter_dimension=0, tiled=True)  27.2 us
    all_gather x1, waiting for transfers between devices, shards(): lax.all_gather(attention, 'req', axis=0, tiled=True)  23 us
    all_gather x1, waiting for transfers between devices, shards(): full_state = lax.all_gather(state, 'req', axis=1, tiled=True)  22.4 us
    all_to_all x1, waiting for transfers between devices, shards(): lax.all_to_all(req_acc, 'req', split_axis=0, concat_axis=0, tiled=True)  18.2 us
  transfers between devices with their start and end apart: 10, of which 8 were waited for; matrix products, arithmetic and copies ran while one was open for 6% of the time, Pallas kernels for 0%

commit v1 on v0

v1 whole, which is shorter than its diff:
```python
import functools
import math

import jax
import jax.numpy as jnp
from jax import lax
from jax.experimental import pallas as pl
from jax.experimental.pallas import tpu as pltpu
from jax.sharding import PartitionSpec as P

HEAD_DIM = 128
LO = 64
NEGATIVE_FILL = -1e30
NORM_EPS = 1e-06
BF16 = jnp.bfloat16
F32 = jnp.float32


def swap(array, axis, bits):
    size = lax.axis_size(axis)
    return lax.ppermute(array, axis, [(i, i ^ bits) for i in range(size)])


def whole(shape):
    return pl.BlockSpec(shape, lambda *_: (0,) * len(shape))


def in_vmem(array):
    return pltpu.with_memory_space_constraint(array, pltpu.VMEM)


def params(mebibytes=24):
    return pltpu.CompilerParams(vmem_limit_bytes=mebibytes * 1024 * 1024)


def pack_kernel(page_len, lengths, table, queries, out):
    reqs, slots = table.shape
    query_rows = queries.shape[0]
    inverse_rows = out.shape[0] - query_rows
    high = lax.broadcasted_iota(jnp.int32, (inverse_rows, slots), 0)
    lane = lax.broadcasted_iota(jnp.int32, (2 * LO, slots), 0)
    first = lax.broadcasted_iota(jnp.int32, (1, slots), 1) * page_len
    total = jnp.zeros((inverse_rows, 2 * LO), F32)
    for r in range(reqs):
        ids = table[pl.ds(r, 1), :]
        tokens = jnp.clip(lengths[r] - first, 0, page_len)
        row_hit = jnp.where((ids >> 6) == high, 1.0, 0.0).astype(BF16)
        held = jnp.where(lane < LO, r + 1, tokens)
        lane_hit = jnp.where((ids & (LO - 1)) == (lane & (LO - 1)), held, 0).astype(F32).astype(BF16)
        total += lax.dot_general(
            row_hit, lane_hit, (((1,), (1,)), ((), ())), preferred_element_type=F32
        )
    out[pl.ds(0, query_rows), :] = queries[...]
    out[pl.ds(query_rows, inverse_rows), :] = total.astype(BF16)


def attend_kernel(
    heads, kv_local, reqs, step_pages, owners, tokens, near, far, keys, values, near_out, far_out,
    query, score, top, weight, acc,
):
    chips = near.shape[0]
    steps = keys.shape[0] // step_pages
    rows = reqs * heads
    group = heads // kv_local
    scale = 1.0 / math.sqrt(HEAD_DIM)
    lane = lax.broadcasted_iota(jnp.int32, (heads, HEAD_DIM), 1)
    head = lax.broadcasted_iota(jnp.int32, (heads, HEAD_DIM), 0)

    for side, ref in enumerate((near, far)):
        for chip in range(chips):
            at = (side * chips + chip) * rows
            query[pl.ds(at, rows), :] = ref[chip, pl.ds(0, rows), :].astype(F32)
    top[...] = jnp.full(top.shape, NEGATIVE_FILL, F32)
    weight[...] = jnp.zeros(weight.shape, F32)
    acc[...] = jnp.zeros(acc.shape, F32)

    def place(page):
        return pl.ds(pl.multiple_of(owners[page] * heads, heads), heads)

    @pl.loop(0, steps)
    def _(step):
        first = step * step_pages
        scores = []
        for p in range(step_pages):
            q = query[place(first + p), :]
            q = jnp.concatenate(
                [jnp.where(head // group == kv, q, 0.0) for kv in range(kv_local)], axis=1
            ).astype(BF16)
            s = lax.dot_general(
                q, keys[first + p], (((1,), (1,)), ((), ())), preferred_element_type=F32
            ) * scale
            scores.append(jnp.where(lane < tokens[first + p], s, NEGATIVE_FILL))
        best = [jnp.max(s, axis=1, keepdims=True) for s in scores]
        for p in range(step_pages):
            score[first + p] = scores[p]
        for p in range(step_pages):
            at = place(first + p)
            top[at, :] = jnp.maximum(top[at, :], best[p])

    top[...] = top[...].astype(BF16).astype(F32)

    @pl.loop(0, steps)
    def _(step):
        first = step * step_pages
        sums, parts = [], []
        for p in range(step_pages):
            page = first + p
            w = jnp.exp(score[page] - top[place(page), :])
            w = jnp.where(lane < tokens[page], w, 0.0).astype(BF16)
            a = jnp.dot(w, values[page], preferred_element_type=F32)
            part = a[:, :HEAD_DIM]
            for kv in range(1, kv_local):
                part = jnp.where(
                    head // group == kv, a[:, kv * HEAD_DIM : (kv + 1) * HEAD_DIM], part
                )
            parts.append(part)
            sums.append(jnp.sum(w.astype(F32), axis=1, keepdims=True))
        for p in range(step_pages):
            at = place(first + p)
            acc[at, :] += parts[p]
            weight[at, :] += sums[p]

    lane3 = lax.broadcasted_iota(jnp.int32, (reqs, heads, HEAD_DIM), 2)
    head3 = lax.broadcasted_iota(jnp.int32, (reqs, heads, HEAD_DIM), 1)
    for side, ref in enumerate((near_out, far_out)):
        for chip in range(chips):
            at = pl.ds((side * chips + chip) * rows, rows)
            ref[chip, pl.ds(0, rows), :] = acc[at, :].astype(BF16)
            t = top[at, :].reshape(reqs, heads, HEAD_DIM)
            s = weight[at, :].reshape(reqs, heads, HEAD_DIM)
            s_high = s.astype(BF16).astype(F32)
            stats = jnp.where(lane3 == head3 + 2 * heads, s - s_high, 0.0)
            stats = jnp.where(lane3 == head3 + heads, s_high, stats)
            stats = jnp.where(lane3 == head3, t, stats)
            ref[chip, pl.ds(rows, reqs), :] = jnp.sum(stats, axis=1).astype(BF16)


def combine_kernel(heads, queries, key_new, value_new, *refs):
    parts, out = refs[:-1], refs[-1]
    rows = queries.shape[0]
    reqs = rows // heads
    lane3 = lax.broadcasted_iota(jnp.int32, (reqs, heads, HEAD_DIM), 2)
    head3 = lax.broadcasted_iota(jnp.int32, (reqs, heads, HEAD_DIM), 1)
    diagonal = lane3 == head3

    def narrow(array):
        return jnp.sum(jnp.where(diagonal, array.reshape(reqs, heads, HEAD_DIM), 0.0), axis=1)

    def wide(array):
        return jnp.sum(jnp.where(diagonal, array[:, None, :], 0.0), axis=2, keepdims=True)

    own = jnp.sum(queries[...].astype(F32) * key_new[...].astype(F32), axis=1, keepdims=True)
    own = narrow(jnp.broadcast_to(own * (1.0 / math.sqrt(HEAD_DIM)), (rows, HEAD_DIM)))
    stats = [part[pl.ds(rows, reqs), :].astype(F32) for part in parts]
    best = functools.reduce(jnp.maximum, stats, own)
    own_factor = jnp.exp(own - best)
    factors = [jnp.exp(stat - best) for stat in stats]
    total = own_factor
    for stat, factor in zip(stats, factors):
        total += factor * (
            pltpu.roll(stat, HEAD_DIM - heads, 1) + pltpu.roll(stat, HEAD_DIM - 2 * heads, 1)
        )
    share = 1.0 / total
    attention = wide(own_factor * share) * value_new[...].astype(F32).reshape(
        reqs, heads, HEAD_DIM
    )
    for part, factor in zip(parts, factors):
        attention += wide(factor * share) * part[pl.ds(0, rows), :].astype(F32).reshape(
            reqs, heads, HEAD_DIM
        )
    out[...] = attention.reshape(reqs, heads * HEAD_DIM).astype(BF16)


def project_kernel(place, near, far, w_out, *refs):
    outs, lines = refs[:-1], refs[-1]
    chips, reqs = near.shape[:2]
    block = outs[0].shape[0]

    @pl.when(pl.program_id(0) == 0)
    def _():
        for side, ref in enumerate((near, far)):
            for chip in range(chips):
                first = (place[0] ^ (2 * chip + side)) * reqs
                at = ((first // block) ^ place[1]) * block + first % block
                lines[pl.ds(pl.multiple_of(at, reqs), reqs), :] = ref[chip]

    product = jnp.dot(lines[...], w_out[...], preferred_element_type=F32)
    for a, out in enumerate(outs):
        out[...] = product[a * block : (a + 1) * block].astype(out.dtype)


def hidden_kernel(groups, place, *refs):
    pieces, (gain, w_gate, w_up, out, lines, square, gate, up) = refs[:-8], refs[-8:]
    step = pl.program_id(0)
    steps = len(pieces) // groups

    @pl.when(step == 0)
    def _():
        square[...] = jnp.zeros(square.shape, F32)
        gate[...] = jnp.zeros(gate.shape, F32)
        up[...] = jnp.zeros(up.shape, F32)

    for t in range(steps):

        @pl.when(step == t)
        def _():
            at = 0
            for piece in pieces[t * groups : (t + 1) * groups]:
                here = pl.ds(at, piece.shape[0])
                at += piece.shape[0]
                state = piece[...].astype(F32)
                square[here, :] += jnp.sum(state * state, axis=1, keepdims=True)
                lines[here, :] = (state * gain[0].astype(F32)).astype(BF16)

    contract = (((1,), (1,)), ((), ()))
    gate[...] += lax.dot_general(lines[...], w_gate[...], contract, preferred_element_type=F32)
    up[...] += lax.dot_general(lines[...], w_up[...], contract, preferred_element_type=F32)

    @pl.when(step == steps - 1)
    def _():
        width = steps * lines.shape[1]
        factor = lax.rsqrt(square[:, 0:1] * (1.0 / width) + NORM_EPS)
        g = gate[...] * factor
        out[...] = (g / (1.0 + jnp.exp(-g)) * (up[...] * factor)).astype(BF16)


def down_kernel(bounds, place, hidden, w_down, *outs):
    count = len(bounds)
    for side in range(2):

        @pl.when(pl.program_id(0) == side)
        def _():
            product = jnp.dot(hidden[...], w_down[...], preferred_element_type=F32)
            for (first, size), out in zip(bounds, outs[side * count : (side + 1) * count]):
                out[...] = product[first : first + size].astype(out.dtype)


def shards(
    queries, key_new, value_new, key_pool, value_pool, page_table, lengths, residual_in,
    w_out, norm_gain, w_gate, w_up, w_down,
):
    req_devices = lax.axis_size("req")
    head_devices = lax.axis_size("head")
    chips = req_devices // 2
    reqs = queries.shape[0]
    heads = queries.shape[1] // HEAD_DIM
    kv_local = key_new.shape[1] // HEAD_DIM
    group = heads // kv_local
    rows = reqs * heads
    pages, page_len = key_pool.shape[:2]
    me = lax.axis_index("req")
    place = jnp.stack([me, lax.axis_index("head")]).astype(jnp.int32)
    vmem = pl.BlockSpec(memory_space=pltpu.VMEM)

    inverse_rows = -(-(pages * req_devices // LO) // 16) * 16
    own_queries = queries.reshape(rows, HEAD_DIM)
    payload = pl.pallas_call(
        functools.partial(pack_kernel, page_len),
        out_shape=jax.ShapeDtypeStruct((rows + inverse_rows, HEAD_DIM), BF16),
        in_specs=[pl.BlockSpec(memory_space=pltpu.SMEM), vmem, vmem],
        out_specs=vmem,
        compiler_params=params(),
        name="pack",
    )(lengths, page_table, own_queries)
    near = jnp.stack([payload] + [swap(payload, "req", 2 * c) for c in range(1, chips)])
    far = swap(near, "req", 1)

    per_device = pages // LO
    inverse = jnp.concatenate([near[:, rows:], far[:, rows:]]).astype(jnp.int32)
    inverse = lax.dynamic_slice_in_dim(inverse, me * per_device, per_device, axis=1)
    found, held = inverse[..., :LO], inverse[..., LO:]
    first = (jnp.arange(req_devices, dtype=jnp.int32) * reqs - 1)[:, None, None]
    owners = jnp.sum(jnp.where(found > 0, found + first, 0), axis=0).reshape(pages)
    tokens = jnp.sum(held, axis=0).reshape(pages)

    step_pages = 16
    total_rows = rows * req_devices
    smem = pl.BlockSpec(memory_space=pltpu.SMEM)
    sent = jax.ShapeDtypeStruct((chips, rows + reqs, HEAD_DIM), BF16)
    near_out, far_out = pl.pallas_call(
        functools.partial(attend_kernel, heads, kv_local, reqs, step_pages),
        out_shape=(sent, sent),
        in_specs=[smem, smem, vmem, vmem, vmem, vmem],
        out_specs=[vmem, vmem],
        scratch_shapes=[
            pltpu.VMEM((total_rows, HEAD_DIM), F32),
            pltpu.VMEM((pages, heads, HEAD_DIM), F32),
            pltpu.VMEM((total_rows, HEAD_DIM), F32),
            pltpu.VMEM((total_rows, HEAD_DIM), F32),
            pltpu.VMEM((total_rows, HEAD_DIM), F32),
        ],
        compiler_params=params(16),
        name="attend",
    )(owners, tokens, near, far, in_vmem(key_pool), in_vmem(value_pool))

    parts = [near_out[0], swap(far_out[0], "req", 1)]
    for c in range(1, chips):
        parts += [swap(near_out[c], "req", 2 * c), swap(far_out[c], "req", 2 * c + 1)]

    def per_head(array):
        array = array.reshape(reqs, kv_local, 1, HEAD_DIM)
        array = jnp.broadcast_to(array, (reqs, kv_local, group, HEAD_DIM))
        return array.reshape(rows, HEAD_DIM)

    attention = pl.pallas_call(
        functools.partial(combine_kernel, heads),
        out_shape=jax.ShapeDtypeStruct((reqs, heads * HEAD_DIM), BF16),
        in_specs=[vmem] * (3 + len(parts)),
        out_specs=vmem,
        compiler_params=params(),
        name="combine",
    )(own_queries, per_head(key_new), per_head(value_new), *parts)

    near = jnp.stack([attention] + [swap(attention, "req", 2 * c) for c in range(1, chips)])
    far = swap(near, "req", 1)
    block = reqs * req_devices // head_devices
    columns = w_out.shape[1]
    step_columns = 256
    summed = pl.pallas_call(
        project_kernel,
        out_shape=[
            jax.ShapeDtypeStruct((block, columns), F32 if a == 0 else BF16)
            for a in range(head_devices)
        ],
        grid_spec=pltpu.PrefetchScalarGridSpec(
            num_scalar_prefetch=1,
            grid=(columns // step_columns,),
            in_specs=[
                whole(near.shape),
                whole(far.shape),
                pl.BlockSpec((w_out.shape[0], step_columns), lambda s, *_: (0, s)),
            ],
            out_specs=[pl.BlockSpec((block, step_columns), lambda s, *_: (0, s))] * head_devices,
            scratch_shapes=[pltpu.VMEM((block * head_devices, w_out.shape[0]), BF16)],
        ),
        compiler_params=params(),
        name="project",
    )(place, near, far, w_out)
    state = residual_in.astype(F32) + summed[0]
    for a in range(1, head_devices):
        state += swap(summed[a], "head", a).astype(F32)
    state = state.astype(BF16)

    pieces = {0: state}
    for a in range(1, head_devices):
        pieces[a] = swap(state, "head", a)
    if head_devices <= 4:
        row_groups = [[a] for a in range(head_devices)]
    else:
        row_groups = [[0], list(range(1, head_devices))]
    count = len(row_groups)
    grouped = [
        pieces[g[0]] if len(g) == 1 else jnp.concatenate([pieces[a] for a in g]) for g in row_groups
    ]
    near = [[x if c == 0 else swap(x, "req", 2 * c) for x in grouped] for c in range(chips)]
    far = [[swap(x, "req", 1) for x in line] for line in near]
    operands = []
    for c in range(chips):
        operands += near[c] + far[c]
    all_rows = block * head_devices
    hidden_width = w_gate.shape[1]
    hidden = pl.pallas_call(
        functools.partial(hidden_kernel, count),
        out_shape=jax.ShapeDtypeStruct((all_rows, hidden_width), BF16),
        grid_spec=pltpu.PrefetchScalarGridSpec(
            num_scalar_prefetch=1,
            grid=(req_devices,),
            in_specs=[whole(x.shape) for x in operands]
            + [
                pl.BlockSpec((1, 1, columns), lambda s, at: (at[0] ^ s, 0, 0)),
                pl.BlockSpec((hidden_width, columns), lambda s, at: (0, at[0] ^ s)),
                pl.BlockSpec((hidden_width, columns), lambda s, at: (0, at[0] ^ s)),
            ],
            out_specs=whole((all_rows, hidden_width)),
            scratch_shapes=[
                pltpu.VMEM((all_rows, columns), BF16),
                pltpu.VMEM((all_rows, HEAD_DIM), F32),
                pltpu.VMEM((all_rows, hidden_width), F32),
                pltpu.VMEM((all_rows, hidden_width), F32),
            ],
        ),
        compiler_params=params(),
        name="hidden",
    )(place, *operands, norm_gain.reshape(req_devices, 1, columns), w_gate.T, w_up.T)

    bounds, at = [], 0
    for g in row_groups:
        bounds.append((at, len(g) * block))
        at += len(g) * block
    shapes = [jax.ShapeDtypeStruct((size, columns), BF16) for _, size in bounds] * 2
    received = [[] for _ in row_groups]
    for c in list(range(1, chips)) + [0]:
        halves = pl.pallas_call(
            functools.partial(down_kernel, bounds),
            out_shape=shapes,
            grid_spec=pltpu.PrefetchScalarGridSpec(
                num_scalar_prefetch=1,
                grid=(2,),
                in_specs=[
                    whole(hidden.shape),
                    pl.BlockSpec(
                        (hidden_width, columns),
                        lambda s, at, c=c: (0, at[0] ^ (2 * c + 1 - s)),
                    ),
                ],
                out_specs=[whole(s.shape) for s in shapes],
            ),
            compiler_params=params(),
            name="down",
        )(place, hidden, w_down)
        for g in range(count):
            both = swap(halves[g], "req", 1).astype(F32) + halves[count + g].astype(F32)
            received[g].append(both if c == 0 else swap(both.astype(BF16), "req", 2 * c))
    output = state.astype(F32)
    for g, arrays in zip(row_groups, received):
        total = functools.reduce(jnp.add, [x.astype(F32) for x in arrays])
        for n, a in enumerate(g):
            part = total[n * block : (n + 1) * block]
            output += part if a == 0 else swap(part.astype(BF16), "head", a).astype(F32)
    return output.astype(BF16)


def solution(mesh):
    return jax.shard_map(
        shards,
        mesh=mesh,
        in_specs=(
            P("req", "head"),
            P("req", "head"),
            P("req", "head"),
            P("req", None, "head"),
            P("req", None, "head"),
            P("req", None),
            P("req"),
            P("head", "req"),
            P("head", "req"),
            P(),
            P(None, ("req", "head")),
            P(None, ("req", "head")),
            P(("req", "head"), None),
        ),
        out_specs=P("head", "req"),
        check_vma=False,
    )
```

time: 510 us -> 222 us (0.44)
  waiting for transfers between devices: 363 us -> 64.2 us
  matrix products: 63.2 us -> 0 us
  starting transfers between devices: 12.1 us -> 67.8 us
  Pallas kernels: 0 us -> 42.5 us
  local copies, waits for them, and re-layouts: 16.3 us -> 44.8 us
  other arithmetic: 21.5 us -> 1.97 us
  blocking collectives: 18 us -> 0 us
  between operations: 14.5 us -> 0.51 us
    reduce_scatter x3 -> x0, waiting for transfers between devices: 216 us -> none  [the longest x1 143 us: shards(): lax.psum_scatter(jnp.dot(hidden, w_down, preferred_element_type=jnp.float...]
    all_gather x4 -> x0, waiting for transfers between devices: 126 us -> none  [the longest x1 80.9 us: shards(): row_piece = lax.all_gather(normed, 'head', axis=0, tiled=True)]
    ppermute x0 -> x80, starting transfers between devices: none -> 67.8 us  [swap(): return lax.ppermute(array, axis, [(i, i ^ bits) for i in range(size)])]
    ppermute x0 -> x80, waiting for transfers between devices: none -> 64.2 us  [swap(): return lax.ppermute(array, axis, [(i, i ^ bits) for i in range(size)])]
    dot_general x8 -> x0, matrix products: 63.2 us -> none  [the longest x1 30.4 us: shards(): jnp.dot(hidden, w_down, preferred_element_type=jnp.float32)]
    pallas_call x0 -> x9, Pallas kernels: none -> 42.5 us  [the longest x1 17.1 us: shards(): pl.pallas_call(functools.partial(hidden_kernel, count), out_shape=jax.Sha...]
    unnamed x23 -> x88, local copies, waits for them, and re-layouts: 3.87 us -> 42.1 us
    all_to_all x3 -> x0, waiting for transfers between devices: 20.5 us -> none  [the longest x1 18.2 us: shards(): lax.all_to_all(req_acc, 'req', split_axis=0, concat_axis=0, tiled=True)]
  transfers between devices with their start and end apart: 10 -> 80, of which waited for: 8 -> 34; matrix products, arithmetic and copies ran while one was open for 6% -> 1% of each run, Pallas kernels for 0% -> 3%
where the time goes in v1:
time: 222 us
  starting transfers between devices  67.8 us (31%)
  waiting for transfers between devices  64.2 us (29%)
  local copies, waits for them, and re-layouts  44.8 us (20%)
  Pallas kernels  42.5 us (19%)
    ppermute x80, starting transfers between devices, swap(): return lax.ppermute(array, axis, [(i, i ^ bits) for i in range(size)])  67.8 us
    ppermute x80, waiting for transfers between devices, swap(): return lax.ppermute(array, axis, [(i, i ^ bits) for i in range(size)])  64.2 us
    unnamed x88, local copies, waits for them, and re-layouts  42.1 us
    pallas_call x1, Pallas kernels, shards(): pl.pallas_call(functools.partial(hidden_kernel, count), out_shape=jax.Sha...  17.1 us
    pallas_call x1, Pallas kernels, shards(): pl.pallas_call(functools.partial(attend_kernel, heads, kv_local, reqs, st...  10.8 us
    pallas_call x4, Pallas kernels, shards(): pl.pallas_call(functools.partial(down_kernel, bounds), out_shape=shapes,...  9.34 us
  transfers between devices with their start and end apart: 80, of which 34 were waited for; matrix products, arithmetic and copies ran while one was open for 1% of the time, Pallas kernels for 3%

profile of v1, /device:TPU:0, one launch (start us, length us, event | category | flops | bytes accessed | tf_op | source)
XLA Modules:
  0.0 221.7 jit_solution(17007628466761765820)
XLA Ops:
  3.6 3.9 %collective-permute-start.2 = (bf16[544,128]{1,0:T(8,128)(2,1)S(1)}, bf16[544,128]{1,0:T(8,128)(2,1)S(1)}, u32[]{:S(2)}, u32[]{:S(2)}) collective-permute-start(bf16[544,128]{1,0:T(8,128)(2,1)S(1)} %pack.1), channel_id=1, source_target_pairs={{0,24},{4,28},{8,16},{12,20},{16,8},{20,12},{24,0},{28,4},{1,25},{... | collective-permute-start | bytes 417800 | tf_op jit(solution)/shard_map/ppermute | solution.py:21
  8.1 3.5 %collective-permute-done.2 = bf16[544,128]{1,0:T(8,128)(2,1)S(1)} collective-permute-done((bf16[544,128]{1,0:T(8,128)(2,1)S(1)}, bf16[544,128]{1,0:T(8,128)(2,1)S(1)}, u32[]{:S(2)}, u32[]{:S(2)}) %collective-permute-start.2) | collective-permute-done | bytes 139296 | tf_op jit(solution)/shard_map/ppermute | solution.py:21
  11.5 2.6 %collective-permute-done.1 = bf16[544,128]{1,0:T(8,128)(2,1)S(1)} collective-permute-done((bf16[544,128]{1,0:T(8,128)(2,1)S(1)}, bf16[544,128]{1,0:T(8,128)(2,1)S(1)}, u32[]{:S(2)}, u32[]{:S(2)}) %collective-permute-start.1) | collective-permute-done | bytes 139296 | tf_op jit(solution)/shard_map/ppermute | solution.py:21
  16.8 4.6 %copy-done.1 = bf16[192,128,256]{2,1,0:T(8,128)(2,1)S(1)} copy-done((bf16[192,128,256]{2,1,0:T(8,128)(2,1)S(1)}, bf16[192,128,256]{2,1,0:T(8,128)(2,1)}, u32[]{:S(2)}) %copy-start.1) | copy-done | bytes 12582936
  21.4 4.6 %copy-done.2 = bf16[192,128,256]{2,1,0:T(8,128)(2,1)S(1)} copy-done((bf16[192,128,256]{2,1,0:T(8,128)(2,1)S(1)}, bf16[192,128,256]{2,1,0:T(8,128)(2,1)}, u32[]{:S(2)}) %copy-start.2) | copy-done | bytes 12582936
  25.9 10.8 %attend.1 = (bf16[4,544,128]{2,1,0:T(8,128)(2,1)S(1)}, bf16[4,544,128]{2,1,0:T(8,128)(2,1)S(1)}) custom-call(s32[192]{0:T(256)S(1)} %reshape.30.owners, s32[192]{0:T(256)S(1)} %reshape.31.tokens, bf16[4,544,128]{2,1,0:T(8,128)(2,1)S(1)} %pad_maximum_fusion.near, bf16[4,544,128]{2,1,0:T(8,128)(2,1)S(1)} %collective-permute-done.3.far, ...), custom_call_target="tpu_custom_call" | custom-call | tf_op jit(solution)/shard_map/attend/pallas_call | solution.py:280
  44.3 3.0 %collective-permute-done.7.refs_4_ = bf16[544,128]{1,0:T(8,128)(2,1)S(1)} collective-permute-done((bf16[544,128]{1,0:T(8,128)(2,1)S(1)}, bf16[544,128]{1,0:T(8,128)(2,1)S(1)}, u32[]{:S(2)}, u32[]{:S(2)}) %collective-permute-start.7) | collective-permute-done | bytes 139296 | tf_op jit(solution)/shard_map/ppermute | solution.py:21
  48.8 3.6 %collective-permute-done.8.refs_5_ = bf16[544,128]{1,0:T(8,128)(2,1)S(1)} collective-permute-done((bf16[544,128]{1,0:T(8,128)(2,1)S(1)}, bf16[544,128]{1,0:T(8,128)(2,1)S(1)}, u32[]{:S(2)}, u32[]{:S(2)}) %collective-permute-start.8) | collective-permute-done | bytes 139296 | tf_op jit(solution)/shard_map/ppermute | solution.py:21
  56.9 3.8 %collective-permute-done.13 = bf16[32,2048]{1,0:T(8,128)(2,1)S(1)} collective-permute-done((bf16[32,2048]{1,0:T(8,128)(2,1)S(1)}, bf16[32,2048]{1,0:T(8,128)(2,1)S(1)}, u32[]{:S(2)}, u32[]{:S(2)}) %collective-permute-start.13) | collective-permute-done | bytes 131104 | tf_op jit(solution)/shard_map/ppermute | solution.py:21
  66.9 3.1 %project.1 = (f32[64,1024]{1,0:T(8,128)S(1)}, bf16[64,1024]{1,0:T(8,128)(2,1)S(1)}, bf16[64,1024]{1,0:T(8,128)(2,1)S(1)}, bf16[64,1024]{1,0:T(8,128)(2,1)S(1)}) custom-call(s32[2]{0:T(128)S(1)} %pad_add_fusion.place, bf16[4,32,2048]{2,1,0:T(8,128)(2,1)S(1)} %pad_maximum_fusion.1.near, bf16[4,32,2048]{2,1,0:T(8,128)(2,1)S(1)} %collective-permute-done.14.far, ...), custom_call_target="tpu_custom_call" | custom-call | tf_op jit(solution)/shard_map/project/pallas_call | solution.py:319
  71.6 2.6 %collective-permute-start.16 = (bf16[64,1024]{1,0:T(8,128)(2,1)S(1)}, bf16[64,1024]{1,0:T(8,128)(2,1)S(1)}, u32[]{:S(2)}, u32[]{:S(2)}) collective-permute-start(bf16[64,1024]{1,0:T(8,128)(2,1)S(1)} %get-tuple-element.47), channel_id=1, source_target_pairs={{0,2},{1,3},{2,0},{3,1},{4,6},{5,7},{6,4},{7,5},{8,10},{9,11},{10,... | collective-permute-start | bytes 393224 | tf_op jit(solution)/shard_map/ppermute | solution.py:21
  74.4 3.1 %collective-permute-done.15 = bf16[64,1024]{1,0:T(8,128)(2,1)S(1)} collective-permute-done((bf16[64,1024]{1,0:T(8,128)(2,1)S(1)}, bf16[64,1024]{1,0:T(8,128)(2,1)S(1)}, u32[]{:S(2)}, u32[]{:S(2)}) %collective-permute-start.15) | collective-permute-done | bytes 131104 | tf_op jit(solution)/shard_map/ppermute | solution.py:21
  77.5 7.0 %collective-permute-done.16 = bf16[64,1024]{1,0:T(8,128)(2,1)S(1)} collective-permute-done((bf16[64,1024]{1,0:T(8,128)(2,1)S(1)}, bf16[64,1024]{1,0:T(8,128)(2,1)S(1)}, u32[]{:S(2)}, u32[]{:S(2)}) %collective-permute-start.16) | collective-permute-done | bytes 131104 | tf_op jit(solution)/shard_map/ppermute | solution.py:21
  88.2 2.5 %collective-permute-start.20 = (bf16[64,1024]{1,0:T(8,128)(2,1)S(1)}, bf16[64,1024]{1,0:T(8,128)(2,1)S(1)}, u32[]{:S(2)}, u32[]{:S(2)}) collective-permute-start(bf16[64,1024]{1,0:T(8,128)(2,1)S(1)} %add_convert_fusion.16.refs_0_), channel_id=1, source_target_pairs={{0,3},{1,2},{2,1},{3,0},{4,7},{5,6},{6,5},{7,4},{8,11},{9,10},{10,... | collective-permute-start | bytes 393224 | tf_op jit(solution)/shard_map/ppermute | solution.py:21
  90.8 4.3 %collective-permute-start.19 = (bf16[64,1024]{1,0:T(8,128)(2,1)S(1)}, bf16[64,1024]{1,0:T(8,128)(2,1)S(1)}, u32[]{:S(2)}, u32[]{:S(2)}) collective-permute-start(bf16[64,1024]{1,0:T(8,128)(2,1)S(1)} %add_convert_fusion.16.refs_0_), channel_id=1, source_target_pairs={{0,2},{1,3},{2,0},{3,1},{4,6},{5,7},{6,4},{7,5},{8,10},{9,11},{10,... | collective-permute-start | bytes 393224 | tf_op jit(solution)/shard_map/ppermute | solution.py:21
  96.4 7.9 %collective-permute-done.19.refs_2_ = bf16[64,1024]{1,0:T(8,128)(2,1)S(1)} collective-permute-done((bf16[64,1024]{1,0:T(8,128)(2,1)S(1)}, bf16[64,1024]{1,0:T(8,128)(2,1)S(1)}, u32[]{:S(2)}, u32[]{:S(2)}) %collective-permute-start.19) | collective-permute-done | bytes 131104 | tf_op jit(solution)/shard_map/ppermute | solution.py:21
  133.1 5.3 %copy-done = bf16[8192,924]{0,1:T(8,128)(2,1)S(1)} copy-done((bf16[8192,924]{0,1:T(8,128)(2,1)S(1)}, bf16[8192,924]{0,1:T(8,128)(2,1)}, u32[]{:S(2)}) %copy-start) | copy-done | bytes 15138840
  152.8 17.1 %hidden.1 = bf16[256,924]{1,0:T(8,128)(2,1)S(1)} custom-call(s32[2]{0:T(128)S(1)} %pad_add_fusion.place, bf16[64,1024]{1,0:T(8,128)(2,1)S(1)} %add_convert_fusion.16.refs_0_, bf16[64,1024]{1,0:T(8,128)(2,1)S(1)} %copy-done.5, bf16[64,1024]{1,0:T(8,128)(2,1)S(1)} %collective-permute-done.19.refs_2_, bf16[64,1024]{1,0:T(8,128)(2,1)S(1)} %collective-permute-done.20.refs_3_, ...), custom_call_target="tpu_custom_call" | custom-call | tf_op jit(solution)/shard_map/hidden/pallas_call | solution.py:362
  170.0 2.3 %down.6 = (bf16[64,1024]{1,0:T(8,128)(2,1)S(1)}, bf16[64,1024]{1,0:T(8,128)(2,1)S(1)}, bf16[64,1024]{1,0:T(8,128)(2,1)S(1)}, bf16[64,1024]{1,0:T(8,128)(2,1)S(1)...) custom-call(s32[2]{0:T(128)S(1)} %pad_add_fusion.place, ...), custom_call_target="tpu_custom_call" | custom-call | tf_op jit(solution)/shard_map/down/pallas_call | solution.py:393
  172.5 2.5 %down.7 = (bf16[64,1024]{1,0:T(8,128)(2,1)S(1)}, bf16[64,1024]{1,0:T(8,128)(2,1)S(1)}, bf16[64,1024]{1,0:T(8,128)(2,1)S(1)}, bf16[64,1024]{1,0:T(8,128)(2,1)S(1)...) custom-call(s32[2]{0:T(128)S(1)} %pad_add_fusion.place, ...), custom_call_target="tpu_custom_call" | custom-call | tf_op jit(solution)/shard_map/down/pallas_call | solution.py:393
  177.3 2.3 %down.4 = (bf16[64,1024]{1,0:T(8,128)(2,1)S(1)}, bf16[64,1024]{1,0:T(8,128)(2,1)S(1)}, bf16[64,1024]{1,0:T(8,128)(2,1)S(1)}, bf16[64,1024]{1,0:T(8,128)(2,1)S(1)...) custom-call(s32[2]{0:T(128)S(1)} %pad_add_fusion.place, ...), custom_call_target="tpu_custom_call" | custom-call | tf_op jit(solution)/shard_map/down/pallas_call | solution.py:393
  188.8 3.4 %collective-permute-done.61 = bf16[64,1024]{1,0:T(8,128)(2,1)S(1)} collective-permute-done((bf16[64,1024]{1,0:T(8,128)(2,1)S(1)}, bf16[64,1024]{1,0:T(8,128)(2,1)S(1)}, u32[]{:S(2)}, u32[]{:S(2)}) %collective-permute-start.61) | collective-permute-done | bytes 131104 | tf_op jit(solution)/shard_map/ppermute | solution.py:21
  209.3 3.1 %collective-permute-start.71 = (bf16[64,1024]{1,0:T(8,128)(2,1)S(1)}, bf16[64,1024]{1,0:T(8,128)(2,1)S(1)}, u32[]{:S(2)}, u32[]{:S(2)}) collective-permute-start(bf16[64,1024]{1,0:T(8,128)(2,1)S(1)} %add_convert_fusion.5), channel_id=1, source_target_pairs={{0,2},{1,3},{2,0},{3,1},{4,6},{5,7},{6,4},{7,5},{8,10},{9,11},{10,... | collective-permute-start | bytes 393224 | tf_op jit(solution)/shard_map/ppermute | solution.py:21
  215.5 5.3 %collective-permute-done.71 = bf16[64,1024]{1,0:T(8,128)(2,1)S(1)} collective-permute-done((bf16[64,1024]{1,0:T(8,128)(2,1)S(1)}, bf16[64,1024]{1,0:T(8,128)(2,1)S(1)}, u32[]{:S(2)}, u32[]{:S(2)}) %collective-permute-start.71) | collective-permute-done | bytes 131104 | tf_op jit(solution)/shard_map/ppermute | solution.py:21
  (269 shorter events, 109.2 us)
Async XLA Ops:
  38.4 9.0 %collective-permute-start.7 = (bf16[544,128]{1,0:T(8,128)(2,1)S(1)}, bf16[544,128]{1,0:T(8,128)(2,1)S(1)}, u32[]{:S(2)}, u32[]{:S(2)}) collective-permute-start(bf16[544,128]{1,0:T(8,128)(2,1)S(1)} %get-tuple-element.88), channel_id=1, source_target_pairs={{0,16},{4,20},{8,24},{12,28},{16,0},{20,4},{24,8},{28,12},{1,17},{... | collective-permute-start | bytes 417800 | tf_op jit(solution)/shard_map/ppermute | solution.py:21
  40.4 8.4 %collective-permute-start.10 = (bf16[544,128]{1,0:T(8,128)(2,1)S(1)}, bf16[544,128]{1,0:T(8,128)(2,1)S(1)}, u32[]{:S(2)}, u32[]{:S(2)}) collective-permute-start(bf16[544,128]{1,0:T(8,128)(2,1)S(1)} %get-tuple-element.83), channel_id=1, source_target_pairs={{0,28},{4,24},{8,20},{12,16},{16,12},{20,8},{24,4},{28,0},{1,29},{... | collective-permute-start | bytes 417800 | tf_op jit(solution)/shard_map/ppermute | solution.py:21
  40.9 11.4 %collective-permute-start.8 = (bf16[544,128]{1,0:T(8,128)(2,1)S(1)}, bf16[544,128]{1,0:T(8,128)(2,1)S(1)}, u32[]{:S(2)}, u32[]{:S(2)}) collective-permute-start(bf16[544,128]{1,0:T(8,128)(2,1)S(1)} %get-tuple-element.84), channel_id=1, source_target_pairs={{0,20},{4,16},{8,28},{12,24},{16,4},{20,0},{24,12},{28,8},{1,21},{... | collective-permute-start | bytes 417800 | tf_op jit(solution)/shard_map/ppermute | solution.py:21
  44.3 8.0 %collective-permute-start.6 = (bf16[544,128]{1,0:T(8,128)(2,1)S(1)}, bf16[544,128]{1,0:T(8,128)(2,1)S(1)}, u32[]{:S(2)}, u32[]{:S(2)}) collective-permute-start(bf16[544,128]{1,0:T(8,128)(2,1)S(1)} %get-tuple-element.85), channel_id=1, source_target_pairs={{0,12},{4,8},{8,4},{12,0},{16,28},{20,24},{24,20},{28,16},{1,13},{... | collective-permute-start | bytes 417800 | tf_op jit(solution)/shard_map/ppermute | solution.py:21
  71.6 12.9 %collective-permute-start.16 = (bf16[64,1024]{1,0:T(8,128)(2,1)S(1)}, bf16[64,1024]{1,0:T(8,128)(2,1)S(1)}, u32[]{:S(2)}, u32[]{:S(2)}) collective-permute-start(bf16[64,1024]{1,0:T(8,128)(2,1)S(1)} %get-tuple-element.47), channel_id=1, source_target_pairs={{0,2},{1,3},{2,0},{3,1},{4,6},{5,7},{6,4},{7,5},{8,10},{9,11},{10,... | collective-permute-start | bytes 393224 | tf_op jit(solution)/shard_map/ppermute | solution.py:21
  74.2 10.3 %collective-permute-start.17 = (bf16[64,1024]{1,0:T(8,128)(2,1)S(1)}, bf16[64,1024]{1,0:T(8,128)(2,1)S(1)}, u32[]{:S(2)}, u32[]{:S(2)}) collective-permute-start(bf16[64,1024]{1,0:T(8,128)(2,1)S(1)} %get-tuple-element.48), channel_id=1, source_target_pairs={{0,3},{1,2},{2,1},{3,0},{4,7},{5,6},{6,5},{7,4},{8,11},{9,10},{10,... | collective-permute-start | bytes 393224 | tf_op jit(solution)/shard_map/ppermute | solution.py:21
  86.3 8.7 %collective-permute-start.33 = (bf16[64,1024]{1,0:T(8,128)(2,1)S(1)}, bf16[64,1024]{1,0:T(8,128)(2,1)S(1)}, u32[]{:S(2)}, u32[]{:S(2)}) collective-permute-start(bf16[64,1024]{1,0:T(8,128)(2,1)S(1)} %add_convert_fusion.16.refs_0_), channel_id=1, source_target_pairs={{0,16},{4,20},{8,24},{12,28},{16,0},{20,4},{24,8},{28,12},{1,17},{... | collective-permute-start | bytes 393224 | tf_op jit(solution)/shard_map/ppermute | solution.py:21
  88.2 8.2 %collective-permute-start.20 = (bf16[64,1024]{1,0:T(8,128)(2,1)S(1)}, bf16[64,1024]{1,0:T(8,128)(2,1)S(1)}, u32[]{:S(2)}, u32[]{:S(2)}) collective-permute-start(bf16[64,1024]{1,0:T(8,128)(2,1)S(1)} %add_convert_fusion.16.refs_0_), channel_id=1, source_target_pairs={{0,3},{1,2},{2,1},{3,0},{4,7},{5,6},{6,5},{7,4},{8,11},{9,10},{10,... | collective-permute-start | bytes 393224 | tf_op jit(solution)/shard_map/ppermute | solution.py:21
  90.8 13.4 %collective-permute-start.19 = (bf16[64,1024]{1,0:T(8,128)(2,1)S(1)}, bf16[64,1024]{1,0:T(8,128)(2,1)S(1)}, u32[]{:S(2)}, u32[]{:S(2)}) collective-permute-start(bf16[64,1024]{1,0:T(8,128)(2,1)S(1)} %add_convert_fusion.16.refs_0_), channel_id=1, source_target_pairs={{0,2},{1,3},{2,0},{3,1},{4,6},{5,7},{6,4},{7,5},{8,10},{9,11},{10,... | collective-permute-start | bytes 393224 | tf_op jit(solution)/shard_map/ppermute | solution.py:21
  95.0 10.9 %collective-permute-start.18 = (bf16[64,1024]{1,0:T(8,128)(2,1)S(1)}, bf16[64,1024]{1,0:T(8,128)(2,1)S(1)}, u32[]{:S(2)}, u32[]{:S(2)}) collective-permute-start(bf16[64,1024]{1,0:T(8,128)(2,1)S(1)} %add_convert_fusion.16.refs_0_), channel_id=1, source_target_pairs={{0,1},{1,0},{2,3},{3,2},{4,5},{5,4},{6,7},{7,6},{8,9},{9,8},{10,11... | collective-permute-start | bytes 393224 | tf_op jit(solution)/shard_map/ppermute | solution.py:21
  95.1 12.1 %collective-permute-start.45 = (bf16[64,1024]{1,0:T(8,128)(2,1)S(1)}, bf16[64,1024]{1,0:T(8,128)(2,1)S(1)}, u32[]{:S(2)}, u32[]{:S(2)}) collective-permute-start(bf16[64,1024]{1,0:T(8,128)(2,1)S(1)} %collective-permute-done.41.refs_24_), channel_id=1, source_target_pairs={{0,4},{4,0},{8,12},{12,8},{16,20},{20,16},{24,28},{28,24},{1,5},{5... | collective-permute-start | bytes 393224 | tf_op jit(solution)/shard_map/ppermute | solution.py:21
  95.1 13.2 %collective-permute-start.37 = (bf16[64,1024]{1,0:T(8,128)(2,1)S(1)}, bf16[64,1024]{1,0:T(8,128)(2,1)S(1)}, u32[]{:S(2)}, u32[]{:S(2)}) collective-permute-start(bf16[64,1024]{1,0:T(8,128)(2,1)S(1)} %collective-permute-done.33.refs_16_), channel_id=1, source_target_pairs={{0,4},{4,0},{8,12},{12,8},{16,20},{20,16},{24,28},{28,24},{1,5},{5... | collective-permute-start | bytes 393224 | tf_op jit(solution)/shard_map/ppermute | solution.py:21
  96.4 12.7 %collective-permute-start.29 = (bf16[64,1024]{1,0:T(8,128)(2,1)S(1)}, bf16[64,1024]{1,0:T(8,128)(2,1)S(1)}, u32[]{:S(2)}, u32[]{:S(2)}) collective-permute-start(bf16[64,1024]{1,0:T(8,128)(2,1)S(1)} %collective-permute-done.25.refs_8_), channel_id=1, source_target_pairs={{0,4},{4,0},{8,12},{12,8},{16,20},{20,16},{24,28},{28,24},{1,5},{5... | collective-permute-start | bytes 393224 | tf_op jit(solution)/shard_map/ppermute | solution.py:21
  111.4 8.0 %collective-permute-start.35 = (bf16[64,1024]{1,0:T(8,128)(2,1)S(1)}, bf16[64,1024]{1,0:T(8,128)(2,1)}, u32[]{:S(2)}, u32[]{:S(2)}) collective-permute-start(bf16[64,1024]{1,0:T(8,128)(2,1)S(1)} %collective-permute-done.19.refs_2_), channel_id=1, source_target_pairs={{0,16},{4,20},{8,24},{12,28},{16,0},{20,4},{24,8},{28,12},{1,17},{... | collective-permute-start | bytes 393224 | tf_op jit(solution)/shard_map/ppermute | solution.py:21
  113.3 8.3 %collective-permute-start.27 = (bf16[64,1024]{1,0:T(8,128)(2,1)S(1)}, bf16[64,1024]{1,0:T(8,128)(2,1)}, u32[]{:S(2)}, u32[]{:S(2)}) collective-permute-start(bf16[64,1024]{1,0:T(8,128)(2,1)S(1)} %collective-permute-done.19.refs_2_), channel_id=1, source_target_pairs={{0,8},{4,12},{8,0},{12,4},{16,24},{20,28},{24,16},{28,20},{1,9},{5... | collective-permute-start | bytes 393224 | tf_op jit(solution)/shard_map/ppermute | solution.py:21
  115.4 8.6 %collective-permute-start.42 = (bf16[64,1024]{1,0:T(8,128)(2,1)S(1)}, bf16[64,1024]{1,0:T(8,128)(2,1)}, u32[]{:S(2)}, u32[]{:S(2)}) collective-permute-start(bf16[64,1024]{1,0:T(8,128)(2,1)S(1)} %collective-permute-done.18.refs_1_), channel_id=1, source_target_pairs={{0,24},{4,28},{8,16},{12,20},{16,8},{20,12},{24,0},{28,4},{1,25},{... | collective-permute-start | bytes 393224 | tf_op jit(solution)/shard_map/ppermute | solution.py:21
  116.8 8.5 %collective-permute-start.34 = (bf16[64,1024]{1,0:T(8,128)(2,1)S(1)}, bf16[64,1024]{1,0:T(8,128)(2,1)}, u32[]{:S(2)}, u32[]{:S(2)}) collective-permute-start(bf16[64,1024]{1,0:T(8,128)(2,1)S(1)} %collective-permute-done.18.refs_1_), channel_id=1, source_target_pairs={{0,16},{4,20},{8,24},{12,28},{16,0},{20,4},{24,8},{28,12},{1,17},{... | collective-permute-start | bytes 393224 | tf_op jit(solution)/shard_map/ppermute | solution.py:21
  172.3 8.4 %collective-permute-start.53 = (bf16[64,1024]{1,0:T(8,128)(2,1)S(1)}, bf16[64,1024]{1,0:T(8,128)(2,1)S(1)}, u32[]{:S(2)}, u32[]{:S(2)}) collective-permute-start(bf16[64,1024]{1,0:T(8,128)(2,1)S(1)} %get-tuple-element.53), channel_id=1, source_target_pairs={{0,4},{4,0},{8,12},{12,8},{16,20},{20,16},{24,28},{28,24},{1,5},{5... | collective-permute-start | bytes 393224 | tf_op jit(solution)/shard_map/ppermute | solution.py:21
  179.6 29.7 %collective-permute-start.55 = (bf16[64,1024]{1,0:T(8,128)(2,1)S(1)}, bf16[64,1024]{1,0:T(8,128)(2,1)S(1)}, u32[]{:S(2)}, u32[]{:S(2)}) collective-permute-start(bf16[64,1024]{1,0:T(8,128)(2,1)S(1)} %get-tuple-element.55), channel_id=1, source_target_pairs={{0,4},{4,0},{8,12},{12,8},{16,20},{20,16},{24,28},{28,24},{1,5},{5... | collective-permute-start | bytes 393224 | tf_op jit(solution)/shard_map/ppermute | solution.py:21
  180.0 8.7 %collective-permute-start.62 = (bf16[64,1024]{1,0:T(8,128)(2,1)S(1)}, bf16[64,1024]{1,0:T(8,128)(2,1)S(1)}, u32[]{:S(2)}, u32[]{:S(2)}) collective-permute-start(bf16[64,1024]{1,0:T(8,128)(2,1)S(1)} %get-tuple-element.63), channel_id=1, source_target_pairs={{0,4},{4,0},{8,12},{12,8},{16,20},{20,16},{24,28},{28,24},{1,5},{5... | collective-permute-start | bytes 393224 | tf_op jit(solution)/shard_map/ppermute | solution.py:21
  203.3 9.1 %collective-permute-start.54 = (bf16[64,1024]{1,0:T(8,128)(2,1)S(1)}, bf16[64,1024]{1,0:T(8,128)(2,1)S(1)}, u32[]{:S(2)}, u32[]{:S(2)}) collective-permute-start(bf16[64,1024]{1,0:T(8,128)(2,1)S(1)} %add_convert_fusion.13), channel_id=1, source_target_pairs={{0,24},{4,28},{8,16},{12,20},{16,8},{20,12},{24,0},{28,4},{1,25},{... | collective-permute-start | bytes 393224 | tf_op jit(solution)/shard_map/ppermute | solution.py:21
  204.8 9.0 %collective-permute-start.52 = (bf16[64,1024]{1,0:T(8,128)(2,1)S(1)}, bf16[64,1024]{1,0:T(8,128)(2,1)S(1)}, u32[]{:S(2)}, u32[]{:S(2)}) collective-permute-start(bf16[64,1024]{1,0:T(8,128)(2,1)S(1)} %add_convert_fusion.14), channel_id=1, source_target_pairs={{0,16},{4,20},{8,24},{12,28},{16,0},{20,4},{24,8},{28,12},{1,17},{... | collective-permute-start | bytes 393224 | tf_op jit(solution)/shard_map/ppermute | solution.py:21
  209.3 11.5 %collective-permute-start.71 = (bf16[64,1024]{1,0:T(8,128)(2,1)S(1)}, bf16[64,1024]{1,0:T(8,128)(2,1)S(1)}, u32[]{:S(2)}, u32[]{:S(2)}) collective-permute-start(bf16[64,1024]{1,0:T(8,128)(2,1)S(1)} %add_convert_fusion.5), channel_id=1, source_target_pairs={{0,2},{1,3},{2,0},{3,1},{4,6},{5,7},{6,4},{7,5},{8,10},{9,11},{10,... | collective-permute-start | bytes 393224 | tf_op jit(solution)/shard_map/ppermute | solution.py:21
  212.4 8.4 %collective-permute-start.79 = (bf16[64,1024]{1,0:T(8,128)(2,1)S(1)}, bf16[64,1024]{1,0:T(8,128)(2,1)S(1)}, u32[]{:S(2)}, u32[]{:S(2)}) collective-permute-start(bf16[64,1024]{1,0:T(8,128)(2,1)S(1)} %add_convert_fusion.1), channel_id=1, source_target_pairs={{0,3},{1,2},{2,1},{3,0},{4,7},{5,6},{6,5},{7,4},{8,11},{9,10},{10,... | collective-permute-start | bytes 393224 | tf_op jit(solution)/shard_map/ppermute | solution.py:21
  (100 other events, 623.9 us)

commit v2 on v1

v2 whole, which is shorter than its diff:
```python
import functools
import math

import jax
import jax.numpy as jnp
from jax import lax
from jax.experimental import pallas as pl
from jax.experimental.pallas import tpu as pltpu
from jax.sharding import PartitionSpec as P

HEAD_DIM = 128
LO = 64
NEGATIVE_FILL = -1e30
NORM_EPS = 1e-06
BF16 = jnp.bfloat16
F32 = jnp.float32


def swap(array, axis, bits):
    size = lax.axis_size(axis)
    return lax.ppermute(array, axis, [(i, i ^ bits) for i in range(size)])


def whole(shape):
    return pl.BlockSpec(shape, lambda *_: (0,) * len(shape))


def in_vmem(array):
    return pltpu.with_memory_space_constraint(array, pltpu.VMEM)


def in_hbm(array):
    return pltpu.with_memory_space_constraint(array, pltpu.HBM)


def params(mebibytes=8):
    return pltpu.CompilerParams(vmem_limit_bytes=mebibytes * 1024 * 1024)


def stage_kernel(count, pieces, *refs):
    sources, outs, sems = refs[:count], refs[-1 - count : -1], refs[-1]
    copies = []
    for n in range(count):
        rows = sources[n].shape[0] // pieces // 16 * 16
        for p in range(pieces):
            size = rows if p < pieces - 1 else sources[n].shape[0] - rows * (pieces - 1)
            here = pl.ds(p * rows, size)
            copies.append(
                pltpu.make_async_copy(
                    sources[n].at[here], outs[n].at[here], sems.at[n * pieces + p]
                )
            )
    for copy in copies:
        copy.start()
    for copy in copies:
        copy.wait()


def staged(after, *arrays, name):
    pieces = 4
    size = sum(math.prod(array.shape) * 2 for array in arrays)
    return pl.pallas_call(
        functools.partial(stage_kernel, len(arrays), pieces),
        out_shape=[jax.ShapeDtypeStruct(array.shape, array.dtype) for array in arrays],
        in_specs=[pl.BlockSpec(memory_space=pl.ANY)] * (len(arrays) + len(after)),
        out_specs=[pl.BlockSpec(memory_space=pl.ANY)] * len(arrays),
        scratch_shapes=[pltpu.SemaphoreType.DMA((len(arrays) * pieces,))],
        compiler_params=params(1),
        cost_estimate=pl.CostEstimate(flops=0, bytes_accessed=size, transcendentals=0),
        name=name,
    )(*[in_hbm(array) for array in arrays], *after)


def split_kernel(count, steps, place, *refs):
    sources, outs, sems = refs[:count], refs[-1 - count * steps : -1], refs[-1]
    copies = []
    for n, source in enumerate(sources):
        width = outs[n * steps].shape[1]
        for t in range(steps):
            here = pl.ds(pl.multiple_of((place[0] ^ t) * width, width), width)
            k = n * steps + t
            copies.append(pltpu.make_async_copy(source.at[:, here], outs[k], sems.at[k]))
    for copy in copies:
        copy.start()
    for copy in copies:
        copy.wait()


def staged_blocks(place, steps, after, *arrays, name):
    anywhere = pl.BlockSpec(memory_space=pl.ANY)
    count = len(arrays)
    size = sum(math.prod(array.shape) * 2 for array in arrays)
    blocks = pl.pallas_call(
        functools.partial(split_kernel, count, steps),
        out_shape=[
            jax.ShapeDtypeStruct((array.shape[0], array.shape[1] // steps), array.dtype)
            for array in arrays
            for _ in range(steps)
        ],
        in_specs=[pl.BlockSpec(memory_space=pltpu.SMEM)] + [anywhere] * (count + len(after)),
        out_specs=[anywhere] * (count * steps),
        scratch_shapes=[pltpu.SemaphoreType.DMA((count * steps,))],
        compiler_params=params(1),
        cost_estimate=pl.CostEstimate(flops=0, bytes_accessed=size, transcendentals=0),
        name=name,
    )(place, *[in_hbm(array) for array in arrays], *after)
    return [blocks[n * steps : (n + 1) * steps] for n in range(count)]


def pack_kernel(page_len, place, lengths, table, queries, out):
    del place
    reqs, slots = table.shape
    query_rows = queries.shape[0]
    inverse_rows = out.shape[0] - query_rows
    high = lax.broadcasted_iota(jnp.int32, (inverse_rows, slots), 0)
    lane = lax.broadcasted_iota(jnp.int32, (2 * LO, slots), 0)
    first = lax.broadcasted_iota(jnp.int32, (1, slots), 1) * page_len
    total = jnp.zeros((inverse_rows, 2 * LO), F32)
    for r in range(reqs):
        ids = table[pl.ds(r, 1), :]
        tokens = jnp.clip(lengths[r] - first, 0, page_len)
        row_hit = jnp.where((ids >> 6) == high, 1.0, 0.0).astype(BF16)
        held = jnp.where(lane < LO, r + 1, tokens)
        lane_hit = jnp.where((ids & (LO - 1)) == (lane & (LO - 1)), held, 0).astype(F32).astype(BF16)
        total += lax.dot_general(
            row_hit, lane_hit, (((1,), (1,)), ((), ())), preferred_element_type=F32
        )
    out[pl.ds(0, query_rows), :] = queries[...]
    out[pl.ds(query_rows, inverse_rows), :] = total.astype(BF16)


def stack_kernel(count, *refs):
    out = refs[-1]
    at = 0
    for piece in refs[:count]:
        out[pl.ds(at, piece.shape[0]), :] = piece[...]
        at += piece.shape[0]


def stacked(pieces, *after):
    vmem = pl.BlockSpec(memory_space=pltpu.VMEM)
    rows = sum(piece.shape[0] for piece in pieces)
    return pl.pallas_call(
        functools.partial(stack_kernel, len(pieces)),
        out_shape=jax.ShapeDtypeStruct((rows, pieces[0].shape[1]), pieces[0].dtype),
        in_specs=[vmem] * len(pieces) + [pl.BlockSpec(memory_space=pl.ANY)] * len(after),
        out_specs=vmem,
        compiler_params=params(4),
        name="stack",
    )(*pieces, *after)


def attend_kernel(
    heads, kv_local, reqs, step_pages, place, near, far, keys, values, *refs
):
    outs, (query, score, top, weight, acc, found, index, sem) = refs[:-8], refs[-8:]
    chips = len(outs) // 2
    pages = keys.shape[0]
    steps = pages // step_pages
    rows = reqs * heads
    stride = near.shape[0] // chips
    inverse_rows = stride - rows
    group = heads // kv_local
    scale = 1.0 / math.sqrt(HEAD_DIM)
    lane = lax.broadcasted_iota(jnp.int32, (heads, HEAD_DIM), 1)
    head = lax.broadcasted_iota(jnp.int32, (heads, HEAD_DIM), 0)

    wanted = place[0] * (pages // LO) + lax.broadcasted_iota(jnp.int32, (8, inverse_rows), 0)
    pick = jnp.where(lax.broadcasted_iota(jnp.int32, (8, inverse_rows), 1) == wanted, 1.0, 0.0)
    half = lax.broadcasted_iota(jnp.int32, (8, 2 * LO), 1)
    total = jnp.zeros((8, 2 * LO), F32)
    for side, ref in enumerate((near, far)):
        for chip in range(chips):
            at = (side * chips + chip) * rows
            query[pl.ds(at, rows), :] = ref[pl.ds(chip * stride, rows), :].astype(F32)
            part = jnp.dot(
                pick.astype(BF16),
                ref[pl.ds(chip * stride + rows, inverse_rows), :],
                preferred_element_type=F32,
            )
            base = (side * chips + chip) * reqs - 1
            total += jnp.where((half < LO) & (part > 0.0), part + base, part)
    found[...] = total.astype(jnp.int32)
    copy = pltpu.make_async_copy(found, index, sem)
    copy.start()
    top[...] = jnp.full(top.shape, NEGATIVE_FILL, F32)
    weight[...] = jnp.zeros(weight.shape, F32)
    acc[...] = jnp.zeros(acc.shape, F32)
    copy.wait()

    def rows_of(page):
        return pl.ds(pl.multiple_of(index[page // LO, page % LO] * heads, heads), heads)

    def tokens_of(page):
        return index[page // LO, LO + page % LO]

    @pl.loop(0, steps)
    def _(step):
        first = step * step_pages
        scores = []
        for p in range(step_pages):
            q = query[rows_of(first + p), :]
            q = jnp.concatenate(
                [jnp.where(head // group == kv, q, 0.0) for kv in range(kv_local)], axis=1
            ).astype(BF16)
            s = lax.dot_general(
                q, keys[first + p], (((1,), (1,)), ((), ())), preferred_element_type=F32
            ) * scale
            scores.append(jnp.where(lane < tokens_of(first + p), s, NEGATIVE_FILL))
        best = [jnp.max(s, axis=1, keepdims=True) for s in scores]
        for p in range(step_pages):
            score[first + p] = scores[p]
        for p in range(step_pages):
            at = rows_of(first + p)
            top[at, :] = jnp.maximum(top[at, :], best[p])

    top[...] = top[...].astype(BF16).astype(F32)

    @pl.loop(0, steps)
    def _(step):
        first = step * step_pages
        sums, parts = [], []
        for p in range(step_pages):
            page = first + p
            w = jnp.exp(score[page] - top[rows_of(page), :])
            w = jnp.where(lane < tokens_of(page), w, 0.0).astype(BF16)
            a = jnp.dot(w, values[page], preferred_element_type=F32)
            part = a[:, :HEAD_DIM]
            for kv in range(1, kv_local):
                part = jnp.where(
                    head // group == kv, a[:, kv * HEAD_DIM : (kv + 1) * HEAD_DIM], part
                )
            parts.append(part)
            sums.append(jnp.sum(w.astype(F32), axis=1, keepdims=True))
        for p in range(step_pages):
            at = rows_of(first + p)
            acc[at, :] += parts[p]
            weight[at, :] += sums[p]

    lane3 = lax.broadcasted_iota(jnp.int32, (reqs, heads, HEAD_DIM), 2)
    head3 = lax.broadcasted_iota(jnp.int32, (reqs, heads, HEAD_DIM), 1)
    for n, out in enumerate(outs):
        at = pl.ds(n * rows, rows)
        out[pl.ds(0, rows), :] = acc[at, :].astype(BF16)
        t = top[at, :].reshape(reqs, heads, HEAD_DIM)
        s = weight[at, :].reshape(reqs, heads, HEAD_DIM)
        s_high = s.astype(BF16).astype(F32)
        stats = jnp.where(lane3 == head3 + 2 * heads, s - s_high, 0.0)
        stats = jnp.where(lane3 == head3 + heads, s_high, stats)
        stats = jnp.where(lane3 == head3, t, stats)
        out[pl.ds(rows, reqs), :] = jnp.sum(stats, axis=1).astype(BF16)


def combine_kernel(heads, queries, key_new, value_new, *refs):
    parts, out = refs[2:-1], refs[-1]
    rows = queries.shape[0]
    reqs = rows // heads
    lane3 = lax.broadcasted_iota(jnp.int32, (reqs, heads, HEAD_DIM), 2)
    head3 = lax.broadcasted_iota(jnp.int32, (reqs, heads, HEAD_DIM), 1)
    diagonal = lane3 == head3

    def narrow(array):
        return jnp.sum(jnp.where(diagonal, array.reshape(reqs, heads, HEAD_DIM), 0.0), axis=1)

    def wide(array):
        return jnp.sum(jnp.where(diagonal, array[:, None, :], 0.0), axis=2, keepdims=True)

    def per_head(ref):
        kv_local = ref.shape[1] // HEAD_DIM
        array = ref[...].astype(F32)
        return jnp.concatenate(
            [
                jnp.broadcast_to(
                    array[:, None, kv * HEAD_DIM : (kv + 1) * HEAD_DIM],
                    (reqs, heads // kv_local, HEAD_DIM),
                )
                for kv in range(kv_local)
            ],
            axis=1,
        )

    own = queries[...].astype(F32).reshape(reqs, heads, HEAD_DIM) * per_head(key_new)
    own = jnp.sum(own, axis=2, keepdims=True) * (1.0 / math.sqrt(HEAD_DIM))
    own = narrow(jnp.broadcast_to(own, (reqs, heads, HEAD_DIM)))
    stats = [part[pl.ds(rows, reqs), :].astype(F32) for part in parts]
    best = functools.reduce(jnp.maximum, stats, own)
    own_factor = jnp.exp(own - best)
    factors = [jnp.exp(stat - best) for stat in stats]
    total = own_factor
    for stat, factor in zip(stats, factors):
        total += factor * (
            pltpu.roll(stat, HEAD_DIM - heads, 1) + pltpu.roll(stat, HEAD_DIM - 2 * heads, 1)
        )
    share = 1.0 / total
    attention = wide(own_factor * share) * per_head(value_new)
    for part, factor in zip(parts, factors):
        attention += wide(factor * share) * part[pl.ds(0, rows), :].astype(F32).reshape(
            reqs, heads, HEAD_DIM
        )
    out[...] = attention.reshape(reqs, heads * HEAD_DIM).astype(BF16)


def project_kernel(chips, place, *refs):
    near, far, w_out = refs[:chips], refs[chips : 2 * chips], refs[2 * chips]
    outs, lines = refs[2 * chips + 1 : -1], refs[-1]
    reqs = near[0].shape[0]
    block = outs[0].shape[0]

    for side, line in enumerate((near, far)):
        for chip in range(chips):
            first = (place[0] ^ (2 * chip + side)) * reqs
            at = ((first // block) ^ place[1]) * block + first % block
            lines[pl.ds(pl.multiple_of(at, reqs), reqs), :] = line[chip][...]

    product = jnp.dot(lines[...], w_out[...], preferred_element_type=F32)
    for a, out in enumerate(outs):
        out[...] = product[a * block : (a + 1) * block].astype(out.dtype)


def state_kernel(ready, residual, *refs):
    del ready
    total = residual[...].astype(F32)
    for part in refs[:-1]:
        total += part[...].astype(F32)
    refs[-1][...] = total.astype(BF16)


def gain_kernel(gain, out):
    out[...] = gain[...].astype(F32)


def hidden_kernel(groups, chip, last, total_width, place, *refs):
    pieces, refs = refs[: 2 * groups], refs[2 * groups :]
    gain, w_gate, w_up = refs[0], refs[1:3], refs[3:5]
    before = refs[5:8] if chip else None
    outs, lines = refs[8 if chip else 5 : -1], refs[-1]
    width = lines.shape[2]
    rows, units = outs[0].shape
    contract = (((1,), (1,)), ((), ()))
    square = [None] * groups
    for side in range(2):
        scale = gain[pl.ds(place[0] ^ (2 * chip + side), 1), :]
        at = 0
        for n, piece in enumerate(pieces[side * groups : (side + 1) * groups]):
            state = piece[...].astype(F32)
            part = jnp.sum(state * state, axis=1, keepdims=True)
            square[n] = part if side == 0 else square[n] + part
            lines[side, pl.ds(at, piece.shape[0]), :] = (state * scale).astype(BF16)
            at += piece.shape[0]
    square = jnp.broadcast_to(jnp.concatenate(square, axis=0), (rows, HEAD_DIM))
    if before is not None:
        square = square + before[2][...]
    factor = lax.rsqrt(square[:, 0:1] * (1.0 / total_width) + NORM_EPS)
    for first in range(0, units, 512):
        here = slice(first, min(first + 512, units))
        sums = []
        for n, weight in enumerate((w_gate, w_up)):
            total = None if before is None else before[n][:, here]
            for side in range(2):
                part = lax.dot_general(
                    lines[side], weight[side][here, :], contract, preferred_element_type=F32
                )
                total = part if total is None else total + part
            sums.append(total)
        if last:
            gate = sums[0] * factor
            outs[0][:, here] = (gate / (1.0 + jnp.exp(-gate)) * (sums[1] * factor)).astype(BF16)
        else:
            outs[0][:, here], outs[1][:, here] = sums
    if not last:
        outs[2][...] = square


def down_kernel(bounds, hidden, far, near, *outs):
    count = len(bounds)
    for side, weight in enumerate((far, near)):
        product = jnp.dot(hidden[...], weight[...], preferred_element_type=F32)
        for (first, size), out in zip(bounds, outs[side * count : (side + 1) * count]):
            out[...] = product[first : first + size].astype(out.dtype)


def shards(
    queries, key_new, value_new, key_pool, value_pool, page_table, lengths, residual_in,
    w_out, norm_gain, w_gate, w_up, w_down,
):
    req_devices = lax.axis_size("req")
    head_devices = lax.axis_size("head")
    chips = req_devices // 2
    reqs = queries.shape[0]
    heads = queries.shape[1] // HEAD_DIM
    kv_local = key_new.shape[1] // HEAD_DIM
    hidden_width = w_down.shape[0]
    rows = reqs * heads
    pages, page_len = key_pool.shape[:2]
    me = lax.axis_index("req")
    place = jnp.stack([me, lax.axis_index("head")]).astype(jnp.int32)
    vmem = pl.BlockSpec(memory_space=pltpu.VMEM)
    smem = pl.BlockSpec(memory_space=pltpu.SMEM)

    inverse_rows = -(-(pages * req_devices // LO) // 16) * 16
    own_queries = queries.reshape(rows, HEAD_DIM)
    payload = pl.pallas_call(
        functools.partial(pack_kernel, page_len),
        out_shape=jax.ShapeDtypeStruct((rows + inverse_rows, HEAD_DIM), BF16),
        in_specs=[smem, smem, vmem, vmem],
        out_specs=vmem,
        compiler_params=params(),
        name="pack",
    )(place, lengths, page_table, own_queries)
    near = [payload] + [swap(payload, "req", 2 * c) for c in range(1, chips)]
    columns = w_out.shape[1]
    gain = pl.pallas_call(
        gain_kernel,
        out_shape=jax.ShapeDtypeStruct((req_devices, columns), F32),
        in_specs=[vmem],
        out_specs=vmem,
        compiler_params=params(1),
        name="gain",
    )(norm_gain.reshape(req_devices, columns))
    keys, values = staged([payload, gain], key_pool, value_pool, name="stage_pools")
    near = stacked(near, keys)
    far = swap(near, "req", 1)

    step_pages = 16
    total_rows = rows * req_devices
    anywhere = pl.BlockSpec(memory_space=pl.ANY)
    sent = jax.ShapeDtypeStruct((rows + reqs, HEAD_DIM), BF16)
    partials = pl.pallas_call(
        functools.partial(attend_kernel, heads, kv_local, reqs, step_pages),
        out_shape=[sent] * req_devices,
        in_specs=[smem, vmem, vmem, vmem, vmem],
        out_specs=[vmem] * req_devices,
        scratch_shapes=[
            pltpu.VMEM((total_rows, HEAD_DIM), F32),
            pltpu.VMEM((pages, heads, HEAD_DIM), F32),
            pltpu.VMEM((total_rows, HEAD_DIM), F32),
            pltpu.VMEM((total_rows, HEAD_DIM), F32),
            pltpu.VMEM((total_rows, HEAD_DIM), F32),
            pltpu.VMEM((8, 2 * LO), jnp.int32),
            pltpu.SMEM((8, 2 * LO), jnp.int32),
            pltpu.SemaphoreType.DMA,
        ],
        compiler_params=params(16),
        name="attend",
    )(place, near, far, keys, values)
    w_out, = staged([partials[0]], w_out, name="stage_out")
    w_gate, w_up = staged_blocks(
        place, req_devices, [partials[0]], w_gate.T, w_up.T, name="stage_hidden"
    )

    near_out, far_out = partials[:chips], partials[chips:]
    parts = [near_out[0], swap(far_out[0], "req", 1)]
    for c in range(1, chips):
        parts += [swap(near_out[c], "req", 2 * c), swap(far_out[c], "req", 2 * c + 1)]
    attention = pl.pallas_call(
        functools.partial(combine_kernel, heads),
        out_shape=jax.ShapeDtypeStruct((reqs, heads * HEAD_DIM), BF16),
        in_specs=[vmem] * 3 + [anywhere] * 2 + [vmem] * len(parts),
        out_specs=vmem,
        compiler_params=params(4),
        name="combine",
    )(own_queries, key_new, value_new, w_gate[0], w_out, *parts)

    near = [attention] + [swap(attention, "req", 2 * c) for c in range(1, chips)]
    far = [swap(x, "req", 1) for x in near]
    block = reqs * req_devices // head_devices
    summed = pl.pallas_call(
        functools.partial(project_kernel, chips),
        out_shape=[
            jax.ShapeDtypeStruct((block, columns), F32 if a == 0 else BF16)
            for a in range(head_devices)
        ],
        in_specs=[smem] + [vmem] * (2 * chips + 1),
        out_specs=[vmem] * head_devices,
        scratch_shapes=[pltpu.VMEM((block * head_devices, w_out.shape[0]), BF16)],
        compiler_params=params(5),
        name="project",
    )(place, *near, *far, w_out)
    w_down, = staged_blocks(place, req_devices, [summed[0]], w_down, name="stage_down")
    terms = [summed[0]] + [swap(summed[a], "head", a) for a in range(1, head_devices)]
    state = pl.pallas_call(
        state_kernel,
        out_shape=jax.ShapeDtypeStruct((block, columns), BF16),
        in_specs=[anywhere] + [vmem] * (1 + head_devices),
        out_specs=vmem,
        compiler_params=params(4),
        name="state",
    )(w_down[0], residual_in, *terms)

    pieces = {0: state}
    for a in range(1, head_devices):
        pieces[a] = swap(state, "head", a)
    row_groups = [[0], [1], list(range(2, head_devices))]
    count = len(row_groups)
    grouped = [
        pieces[g[0]] if len(g) == 1 else stacked([pieces[a] for a in g]) for g in row_groups
    ]
    near = [[x if c == 0 else swap(x, "req", 2 * c) for x in grouped] for c in range(chips)]
    far = [[swap(x, "req", 1) for x in line] for line in near]
    all_rows = block * head_devices
    sums = []
    for c in range(chips):
        last = c == chips - 1
        sums = pl.pallas_call(
            functools.partial(hidden_kernel, count, c, last, columns * req_devices),
            out_shape=[jax.ShapeDtypeStruct((all_rows, hidden_width), BF16)]
            if last
            else [
                jax.ShapeDtypeStruct((all_rows, hidden_width), F32),
                jax.ShapeDtypeStruct((all_rows, hidden_width), F32),
                jax.ShapeDtypeStruct((all_rows, HEAD_DIM), F32),
            ],
            in_specs=[smem] + [vmem] * (2 * count + 5 + len(sums)),
            out_specs=[vmem] if last else [vmem] * 3,
            scratch_shapes=[pltpu.VMEM((2, all_rows, columns), BF16)],
            input_output_aliases={} if c == 0 or last else {2 * count + 6 + n: n for n in range(3)},
            compiler_params=params(5),
            cost_estimate=pl.CostEstimate(
                flops=8 * all_rows * columns * hidden_width, bytes_accessed=0, transcendentals=0
            ),
            name="hidden",
        )(
            place, *near[c], *far[c], gain, *w_gate[2 * c : 2 * c + 2], *w_up[2 * c : 2 * c + 2], *sums
        )
    hidden, = sums

    bounds, at = [], 0
    for g in row_groups:
        bounds.append((at, len(g) * block))
        at += len(g) * block
    shapes = [jax.ShapeDtypeStruct((size, columns), BF16) for _, size in bounds] * 2
    received = [[] for _ in row_groups]
    for c in list(range(1, chips)) + [0]:
        halves = pl.pallas_call(
            functools.partial(down_kernel, bounds),
            out_shape=shapes,
            in_specs=[vmem] * 3,
            out_specs=[vmem] * len(shapes),
            compiler_params=params(5),
            cost_estimate=pl.CostEstimate(
                flops=4 * all_rows * columns * hidden_width, bytes_accessed=0, transcendentals=0
            ),
            name="down",
        )(hidden, w_down[2 * c + 1], w_down[2 * c])
        for g in range(count):
            both = swap(halves[g], "req", 1).astype(F32) + halves[count + g].astype(F32)
            received[g].append(both if c == 0 else swap(both.astype(BF16), "req", 2 * c))
    output = state.astype(F32)
    for g, arrays in zip(row_groups, received):
        total = functools.reduce(jnp.add, [x.astype(F32) for x in arrays])
        for n, a in enumerate(g):
            part = total[n * block : (n + 1) * block]
            output += part if a == 0 else swap(part.astype(BF16), "head", a).astype(F32)
    return output.astype(BF16)


def solution(mesh):
    return jax.shard_map(
        shards,
        mesh=mesh,
        in_specs=(
            P("req", "head"),
            P("req", "head"),
            P("req", "head"),
            P("req", None, "head"),
            P("req", None, "head"),
            P("req", None),
            P("req"),
            P("head", "req"),
            P("head", "req"),
            P(),
            P(None, ("req", "head")),
            P(None, ("req", "head")),
            P(("req", "head"), None),
        ),
        out_specs=P("head", "req"),
        check_vma=False,
    )
```

time: 222 us -> 177 us (0.80)
  local copies, waits for them, and re-layouts: 44.8 us -> 3.11 us
  Pallas kernels: 42.5 us -> 61 us
  waiting for transfers between devices: 64.2 us -> 52.8 us
  starting transfers between devices: 67.8 us -> 57.3 us
    unnamed x88 -> x10, local copies, waits for them, and re-layouts: 42.1 us -> 1.39 us
    pallas_call x2 -> x13, Pallas kernels: 20.2 us -> 42 us  [the longest x2 16.6 us: staged_blocks(): pl.pallas_call(functools.partial(split_kernel, count, steps), out_shape=[...]
    ppermute x80 -> x69, waiting for transfers between devices: 64.2 us -> 52.8 us  [swap(): return lax.ppermute(array, axis, [(i, i ^ bits) for i in range(size)])]
    ppermute x80 -> x69, starting transfers between devices: 67.8 us -> 57.3 us  [swap(): return lax.ppermute(array, axis, [(i, i ^ bits) for i in range(size)])]
    pallas_call x4, Pallas kernels: 9.34 us -> 5.02 us  [shards(): pl.pallas_call(functools.partial(down_kernel, bounds), out_shape=shapes,...]
  transfers between devices with their start and end apart: 80 -> 69, of which waited for: 34 -> 21; matrix products, arithmetic and copies ran while one was open for 1% -> 1% of each run, Pallas kernels for 3% -> 23%
where the time goes in v2:
time: 177 us; the launch traced here: 176 us
  Pallas kernels  61 us (34%)
  starting transfers between devices  57.3 us (32%)
  waiting for transfers between devices  52.8 us (30%)
  local copies, waits for them, and re-layouts  3.11 us (2%)
    ppermute x69, starting transfers between devices, swap(): return lax.ppermute(array, axis, [(i, i ^ bits) for i in range(size)])  57.3 us
    ppermute x69, waiting for transfers between devices, swap(): return lax.ppermute(array, axis, [(i, i ^ bits) for i in range(size)])  52.8 us
    pallas_call x2, Pallas kernels, staged_blocks(): pl.pallas_call(functools.partial(split_kernel, count, steps), out_shape=[...  16.6 us
    pallas_call x4, Pallas kernels, shards(): pl.pallas_call(functools.partial(hidden_kernel, count, c, last, columns *...  12.9 us
    pallas_call x1, Pallas kernels, shards(): pl.pallas_call(functools.partial(attend_kernel, heads, kv_local, reqs, st...  11.9 us
    pallas_call x2, Pallas kernels, staged(): pl.pallas_call(functools.partial(stage_kernel, len(arrays), pieces), out_...  10.5 us
    pallas_call x4, Pallas kernels, shards(): pl.pallas_call(functools.partial(down_kernel, bounds), out_shape=shapes,...  5.02 us
  transfers between devices with their start and end apart: 69, of which 21 were waited for; matrix products, arithmetic and copies ran while one was open for 1% of the time, Pallas kernels for 23%

profile of v2, /device:TPU:0, one launch (start us, length us, event | category | flops | bytes accessed | tf_op | source)
XLA Modules:
  0.0 176.5 jit_solution(1346791224692656658)
XLA Ops:
  3.6 3.0 %collective-permute-start = (bf16[544,128]{1,0:T(8,128)(2,1)S(1)}, bf16[544,128]{1,0:T(8,128)(2,1)S(1)}, u32[]{:S(2)}, u32[]{:S(2)}) collective-permute-start(bf16[544,128]{1,0:T(8,128)(2,1)S(1)} %pack.1.refs_2_.refs_0_), channel_id=1, source_target_pairs={{0,8},{4,12},{8,0},{12,4},{16,24},{20,28},{24,16},{28,20},{1,9},{5... | collective-permute-start | bytes 417800 | tf_op jit(solution)/shard_map/ppermute | solution.py:21
  8.8 8.3 %stage_pools.1 = (bf16[192,128,256]{2,1,0:T(8,128)(2,1)S(1)}, bf16[192,128,256]{2,1,0:T(8,128)(2,1)S(1)}) custom-call(bf16[192,128,256]{2,1,0:T(8,128)(2,1)} %refs_0_.3, bf16[192,128,256]{2,1,0:T(8,128)(2,1)} %refs_1_.1, bf16[544,128]{1,0:T(8,128)(2,1)S(1)} %pack.1.refs_2_.refs_0_, f32[8,1024]{1,0:T(8,128)S(1)} %gain.1.refs_3_.refs_6_), custom_call_target="tpu_custom_call" | custom-call | bytes 25165824 | tf_op jit(solution)/shard_map/stage_pools/pallas_call | solution.py:62
  19.3 11.9 %attend.1 = (bf16[544,128]{1,0:T(8,128)(2,1)S(1)}, bf16[544,128]{1,0:T(8,128)(2,1)S(1)}, bf16[544,128]{1,0:T(8,128)(2,1)S(1)}, bf16[544,128]{1,0:T(8,128)(2,1)S(...) custom-call(s32[2]{0:T(128)S(1)} %pad_add_fusion.place, ...), custom_call_target="tpu_custom_call" | custom-call | tf_op jit(solution)/shard_map/attend/pallas_call | solution.py:428
  31.2 2.7 %collective-permute-start.10 = (bf16[544,128]{1,0:T(8,128)(2,1)S(1)}, bf16[544,128]{1,0:T(8,128)(2,1)S(1)}, u32[]{:S(2)}, u32[]{:S(2)}) collective-permute-start(bf16[544,128]{1,0:T(8,128)(2,1)S(1)} %get-tuple-element.86), channel_id=1, source_target_pairs={{0,28},{4,24},{8,20},{12,16},{16,12},{20,8},{24,4},{28,0},{1,29},{... | collective-permute-start | bytes 417800 | tf_op jit(solution)/shard_map/ppermute | solution.py:21
  43.5 10.5 %stage_hidden.1 = (bf16[924,1024]{1,0:T(8,128)(2,1)S(1)}, bf16[924,1024]{1,0:T(8,128)(2,1)S(1)}, bf16[924,1024]{1,0:T(8,128)(2,1)S(1)}, bf16[924,1024]{1,0:T(8,1...) custom-call(s32[2]{0:T(128)S(1)} %pad_add_fusion.place, ...), custom_call_target="tpu_custom_call" | custom-call | bytes 30277632 | tf_op jit(solution)/shard_map/stage_hidden/pallas_call | solution.py:93
  58.6 2.9 %collective-permute-done.11.refs_1_ = bf16[32,2048]{1,0:T(8,128)(2,1)S(1)} collective-permute-done((bf16[32,2048]{1,0:T(8,128)(2,1)S(1)}, bf16[32,2048]{1,0:T(8,128)(2,1)S(1)}, u32[]{:S(2)}, u32[]{:S(2)}) %collective-permute-start.11) | collective-permute-done | bytes 131104 | tf_op jit(solution)/shard_map/ppermute | solution.py:21
  69.0 2.6 %collective-permute-start.19 = (bf16[64,1024]{1,0:T(8,128)(2,1)S(1)}, bf16[64,1024]{1,0:T(8,128)(2,1)S(1)}, u32[]{:S(2)}, u32[]{:S(2)}) collective-permute-start(bf16[64,1024]{1,0:T(8,128)(2,1)S(1)} %get-tuple-element.90), channel_id=1, source_target_pairs={{0,2},{1,3},{2,0},{3,1},{4,6},{5,7},{6,4},{7,5},{8,10},{9,11},{10,... | collective-permute-start | bytes 393224 | tf_op jit(solution)/shard_map/ppermute | solution.py:21
  71.8 6.1 %stage_down.1 = (bf16[924,1024]{1,0:T(8,128)(2,1)S(1)}, bf16[924,1024]{1,0:T(8,128)(2,1)S(1)}, bf16[924,1024]{1,0:T(8,128)(2,1)S(1)}, bf16[924,1024]{1,0:T(8,128...) custom-call(s32[2]{0:T(128)S(1)} %pad_add_fusion.place, ...), custom_call_target="tpu_custom_call" | custom-call | bytes 15138816 | tf_op jit(solution)/shard_map/stage_down/pallas_call | solution.py:93
  77.9 4.0 %collective-permute-done.19.refs_2_ = bf16[64,1024]{1,0:T(8,128)(2,1)S(1)} collective-permute-done((bf16[64,1024]{1,0:T(8,128)(2,1)S(1)}, bf16[64,1024]{1,0:T(8,128)(2,1)S(1)}, u32[]{:S(2)}, u32[]{:S(2)}) %collective-permute-start.19) | collective-permute-done | bytes 131104 | tf_op jit(solution)/shard_map/ppermute | solution.py:21
  82.0 3.4 %collective-permute-start.24 = (bf16[64,1024]{1,0:T(8,128)(2,1)S(1)}, bf16[64,1024]{1,0:T(8,128)(2,1)S(1)}, u32[]{:S(2)}, u32[]{:S(2)}) collective-permute-start(bf16[64,1024]{1,0:T(8,128)(2,1)S(1)} %state.1.refs_0_), channel_id=1, source_target_pairs={{0,2},{1,3},{2,0},{3,1},{4,6},{5,7},{6,4},{7,5},{8,10},{9,11},{10,... | collective-permute-start | bytes 393224 | tf_op jit(solution)/shard_map/ppermute | solution.py:21
  87.9 7.1 %collective-permute-done.24.refs_0_ = bf16[64,1024]{1,0:T(8,128)(2,1)S(1)} collective-permute-done((bf16[64,1024]{1,0:T(8,128)(2,1)S(1)}, bf16[64,1024]{1,0:T(8,128)(2,1)S(1)}, u32[]{:S(2)}, u32[]{:S(2)}) %collective-permute-start.24) | collective-permute-done | bytes 131104 | tf_op jit(solution)/shard_map/ppermute | solution.py:21
  103.7 3.4 %collective-permute-done.37.refs_1_ = bf16[64,1024]{1,0:T(8,128)(2,1)S(1)} collective-permute-done((bf16[64,1024]{1,0:T(8,128)(2,1)S(1)}, bf16[64,1024]{1,0:T(8,128)(2,1)S(1)}, u32[]{:S(2)}, u32[]{:S(2)}) %collective-permute-start.37) | collective-permute-done | bytes 131104 | tf_op jit(solution)/shard_map/ppermute | solution.py:21
  110.7 3.0 %hidden.4 = (f32[256,924]{1,0:T(8,128)S(1)}, f32[256,924]{1,0:T(8,128)S(1)}, f32[256,128]{1,0:T(8,128)S(1)}) custom-call(s32[2]{0:T(128)S(1)} %pad_add_fusion.place, bf16[64,1024]{1,0:T(8,128)(2,1)S(1)} %state.1.refs_0_, bf16[64,1024]{1,0:T(8,128)(2,1)S(1)} %collective-permute-done.22.refs_1_, bf16[128,1024]{1,0:T(8,128)(2,1)S(1)} %stack.15.refs_2_, ...), custom_call_target="tpu_custom_call" | custom-call | flops 1937768448 | tf_op jit(solution)/shard_map/hidden/pallas_call | solution.py:504
  113.7 3.9 %collective-permute-done.31.refs_1_ = bf16[64,1024]{1,0:T(8,128)(2,1)S(1)} collective-permute-done((bf16[64,1024]{1,0:T(8,128)(2,1)S(1)}, bf16[64,1024]{1,0:T(8,128)(2,1)S(1)}, u32[]{:S(2)}, u32[]{:S(2)}) %collective-permute-start.31) | collective-permute-done | bytes 131104 | tf_op jit(solution)/shard_map/ppermute | solution.py:21
  119.7 3.2 %hidden.5 = (f32[256,924]{1,0:T(8,128)S(1)}, f32[256,924]{1,0:T(8,128)S(1)}, f32[256,128]{1,0:T(8,128)S(1)}) custom-call(s32[2]{0:T(128)S(1)} %pad_add_fusion.place, bf16[64,1024]{1,0:T(8,128)(2,1)S(1)} %collective-permute-done.36.refs_0_, ...), custom_call_target="tpu_custom_call", output_to_operand_aliasing={{0}: (12, {}), {1}: (13, {}), {2}: (14, {})} | custom-call | flops 1937768448 | tf_op jit(solution)/shard_map/hidden/pallas_call | solution.py:504
  124.0 3.5 %hidden.6 = (f32[256,924]{1,0:T(8,128)S(1)}, f32[256,924]{1,0:T(8,128)S(1)}, f32[256,128]{1,0:T(8,128)S(1)}) custom-call(s32[2]{0:T(128)S(1)} %pad_add_fusion.place, bf16[64,1024]{1,0:T(8,128)(2,1)S(1)} %collective-permute-done.30.refs_0_, ...), custom_call_target="tpu_custom_call", output_to_operand_aliasing={{0}: (12, {}), {1}: (13, {}), {2}: (14, {})} | custom-call | flops 1937768448 | tf_op jit(solution)/shard_map/hidden/pallas_call | solution.py:504
  127.5 3.2 %hidden.7 = bf16[256,924]{1,0:T(8,128)(2,1)S(1)} custom-call(s32[2]{0:T(128)S(1)} %pad_add_fusion.place, bf16[64,1024]{1,0:T(8,128)(2,1)S(1)} %collective-permute-done.21.refs_0_, bf16[64,1024]{1,0:T(8,128)(2,1)S(1)} %collective-permute-done.23.refs_1_, bf16[128,1024]{1,0:T(8,128)(2,1)S(1)} %collective-permute-done.26.refs_2_, ...), custom_call_target="tpu_custom_call" | custom-call | flops 1937768448 | tf_op jit(solution)/shard_map/hidden/pallas_call | solution.py:504
  147.5 2.9 %collective-permute-done.55 = bf16[64,1024]{1,0:T(8,128)(2,1)S(1)} collective-permute-done((bf16[64,1024]{1,0:T(8,128)(2,1)S(1)}, bf16[64,1024]{1,0:T(8,128)(2,1)S(1)}, u32[]{:S(2)}, u32[]{:S(2)}) %collective-permute-start.55) | collective-permute-done | bytes 131104 | tf_op jit(solution)/shard_map/ppermute | solution.py:21
  151.9 3.4 %collective-permute-done.61 = bf16[128,1024]{1,0:T(8,128)(2,1)S(1)} collective-permute-done((bf16[128,1024]{1,0:T(8,128)(2,1)S(1)}, bf16[128,1024]{1,0:T(8,128)(2,1)S(1)}, u32[]{:S(2)}, u32[]{:S(2)}) %collective-permute-start.61) | collective-permute-done | bytes 262176 | tf_op jit(solution)/shard_map/ppermute | solution.py:21
  156.0 5.7 %collective-permute-done.63 = bf16[128,1024]{1,0:T(8,128)(2,1)S(1)} collective-permute-done((bf16[128,1024]{1,0:T(8,128)(2,1)S(1)}, bf16[128,1024]{1,0:T(8,128)(2,1)S(1)}, u32[]{:S(2)}, u32[]{:S(2)}) %collective-permute-start.63) | collective-permute-done | bytes 262176 | tf_op jit(solution)/shard_map/ppermute | solution.py:21
  161.7 3.3 %collective-permute-start.59 = (bf16[64,1024]{1,0:T(8,128)(2,1)S(1)}, bf16[64,1024]{1,0:T(8,128)(2,1)S(1)}, u32[]{:S(2)}, u32[]{:S(2)}) collective-permute-start(bf16[64,1024]{1,0:T(8,128)(2,1)S(1)} %add_convert_fusion.5), channel_id=1, source_target_pairs={{0,1},{1,0},{2,3},{3,2},{4,5},{5,4},{6,7},{7,6},{8,9},{9,8},{10,11... | collective-permute-start | bytes 393224 | tf_op jit(solution)/shard_map/ppermute | solution.py:21
  165.4 2.4 %collective-permute-start.68 = (bf16[64,1024]{1,0:T(8,128)(2,1)S(1)}, bf16[64,1024]{1,0:T(8,128)(2,1)S(1)}, u32[]{:S(2)}, u32[]{:S(2)}) collective-permute-start(bf16[64,1024]{1,0:T(8,128)(2,1)S(1)} %get-tuple-element.148), channel_id=1, source_target_pairs={{0,3},{1,2},{2,1},{3,0},{4,7},{5,6},{6,5},{7,4},{8,11},{9,10},{10,... | collective-permute-start | bytes 393224 | tf_op jit(solution)/shard_map/ppermute | solution.py:21
  167.7 2.9 %collective-permute-done.59 = bf16[64,1024]{1,0:T(8,128)(2,1)S(1)} collective-permute-done((bf16[64,1024]{1,0:T(8,128)(2,1)S(1)}, bf16[64,1024]{1,0:T(8,128)(2,1)S(1)}, u32[]{:S(2)}, u32[]{:S(2)}) %collective-permute-start.59) | collective-permute-done | bytes 131104 | tf_op jit(solution)/shard_map/ppermute | solution.py:21
  170.7 5.0 %collective-permute-done.67 = bf16[64,1024]{1,0:T(8,128)(2,1)S(1)} collective-permute-done((bf16[64,1024]{1,0:T(8,128)(2,1)S(1)}, bf16[64,1024]{1,0:T(8,128)(2,1)S(1)}, u32[]{:S(2)}, u32[]{:S(2)}) %collective-permute-start.67) | collective-permute-done | bytes 131104 | tf_op jit(solution)/shard_map/ppermute | solution.py:21
  (160 shorter events, 67.8 us)
Async XLA Ops:
  3.6 13.5 %collective-permute-start = (bf16[544,128]{1,0:T(8,128)(2,1)S(1)}, bf16[544,128]{1,0:T(8,128)(2,1)S(1)}, u32[]{:S(2)}, u32[]{:S(2)}) collective-permute-start(bf16[544,128]{1,0:T(8,128)(2,1)S(1)} %pack.1.refs_2_.refs_0_), channel_id=1, source_target_pairs={{0,8},{4,12},{8,0},{12,4},{16,24},{20,28},{24,16},{28,20},{1,9},{5... | collective-permute-start | bytes 417800 | tf_op jit(solution)/shard_map/ppermute | solution.py:21
  6.6 10.6 %collective-permute-start.1 = (bf16[544,128]{1,0:T(8,128)(2,1)S(1)}, bf16[544,128]{1,0:T(8,128)(2,1)S(1)}, u32[]{:S(2)}, u32[]{:S(2)}) collective-permute-start(bf16[544,128]{1,0:T(8,128)(2,1)S(1)} %pack.1.refs_2_.refs_0_), channel_id=1, source_target_pairs={{0,16},{4,20},{8,24},{12,28},{16,0},{20,4},{24,8},{28,12},{1,17},{... | collective-permute-start | bytes 417800 | tf_op jit(solution)/shard_map/ppermute | solution.py:21
  34.3 19.8 %collective-permute-start.5 = (bf16[544,128]{1,0:T(8,128)(2,1)S(1)}, bf16[544,128]{1,0:T(8,128)(2,1)S(1)}, u32[]{:S(2)}, u32[]{:S(2)}) collective-permute-start(bf16[544,128]{1,0:T(8,128)(2,1)S(1)} %get-tuple-element.81), channel_id=1, source_target_pairs={{0,8},{4,12},{8,0},{12,4},{16,24},{20,28},{24,16},{28,20},{1,9},{5... | collective-permute-start | bytes 417800 | tf_op jit(solution)/shard_map/ppermute | solution.py:21
  34.8 19.3 %collective-permute-start.6 = (bf16[544,128]{1,0:T(8,128)(2,1)S(1)}, bf16[544,128]{1,0:T(8,128)(2,1)S(1)}, u32[]{:S(2)}, u32[]{:S(2)}) collective-permute-start(bf16[544,128]{1,0:T(8,128)(2,1)S(1)} %get-tuple-element.82), channel_id=1, source_target_pairs={{0,12},{4,8},{8,4},{12,0},{16,28},{20,24},{24,20},{28,16},{1,13},{... | collective-permute-start | bytes 417800 | tf_op jit(solution)/shard_map/ppermute | solution.py:21
  35.8 18.3 %collective-permute-start.7 = (bf16[544,128]{1,0:T(8,128)(2,1)S(1)}, bf16[544,128]{1,0:T(8,128)(2,1)S(1)}, u32[]{:S(2)}, u32[]{:S(2)}) collective-permute-start(bf16[544,128]{1,0:T(8,128)(2,1)S(1)} %get-tuple-element.83), channel_id=1, source_target_pairs={{0,16},{4,20},{8,24},{12,28},{16,0},{20,4},{24,8},{28,12},{1,17},{... | collective-permute-start | bytes 417800 | tf_op jit(solution)/shard_map/ppermute | solution.py:21
  38.0 16.2 %collective-permute-start.8 = (bf16[544,128]{1,0:T(8,128)(2,1)S(1)}, bf16[544,128]{1,0:T(8,128)(2,1)S(1)}, u32[]{:S(2)}, u32[]{:S(2)}) collective-permute-start(bf16[544,128]{1,0:T(8,128)(2,1)S(1)} %get-tuple-element.84), channel_id=1, source_target_pairs={{0,20},{4,16},{8,28},{12,24},{16,4},{20,0},{24,12},{28,8},{1,21},{... | collective-permute-start | bytes 417800 | tf_op jit(solution)/shard_map/ppermute | solution.py:21
  39.8 14.3 %collective-permute-start.9 = (bf16[544,128]{1,0:T(8,128)(2,1)S(1)}, bf16[544,128]{1,0:T(8,128)(2,1)S(1)}, u32[]{:S(2)}, u32[]{:S(2)}) collective-permute-start(bf16[544,128]{1,0:T(8,128)(2,1)S(1)} %get-tuple-element.85), channel_id=1, source_target_pairs={{0,24},{4,28},{8,16},{12,20},{16,8},{20,12},{24,0},{28,4},{1,25},{... | collective-permute-start | bytes 417800 | tf_op jit(solution)/shard_map/ppermute | solution.py:21
  69.0 12.9 %collective-permute-start.19 = (bf16[64,1024]{1,0:T(8,128)(2,1)S(1)}, bf16[64,1024]{1,0:T(8,128)(2,1)S(1)}, u32[]{:S(2)}, u32[]{:S(2)}) collective-permute-start(bf16[64,1024]{1,0:T(8,128)(2,1)S(1)} %get-tuple-element.90), channel_id=1, source_target_pairs={{0,2},{1,3},{2,0},{3,1},{4,6},{5,7},{6,4},{7,5},{8,10},{9,11},{10,... | collective-permute-start | bytes 393224 | tf_op jit(solution)/shard_map/ppermute | solution.py:21
  82.0 12.9 %collective-permute-start.24 = (bf16[64,1024]{1,0:T(8,128)(2,1)S(1)}, bf16[64,1024]{1,0:T(8,128)(2,1)S(1)}, u32[]{:S(2)}, u32[]{:S(2)}) collective-permute-start(bf16[64,1024]{1,0:T(8,128)(2,1)S(1)} %state.1.refs_0_), channel_id=1, source_target_pairs={{0,2},{1,3},{2,0},{3,1},{4,6},{5,7},{6,4},{7,5},{8,10},{9,11},{10,... | collective-permute-start | bytes 393224 | tf_op jit(solution)/shard_map/ppermute | solution.py:21
  85.4 10.8 %collective-permute-start.25 = (bf16[64,1024]{1,0:T(8,128)(2,1)S(1)}, bf16[64,1024]{1,0:T(8,128)(2,1)S(1)}, u32[]{:S(2)}, u32[]{:S(2)}) collective-permute-start(bf16[64,1024]{1,0:T(8,128)(2,1)S(1)} %state.1.refs_0_), channel_id=1, source_target_pairs={{0,3},{1,2},{2,1},{3,0},{4,7},{5,6},{6,5},{7,4},{8,11},{9,10},{10,... | collective-permute-start | bytes 393224 | tf_op jit(solution)/shard_map/ppermute | solution.py:21
  86.7 11.0 %collective-permute-start.22 = (bf16[64,1024]{1,0:T(8,128)(2,1)S(1)}, bf16[64,1024]{1,0:T(8,128)(2,1)S(1)}, u32[]{:S(2)}, u32[]{:S(2)}) collective-permute-start(bf16[64,1024]{1,0:T(8,128)(2,1)S(1)} %state.1.refs_0_), channel_id=1, source_target_pairs={{0,1},{1,0},{2,3},{3,2},{4,5},{5,4},{6,7},{7,6},{8,9},{9,8},{10,11... | collective-permute-start | bytes 393224 | tf_op jit(solution)/shard_map/ppermute | solution.py:21
  86.7 11.8 %collective-permute-start.42 = (bf16[64,1024]{1,0:T(8,128)(2,1)S(1)}, bf16[64,1024]{1,0:T(8,128)(2,1)S(1)}, u32[]{:S(2)}, u32[]{:S(2)}) collective-permute-start(bf16[64,1024]{1,0:T(8,128)(2,1)S(1)} %state.1.refs_0_), channel_id=1, source_target_pairs={{0,4},{4,0},{8,12},{12,8},{16,20},{20,16},{24,28},{28,24},{1,5},{5... | collective-permute-start | bytes 393224 | tf_op jit(solution)/shard_map/ppermute | solution.py:21
  86.7 11.8 %collective-permute-start.36 = (bf16[64,1024]{1,0:T(8,128)(2,1)S(1)}, bf16[64,1024]{1,0:T(8,128)(2,1)S(1)}, u32[]{:S(2)}, u32[]{:S(2)}) collective-permute-start(bf16[64,1024]{1,0:T(8,128)(2,1)S(1)} %state.1.refs_0_), channel_id=1, source_target_pairs={{0,8},{4,12},{8,0},{12,4},{16,24},{20,28},{24,16},{28,20},{1,9},{5... | collective-permute-start | bytes 393224 | tf_op jit(solution)/shard_map/ppermute | solution.py:21
  97.7 11.5 %collective-permute-start.38 = (bf16[128,1024]{1,0:T(8,128)(2,1)S(1)}, bf16[128,1024]{1,0:T(8,128)(2,1)S(1)}, u32[]{:S(2)}, u32[]{:S(2)}) collective-permute-start(bf16[128,1024]{1,0:T(8,128)(2,1)S(1)} %stack.15.refs_2_), channel_id=1, source_target_pairs={{0,8},{4,12},{8,0},{12,4},{16,24},{20,28},{24,16},{28,20},{1,9},{5... | collective-permute-start | bytes 786440 | tf_op jit(solution)/shard_map/ppermute | solution.py:21
  98.5 11.7 %collective-permute-start.44 = (bf16[128,1024]{1,0:T(8,128)(2,1)S(1)}, bf16[128,1024]{1,0:T(8,128)(2,1)S(1)}, u32[]{:S(2)}, u32[]{:S(2)}) collective-permute-start(bf16[128,1024]{1,0:T(8,128)(2,1)S(1)} %stack.15.refs_2_), channel_id=1, source_target_pairs={{0,4},{4,0},{8,12},{12,8},{16,20},{20,16},{24,28},{28,24},{1,5},{5... | collective-permute-start | bytes 786440 | tf_op jit(solution)/shard_map/ppermute | solution.py:21
  107.1 12.0 %collective-permute-start.26 = (bf16[128,1024]{1,0:T(8,128)(2,1)S(1)}, bf16[128,1024]{1,0:T(8,128)(2,1)S(1)}, u32[]{:S(2)}, u32[]{:S(2)}) collective-permute-start(bf16[128,1024]{1,0:T(8,128)(2,1)S(1)} %stack.15.refs_2_), channel_id=1, source_target_pairs={{0,24},{4,28},{8,16},{12,20},{16,8},{20,12},{24,0},{28,4},{1,25},{... | collective-permute-start | bytes 786440 | tf_op jit(solution)/shard_map/ppermute | solution.py:21
  110.4 13.6 %collective-permute-start.35 = (bf16[128,1024]{1,0:T(8,128)(2,1)S(1)}, bf16[128,1024]{1,0:T(8,128)(2,1)S(1)}, u32[]{:S(2)}, u32[]{:S(2)}) collective-permute-start(bf16[128,1024]{1,0:T(8,128)(2,1)S(1)} %collective-permute-done.32.refs_2_), channel_id=1, source_target_pairs={{0,4},{4,0},{8,12},{12,8},{16,20},{20,16},{24,28},{28,24},{1,5},{5... | collective-permute-start | bytes 786440 | tf_op jit(solution)/shard_map/ppermute | solution.py:21
  139.8 10.9 %collective-permute-start.66 = (bf16[128,1024]{1,0:T(8,128)(2,1)S(1)}, bf16[128,1024]{1,0:T(8,128)(2,1)S(1)}, u32[]{:S(2)}, u32[]{:S(2)}) collective-permute-start(bf16[128,1024]{1,0:T(8,128)(2,1)S(1)} %get-tuple-element.145), channel_id=1, source_target_pairs={{0,4},{4,0},{8,12},{12,8},{16,20},{20,16},{24,28},{28,24},{1,5},{5... | collective-permute-start | bytes 786440 | tf_op jit(solution)/shard_map/ppermute | solution.py:21
  144.0 11.3 %collective-permute-start.61 = (bf16[128,1024]{1,0:T(8,128)(2,1)S(1)}, bf16[128,1024]{1,0:T(8,128)(2,1)S(1)}, u32[]{:S(2)}, u32[]{:S(2)}) collective-permute-start(bf16[128,1024]{1,0:T(8,128)(2,1)S(1)} %add_convert_fusion.3), channel_id=1, source_target_pairs={{0,8},{4,12},{8,0},{12,4},{16,24},{20,28},{24,16},{28,20},{1,9},{5... | collective-permute-start | bytes 786440 | tf_op jit(solution)/shard_map/ppermute | solution.py:21
  146.1 15.5 %collective-permute-start.63 = (bf16[128,1024]{1,0:T(8,128)(2,1)S(1)}, bf16[128,1024]{1,0:T(8,128)(2,1)S(1)}, u32[]{:S(2)}, u32[]{:S(2)}) collective-permute-start(bf16[128,1024]{1,0:T(8,128)(2,1)S(1)} %add_convert_fusion.2), channel_id=1, source_target_pairs={{0,16},{4,20},{8,24},{12,28},{16,0},{20,4},{24,8},{28,12},{1,17},{... | collective-permute-start | bytes 786440 | tf_op jit(solution)/shard_map/ppermute | solution.py:21
  150.4 11.2 %collective-permute-start.65 = (bf16[128,1024]{1,0:T(8,128)(2,1)S(1)}, bf16[128,1024]{1,0:T(8,128)(2,1)S(1)}, u32[]{:S(2)}, u32[]{:S(2)}) collective-permute-start(bf16[128,1024]{1,0:T(8,128)(2,1)S(1)} %add_convert_fusion.1), channel_id=1, source_target_pairs={{0,24},{4,28},{8,16},{12,20},{16,8},{20,12},{24,0},{28,4},{1,25},{... | collective-permute-start | bytes 786440 | tf_op jit(solution)/shard_map/ppermute | solution.py:21
  150.5 14.8 %collective-permute-start.51 = (bf16[64,1024]{1,0:T(8,128)(2,1)S(1)}, bf16[64,1024]{1,0:T(8,128)(2,1)S(1)}, u32[]{:S(2)}, u32[]{:S(2)}) collective-permute-start(bf16[64,1024]{1,0:T(8,128)(2,1)S(1)} %get-tuple-element.129), channel_id=1, source_target_pairs={{0,4},{4,0},{8,12},{12,8},{16,20},{20,16},{24,28},{28,24},{1,5},{5... | collective-permute-start | bytes 393224 | tf_op jit(solution)/shard_map/ppermute | solution.py:21
  150.7 14.7 %collective-permute-start.46 = (bf16[64,1024]{1,0:T(8,128)(2,1)S(1)}, bf16[64,1024]{1,0:T(8,128)(2,1)S(1)}, u32[]{:S(2)}, u32[]{:S(2)}) collective-permute-start(bf16[64,1024]{1,0:T(8,128)(2,1)S(1)} %add_convert_fusion.11), channel_id=1, source_target_pairs={{0,8},{4,12},{8,0},{12,4},{16,24},{20,28},{24,16},{28,20},{1,9},{5... | collective-permute-start | bytes 393224 | tf_op jit(solution)/shard_map/ppermute | solution.py:21
  155.3 12.4 %collective-permute-start.48 = (bf16[64,1024]{1,0:T(8,128)(2,1)S(1)}, bf16[64,1024]{1,0:T(8,128)(2,1)S(1)}, u32[]{:S(2)}, u32[]{:S(2)}) collective-permute-start(bf16[64,1024]{1,0:T(8,128)(2,1)S(1)} %add_convert_fusion.10), channel_id=1, source_target_pairs={{0,16},{4,20},{8,24},{12,28},{16,0},{20,4},{24,8},{28,12},{1,17},{... | collective-permute-start | bytes 393224 | tf_op jit(solution)/shard_map/ppermute | solution.py:21
  (50 other events, 298.8 us)

commit v3 on v2

--- a/solution.py
+++ b/solution.py
@@ -71,46 +71,42 @@
     )(*[in_hbm(array) for array in arrays], *after)
 
 
-def split_kernel(count, steps, place, *refs):
-    sources, outs, sems = refs[:count], refs[-1 - count * steps : -1], refs[-1]
+def split_kernel(count, wanted, place, *refs):
+    sources, outs, sems = refs[:count], refs[-1 - len(wanted) : -1], refs[-1]
     copies = []
-    for n, source in enumerate(sources):
-        width = outs[n * steps].shape[1]
-        for t in range(steps):
-            here = pl.ds(pl.multiple_of((place[0] ^ t) * width, width), width)
-            k = n * steps + t
-            copies.append(pltpu.make_async_copy(source.at[:, here], outs[k], sems.at[k]))
+    for k, ((n, t), out) in enumerate(zip(wanted, outs)):
+        width = out.shape[1]
+        here = pl.ds(pl.multiple_of((place[0] ^ t) * width, width), width)
+        copies.append(pltpu.make_async_copy(sources[n].at[:, here], out, sems.at[k]))
     for copy in copies:
         copy.start()
     for copy in copies:
         copy.wait()
 
 
-def staged_blocks(place, steps, after, *arrays, name):
+def staged_blocks(place, width, after, arrays, wanted, name):
     anywhere = pl.BlockSpec(memory_space=pl.ANY)
-    count = len(arrays)
-    size = sum(math.prod(array.shape) * 2 for array in arrays)
-    blocks = pl.pallas_call(
-        functools.partial(split_kernel, count, steps),
-        out_shape=[
-            jax.ShapeDtypeStruct((array.shape[0], array.shape[1] // steps), array.dtype)
-            for array in arrays
-            for _ in range(steps)
-        ],
-        in_specs=[pl.BlockSpec(memory_space=pltpu.SMEM)] + [anywhere] * (count + len(after)),
-        out_specs=[anywhere] * (count * steps),
-        scratch_shapes=[pltpu.SemaphoreType.DMA((count * steps,))],
+    shapes = [jax.ShapeDtypeStruct((arrays[n].shape[0], width), arrays[n].dtype) for n, _ in wanted]
+    return pl.pallas_call(
+        functools.partial(split_kernel, len(arrays), wanted),
+        out_shape=shapes,
+        in_specs=[pl.BlockSpec(memory_space=pltpu.SMEM)] + [anywhere] * (len(arrays) + len(after)),
+        out_specs=[anywhere] * len(wanted),
+        scratch_shapes=[pltpu.SemaphoreType.DMA((len(wanted),))],
         compiler_params=params(1),
-        cost_estimate=pl.CostEstimate(flops=0, bytes_accessed=size, transcendentals=0),
+        cost_estimate=pl.CostEstimate(
+            flops=0,
+            bytes_accessed=sum(2 * math.prod(shape.shape) for shape in shapes),
+            transcendentals=0,
+        ),
         name=name,
     )(place, *[in_hbm(array) for array in arrays], *after)
-    return [blocks[n * steps : (n + 1) * steps] for n in range(count)]
 
 
 def pack_kernel(page_len, place, lengths, table, queries, out):
     del place
     reqs, slots = table.shape
-    query_rows = queries.shape[0]
+    query_rows = queries.shape[0] * queries.shape[1] // HEAD_DIM
     inverse_rows = out.shape[0] - query_rows
     high = lax.broadcasted_iota(jnp.int32, (inverse_rows, slots), 0)
     lane = lax.broadcasted_iota(jnp.int32, (2 * LO, slots), 0)
@@ -125,7 +121,8 @@
         total += lax.dot_general(
             row_hit, lane_hit, (((1,), (1,)), ((), ())), preferred_element_type=F32
         )
-    out[pl.ds(0, query_rows), :] = queries[...]
+    own = queries[...].astype(F32).reshape(query_rows, HEAD_DIM)
+    out[pl.ds(0, query_rows), :] = own.astype(BF16)
     out[pl.ds(query_rows, inverse_rows), :] = total.astype(BF16)
 
 
@@ -150,10 +147,29 @@
     )(*pieces, *after)
 
 
+def rows_kernel(first, source, out):
+    out[...] = source[pl.ds(first, out.shape[0]), :]
+
+
+def cut_rows(array, first, size):
+    vmem = pl.BlockSpec(memory_space=pltpu.VMEM)
+    return pl.pallas_call(
+        functools.partial(rows_kernel, first),
+        out_shape=jax.ShapeDtypeStruct((size, array.shape[1]), array.dtype),
+        in_specs=[vmem],
+        out_specs=vmem,
+        compiler_params=params(2),
+        name="rows",
+    )(array)
+
+
 def attend_kernel(
-    heads, kv_local, reqs, step_pages, place, near, far, keys, values, *refs
+    devices, heads, kv_local, reqs, step_pages, place, near, far, keys, value_pool, *refs
 ):
-    outs, (query, score, top, weight, acc, found, index, sem) = refs[:-8], refs[-8:]
+    w_out, w_up, refs = refs[0], refs[1], refs[2:]
+    outs, refs = refs[:-11], refs[-11:]
+    outs, w_out_copy, w_up_copies = outs[:devices], outs[devices], outs[devices + 1 :]
+    query, score, top, weight, acc, found, index, values, sem, value_sem, out_sem = refs
     chips = len(outs) // 2
     pages = keys.shape[0]
     steps = pages // step_pages
@@ -164,6 +180,16 @@
     scale = 1.0 / math.sqrt(HEAD_DIM)
     lane = lax.broadcasted_iota(jnp.int32, (heads, HEAD_DIM), 1)
     head = lax.broadcasted_iota(jnp.int32, (heads, HEAD_DIM), 0)
+
+    cut = pages // value_sem.shape[0]
+    loads = [
+        pltpu.make_async_copy(
+            value_pool.at[pl.ds(n * cut, cut)], values.at[pl.ds(n * cut, cut)], value_sem.at[n]
+        )
+        for n in range(value_sem.shape[0])
+    ]
+    for load in loads:
+        load.start()
 
     wanted = place[0] * (pages // LO) + lax.broadcasted_iota(jnp.int32, (8, inverse_rows), 0)
     pick = jnp.where(lax.broadcasted_iota(jnp.int32, (8, inverse_rows), 1) == wanted, 1.0, 0.0)
@@ -215,6 +241,15 @@
             top[at, :] = jnp.maximum(top[at, :], best[p])
 
     top[...] = top[...].astype(BF16).astype(F32)
+    for load in loads:
+        load.wait()
+    weight_loads = [pltpu.make_async_copy(w_out, w_out_copy, out_sem.at[len(w_up_copies)])]
+    for t, copied in enumerate(w_up_copies):
+        width = copied.shape[1]
+        here = pl.ds(pl.multiple_of((place[0] ^ t) * width, width), width)
+        weight_loads.append(pltpu.make_async_copy(w_up.at[:, here], copied, out_sem.at[t]))
+    for load in weight_loads:
+        load.start()
 
     @pl.loop(0, steps)
     def _(step):
@@ -249,12 +284,14 @@
         stats = jnp.where(lane3 == head3 + heads, s_high, stats)
         stats = jnp.where(lane3 == head3, t, stats)
         out[pl.ds(rows, reqs), :] = jnp.sum(stats, axis=1).astype(BF16)
+    for load in weight_loads:
+        load.wait()
 
 
 def combine_kernel(heads, queries, key_new, value_new, *refs):
-    parts, out = refs[2:-1], refs[-1]
-    rows = queries.shape[0]
-    reqs = rows // heads
+    parts, out = refs[1:-1], refs[-1]
+    reqs = key_new.shape[0]
+    rows = reqs * heads
     lane3 = lax.broadcasted_iota(jnp.int32, (reqs, heads, HEAD_DIM), 2)
     head3 = lax.broadcasted_iota(jnp.int32, (reqs, heads, HEAD_DIM), 1)
     diagonal = lane3 == head3
@@ -279,7 +316,7 @@
             axis=1,
         )
 
-    own = queries[...].astype(F32).reshape(reqs, heads, HEAD_DIM) * per_head(key_new)
+    own = queries[pl.ds(0, rows), :].astype(F32).reshape(reqs, heads, HEAD_DIM) * per_head(key_new)
     own = jnp.sum(own, axis=2, keepdims=True) * (1.0 / math.sqrt(HEAD_DIM))
     own = narrow(jnp.broadcast_to(own, (reqs, heads, HEAD_DIM)))
     stats = [part[pl.ds(rows, reqs), :].astype(F32) for part in parts]
@@ -371,12 +408,33 @@
         outs[2][...] = square
 
 
-def down_kernel(bounds, hidden, far, near, *outs):
-    count = len(bounds)
-    for side, weight in enumerate((far, near)):
-        product = jnp.dot(hidden[...], weight[...], preferred_element_type=F32)
-        for (first, size), out in zip(bounds, outs[side * count : (side + 1) * count]):
-            out[...] = product[first : first + size].astype(out.dtype)
+def down_kernel(hidden, far, near, *refs):
+    far_out, near_out = refs[-2:]
+    for weight, out in ((far, far_out), (near, near_out)):
+        out[...] = jnp.dot(hidden[...], weight[...], preferred_element_type=F32).astype(out.dtype)
+
+
+def merge_kernel(block, layout, passed, mine, other, *refs):
+    outs = refs[len(refs) - len(layout) :]
+    for out, blocks in zip(outs, layout):
+        for n, a in enumerate(blocks):
+            here = pl.ds(a * block, block)
+            total = mine[here, :] + other[here, :].astype(F32)
+            if a in passed:
+                total += refs[0][pl.ds(passed.index(a) * block, block), :].astype(F32)
+            out[pl.ds(n * block, block), :] = total.astype(out.dtype)
+
+
+def total_kernel(count, *refs):
+    parts, outs = refs[:count], refs[count:]
+    at = 0
+    for out in outs:
+        here = pl.ds(at, out.shape[0])
+        at += out.shape[0]
+        total = parts[0][here, :]
+        for part in parts[1:]:
+            total = total + part[here, :].astype(F32)
+        out[...] = total.astype(out.dtype)
 
 
 def shards(
@@ -398,7 +456,6 @@
     smem = pl.BlockSpec(memory_space=pltpu.SMEM)
 
     inverse_rows = -(-(pages * req_devices // LO) // 16) * 16
-    own_queries = queries.reshape(rows, HEAD_DIM)
     payload = pl.pallas_call(
         functools.partial(pack_kernel, page_len),
         out_shape=jax.ShapeDtypeStruct((rows + inverse_rows, HEAD_DIM), BF16),
@@ -406,7 +463,7 @@
         out_specs=vmem,
         compiler_params=params(),
         name="pack",
-    )(place, lengths, page_table, own_queries)
+    )(place, in_hbm(lengths), in_hbm(page_table), queries)
     near = [payload] + [swap(payload, "req", 2 * c) for c in range(1, chips)]
     columns = w_out.shape[1]
     gain = pl.pallas_call(
@@ -417,7 +474,7 @@
         compiler_params=params(1),
         name="gain",
     )(norm_gain.reshape(req_devices, columns))
-    keys, values = staged([payload, gain], key_pool, value_pool, name="stage_pools")
+    keys, = staged([payload, gain], key_pool, name="stage_keys")
     near = stacked(near, keys)
     far = swap(near, "req", 1)
 
@@ -425,11 +482,15 @@
     total_rows = rows * req_devices
     anywhere = pl.BlockSpec(memory_space=pl.ANY)
     sent = jax.ShapeDtypeStruct((rows + reqs, HEAD_DIM), BF16)
-    partials = pl.pallas_call(
-        functools.partial(attend_kernel, heads, kv_local, reqs, step_pages),
-        out_shape=[sent] * req_devices,
-        in_specs=[smem, vmem, vmem, vmem, vmem],
-        out_specs=[vmem] * req_devices,
+    copied = jax.ShapeDtypeStruct((hidden_width, columns), BF16)
+    steps, early, w_up = range(req_devices), 3 * req_devices // 8, w_up.T
+    attended = pl.pallas_call(
+        functools.partial(attend_kernel, req_devices, heads, kv_local, reqs, step_pages),
+        out_shape=[sent] * req_devices
+        + [jax.ShapeDtypeStruct(w_out.shape, BF16)]
+        + [copied] * early,
+        in_specs=[smem, vmem, vmem, vmem] + [anywhere] * 3,
+        out_specs=[vmem] * req_devices + [anywhere] * (1 + early),
         scratch_shapes=[
             pltpu.VMEM((total_rows, HEAD_DIM), F32),
             pltpu.VMEM((pages, heads, HEAD_DIM), F32),
@@ -438,14 +499,19 @@
             pltpu.VMEM((total_rows, HEAD_DIM), F32),
             pltpu.VMEM((8, 2 * LO), jnp.int32),
             pltpu.SMEM((8, 2 * LO), jnp.int32),
+            pltpu.VMEM(value_pool.shape, BF16),
             pltpu.SemaphoreType.DMA,
+            pltpu.SemaphoreType.DMA((4,)),
+            pltpu.SemaphoreType.DMA((early + 1,)),
         ],
-        compiler_params=params(16),
+        compiler_params=params(24),
         name="attend",
-    )(place, near, far, keys, values)
-    w_out, = staged([partials[0]], w_out, name="stage_out")
-    w_gate, w_up = staged_blocks(
-        place, req_devices, [partials[0]], w_gate.T, w_up.T, name="stage_hidden"
+    )(place, near, far, keys, in_hbm(value_pool), in_hbm(w_out), in_hbm(w_up))
+    partials, w_out, first_up = (
+        attended[:req_devices], attended[req_devices], attended[req_devices + 1 :]
+    )
+    w_gate = staged_blocks(
+        place, columns, [partials[0]], [w_gate.T], [(0, t) for t in steps], "stage_gate"
     )
 
     near_out, far_out = partials[:chips], partials[chips:]
@@ -455,11 +521,11 @@
     attention = pl.pallas_call(
         functools.partial(combine_kernel, heads),
         out_shape=jax.ShapeDtypeStruct((reqs, heads * HEAD_DIM), BF16),
-        in_specs=[vmem] * 3 + [anywhere] * 2 + [vmem] * len(parts),
+        in_specs=[vmem] * 3 + [anywhere] + [vmem] * len(parts),
         out_specs=vmem,
         compiler_params=params(4),
         name="combine",
-    )(own_queries, key_new, value_new, w_gate[0], w_out, *parts)
+    )(payload, key_new, value_new, w_gate[0], *parts)
 
     near = [attention] + [swap(attention, "req", 2 * c) for c in range(1, chips)]
     far = [swap(x, "req", 1) for x in near]
@@ -476,7 +542,9 @@
         compiler_params=params(5),
         name="project",
     )(place, *near, *far, w_out)
-    w_down, = staged_blocks(place, req_devices, [summed[0]], w_down, name="stage_down")
+    later = [(0, t) for t in steps[early:]] + [(1, t) for t in steps]
+    blocks = staged_blocks(place, columns, [summed[0]], [w_up, w_down], later, "stage_up_down")
+    w_up, w_down = [*first_up, *blocks[: -len(steps)]], blocks[-len(steps) :]
     terms = [summed[0]] + [swap(summed[a], "head", a) for a in range(1, head_devices)]
     state = pl.pallas_call(
         state_kernel,
@@ -487,20 +555,33 @@
         name="state",
     )(w_down[0], residual_in, *terms)
 
-    pieces = {0: state}
-    for a in range(1, head_devices):
-        pieces[a] = swap(state, "head", a)
-    row_groups = [[0], [1], list(range(2, head_devices))]
-    count = len(row_groups)
-    grouped = [
-        pieces[g[0]] if len(g) == 1 else stacked([pieces[a] for a in g]) for g in row_groups
-    ]
-    near = [[x if c == 0 else swap(x, "req", 2 * c) for x in grouped] for c in range(chips)]
-    far = [[swap(x, "req", 1) for x in line] for line in near]
+    pieces = [state] + [swap(state, "head", a) for a in range(1, head_devices)]
+    squares = chips == 4 and head_devices == 4
+
+    def spread(array):
+        return [array] + [swap(array, "req", 2 * c) for c in range(1, chips)]
+
+    if squares:
+        own_x, own_y = swap(state, "req", 2), swap(state, "req", 4)
+        late = stacked(pieces[1:], own_x, own_y)
+        late_x, late_y = swap(late, "req", 2), swap(late, "req", 4)
+        across = [
+            swap(stacked([own_x, cut_rows(late_x, 0, block)]), "req", 4),
+            swap(cut_rows(late_y, block, 2 * block), "req", 2),
+        ]
+        near = [[state, late], [own_x, late_x], [own_y, late_y], across]
+    else:
+        first = spread(state)
+        rest = spread(stacked(pieces[1:], *first[1:]))
+        near = [[first[c], rest[c]] for c in range(chips)]
     all_rows = block * head_devices
     sums = []
     for c in range(chips):
         last = c == chips - 1
+        if squares and last:
+            near[c] = [stacked(near[c], after)]
+        far = [swap(x, "req", 1) for x in near[c]]
+        count = len(far)
         sums = pl.pallas_call(
             functools.partial(hidden_kernel, count, c, last, columns * req_devices),
             out_shape=[jax.ShapeDtypeStruct((all_rows, hidden_width), BF16)]
@@ -513,44 +594,86 @@
             in_specs=[smem] + [vmem] * (2 * count + 5 + len(sums)),
             out_specs=[vmem] if last else [vmem] * 3,
             scratch_shapes=[pltpu.VMEM((2, all_rows, columns), BF16)],
-            input_output_aliases={} if c == 0 or last else {2 * count + 6 + n: n for n in range(3)},
+            input_output_aliases={} if c == 0 or last else {2 * count + 6 + n: n for n in range(2)},
             compiler_params=params(5),
             cost_estimate=pl.CostEstimate(
                 flops=8 * all_rows * columns * hidden_width, bytes_accessed=0, transcendentals=0
             ),
             name="hidden",
         )(
-            place, *near[c], *far[c], gain, *w_gate[2 * c : 2 * c + 2], *w_up[2 * c : 2 * c + 2], *sums
+            place, *near[c], *far, gain, *w_gate[2 * c : 2 * c + 2], *w_up[2 * c : 2 * c + 2], *sums
         )
+        if c == 1:
+            after = sums[2]
     hidden, = sums
 
-    bounds, at = [], 0
-    for g in row_groups:
-        bounds.append((at, len(g) * block))
-        at += len(g) * block
-    shapes = [jax.ShapeDtypeStruct((size, columns), BF16) for _, size in bounds] * 2
-    received = [[] for _ in row_groups]
-    for c in list(range(1, chips)) + [0]:
-        halves = pl.pallas_call(
-            functools.partial(down_kernel, bounds),
-            out_shape=shapes,
-            in_specs=[vmem] * 3,
-            out_specs=[vmem] * len(shapes),
+
+    def down(c, *after):
+        far_part, near_part = pl.pallas_call(
+            down_kernel,
+            out_shape=[
+                jax.ShapeDtypeStruct((all_rows, columns), BF16),
+                jax.ShapeDtypeStruct((all_rows, columns), F32),
+            ],
+            in_specs=[vmem] * 3 + [anywhere] * len(after),
+            out_specs=[vmem] * 2,
             compiler_params=params(5),
             cost_estimate=pl.CostEstimate(
                 flops=4 * all_rows * columns * hidden_width, bytes_accessed=0, transcendentals=0
             ),
             name="down",
-        )(hidden, w_down[2 * c + 1], w_down[2 * c])
-        for g in range(count):
-            both = swap(halves[g], "req", 1).astype(F32) + halves[count + g].astype(F32)
-            received[g].append(both if c == 0 else swap(both.astype(BF16), "req", 2 * c))
-    output = state.astype(F32)
-    for g, arrays in zip(row_groups, received):
-        total = functools.reduce(jnp.add, [x.astype(F32) for x in arrays])
-        for n, a in enumerate(g):
-            part = total[n * block : (n + 1) * block]
-            output += part if a == 0 else swap(part.astype(BF16), "head", a).astype(F32)
+        )(hidden, w_down[2 * c + 1], w_down[2 * c], *after)
+        return near_part, swap(far_part, "req", 1)
+
+    def merge(c, layout, halves, passed=(), extra=()):
+        return pl.pallas_call(
+            functools.partial(merge_kernel, block, layout, passed),
+            out_shape=[
+                jax.ShapeDtypeStruct((len(blocks) * block, columns), BF16 if c else F32)
+                for blocks in layout
+            ],
+            in_specs=[vmem] * (2 + len(extra)),
+            out_specs=[vmem] * len(layout),
+            compiler_params=params(4),
+            name="merge",
+        )(*halves, *extra)
+
+    def total(blocks, parts):
+        return pl.pallas_call(
+            functools.partial(total_kernel, len(parts)),
+            out_shape=[
+                jax.ShapeDtypeStruct((block, columns), BF16 if a else F32) for a in blocks
+            ],
+            in_specs=[vmem] * len(parts),
+            out_specs=[vmem] * len(blocks),
+            compiler_params=params(4),
+            name="total",
+        )(*parts)
+
+    totals = {}
+    if squares:
+        corner = down(3)
+        halves_x = down(1)
+        by_x, by_y = merge(3, [[2, 0], [3, 1]], corner)
+        halves_y = down(2, by_x)
+        halves_own = down(0, by_x)
+        by_x, by_y = swap(by_x, "req", 2), swap(by_y, "req", 4)
+        layout = [[1, 0], [2, 3]]
+        own = merge(0, layout, halves_own)
+        to_x = merge(1, layout, halves_x, (3, 1), (by_y,))
+        to_y = merge(2, layout, halves_y, (2, 0), (by_x,))
+        for n, blocks in enumerate(layout):
+            parts = [own[n], swap(to_x[n], "req", 2), swap(to_y[n], "req", 4)]
+            totals.update(zip(blocks, total(blocks, parts)))
+    else:
+        layout = [list(range(1, head_devices)), [0]]
+        merged = [merge(c, layout, down(c)) for c in range(chips)]
+        for n, blocks in enumerate(layout):
+            parts = [merged[0][n]] + [swap(merged[c][n], "req", 2 * c) for c in range(1, chips)]
+            totals.update(zip(blocks, total(blocks, parts)))
+    output = state.astype(F32) + totals[0]
+    for a in range(head_devices - 1, 0, -1):
+        output += swap(totals[a], "head", a).astype(F32)
     return output.astype(BF16)
 
 

time: 177 us -> 153 us (0.86)
  starting transfers between devices: 57.3 us -> 47.8 us
  Pallas kernels: 61 us -> 54.4 us
  waiting for transfers between devices: 52.8 us -> 46.8 us
    ppermute x69 -> x50, starting transfers between devices: 57.3 us -> 47.8 us  [swap(): return lax.ppermute(array, axis, [(i, i ^ bits) for i in range(size)])]
    ppermute x69 -> x50, waiting for transfers between devices: 52.8 us -> 46.8 us  [swap(): return lax.ppermute(array, axis, [(i, i ^ bits) for i in range(size)])]
    pallas_call x2 -> x1, Pallas kernels: 10.5 us -> 4.69 us  [staged(): pl.pallas_call(functools.partial(stage_kernel, len(arrays), pieces), out_...]
    pallas_call x7 -> x15, Pallas kernels: 33.5 us -> 32.6 us  [the longest x2 14.9 us: staged_blocks(): pl.pallas_call(functools.partial(split_kernel, len(arrays), wanted), out_...]
  transfers between devices with their start and end apart: 69 -> 50, of which waited for: 21 -> 20; matrix products, arithmetic and copies ran while one was open for 1% -> 0% of each run, Pallas kernels for 23% -> 22%
where the time goes in v3:
time: 153 us
  Pallas kernels  54.4 us (36%)
  starting transfers between devices  47.8 us (31%)
  waiting for transfers between devices  46.8 us (31%)
  local copies, waits for them, and re-layouts  2.93 us (2%)
    ppermute x50, starting transfers between devices, swap(): return lax.ppermute(array, axis, [(i, i ^ bits) for i in range(size)])  47.8 us
    ppermute x50, waiting for transfers between devices, swap(): return lax.ppermute(array, axis, [(i, i ^ bits) for i in range(size)])  46.8 us
    pallas_call x2, Pallas kernels, staged_blocks(): pl.pallas_call(functools.partial(split_kernel, len(arrays), wanted), out_...  14.9 us
    pallas_call x4, Pallas kernels, shards(): pl.pallas_call(functools.partial(hidden_kernel, count, c, last, columns *...  12.8 us
    pallas_call x1, Pallas kernels, shards(): pl.pallas_call(functools.partial(attend_kernel, req_devices, heads, kv_lo...  11.9 us
    pallas_call x4, Pallas kernels, down(): pl.pallas_call(down_kernel, out_shape=[jax.ShapeDtypeStruct((all_rows, co...  5.01 us
    pallas_call x1, Pallas kernels, staged(): pl.pallas_call(functools.partial(stage_kernel, len(arrays), pieces), out_...  4.69 us
  transfers between devices with their start and end apart: 50, of which 20 were waited for; matrix products, arithmetic and copies ran while one was open for 0% of the time, Pallas kernels for 22%

profile of v3, /device:TPU:0, one launch (start us, length us, event | category | flops | bytes accessed | tf_op | source)
XLA Modules:
  0.0 153.0 jit_solution(10599931029786212760)
XLA Ops:
  2.4 2.9 %collective-permute-start = (bf16[544,128]{1,0:T(8,128)(2,1)S(1)}, bf16[544,128]{1,0:T(8,128)(2,1)S(1)}, u32[]{:S(2)}, u32[]{:S(2)}) collective-permute-start(bf16[544,128]{1,0:T(8,128)(2,1)S(1)} %pack.1.refs_1_.refs_0_.queries), channel_id=1, source_target_pairs={{0,8},{4,12},{8,0},{12,4},{16,24},{20,28},{24,16},{28,20},{1,9},{5... | collective-permute-start | bytes 417800 | tf_op jit(solution)/shard_map/ppermute | solution.py:21
  7.6 4.7 %stage_keys.1.refs_4_.keys = bf16[192,128,256]{2,1,0:T(8,128)(2,1)S(1)} custom-call(bf16[192,128,256]{2,1,0:T(8,128)(2,1)} %refs_0_.2, bf16[544,128]{1,0:T(8,128)(2,1)S(1)} %pack.1.refs_1_.refs_0_.queries, f32[8,1024]{1,0:T(8,128)S(1)} %gain.1.refs_2_.refs_4_), custom_call_target="tpu_custom_call" | custom-call | bytes 12582912 | tf_op jit(solution)/shard_map/stage_keys/pallas_call | solution.py:62
  13.6 1.9 %collective-permute-done.3.far = bf16[2176,128]{1,0:T(8,128)(2,1)S(1)} collective-permute-done((bf16[2176,128]{1,0:T(8,128)(2,1)S(1)}, bf16[2176,128]{1,0:T(8,128)(2,1)S(1)}, u32[]{:S(2)}, u32[]{:S(2)}) %collective-permute-start.3) | collective-permute-done | bytes 557088 | tf_op jit(solution)/shard_map/ppermute | solution.py:21
  15.5 11.9 %attend.1 = (bf16[544,128]{1,0:T(8,128)(2,1)S(1)}, bf16[544,128]{1,0:T(8,128)(2,1)S(1)}, bf16[544,128]{1,0:T(8,128)(2,1)S(1)}, bf16[544,128]{1,0:T(8,128)(2,1)S(...) custom-call(s32[2]{0:T(128)S(1)} %pad_add_fusion.place, ...), custom_call_target="tpu_custom_call" | custom-call | tf_op jit(solution)/shard_map/attend/pallas_call | solution.py:487
  33.0 2.2 %collective-permute-done.10.refs_8_ = bf16[544,128]{1,0:T(8,128)(2,1)S(1)} collective-permute-done((bf16[544,128]{1,0:T(8,128)(2,1)S(1)}, bf16[544,128]{1,0:T(8,128)(2,1)S(1)}, u32[]{:S(2)}, u32[]{:S(2)}) %collective-permute-start.10) | collective-permute-done | bytes 139296 | tf_op jit(solution)/shard_map/ppermute | solution.py:21
  38.0 6.1 %stage_gate.1 = (bf16[924,1024]{1,0:T(8,128)(2,1)S(1)}, bf16[924,1024]{1,0:T(8,128)(2,1)S(1)}, bf16[924,1024]{1,0:T(8,128)(2,1)S(1)}, bf16[924,1024]{1,0:T(8,128...) custom-call(s32[2]{0:T(128)S(1)} %pad_add_fusion.place, ...), custom_call_target="tpu_custom_call" | custom-call | bytes 15138816 | tf_op jit(solution)/shard_map/stage_gate/pallas_call | solution.py:90
  49.1 2.3 %collective-permute-done.11.refs_1_ = bf16[32,2048]{1,0:T(8,128)(2,1)S(1)} collective-permute-done((bf16[32,2048]{1,0:T(8,128)(2,1)S(1)}, bf16[32,2048]{1,0:T(8,128)(2,1)S(1)}, u32[]{:S(2)}, u32[]{:S(2)}) %collective-permute-start.11) | collective-permute-done | bytes 131104 | tf_op jit(solution)/shard_map/ppermute | solution.py:21
  51.4 3.2 %collective-permute-done.12.refs_2_ = bf16[32,2048]{1,0:T(8,128)(2,1)S(1)} collective-permute-done((bf16[32,2048]{1,0:T(8,128)(2,1)S(1)}, bf16[32,2048]{1,0:T(8,128)(2,1)S(1)}, u32[]{:S(2)}, u32[]{:S(2)}) %collective-permute-start.12) | collective-permute-done | bytes 131104 | tf_op jit(solution)/shard_map/ppermute | solution.py:21
  56.1 1.9 %project.1 = (f32[64,1024]{1,0:T(8,128)S(1)}, bf16[64,1024]{1,0:T(8,128)(2,1)S(1)}, bf16[64,1024]{1,0:T(8,128)(2,1)S(1)}, bf16[64,1024]{1,0:T(8,128)(2,1)S(1)}) custom-call(s32[2]{0:T(128)S(1)} %pad_add_fusion.place, bf16[32,2048]{1,0:T(8,128)(2,1)S(1)} %combine.1.refs_0_, bf16[32,2048]{1,0:T(8,128)(2,1)S(1)} %collective-permute-done.11.refs_1_, ...), custom_call_target="tpu_custom_call" | custom-call | tf_op jit(solution)/shard_map/project/pallas_call | solution.py:533
  59.6 2.6 %collective-permute-start.19 = (bf16[64,1024]{1,0:T(8,128)(2,1)S(1)}, bf16[64,1024]{1,0:T(8,128)(2,1)S(1)}, u32[]{:S(2)}, u32[]{:S(2)}) collective-permute-start(bf16[64,1024]{1,0:T(8,128)(2,1)S(1)} %get-tuple-element.84), channel_id=1, source_target_pairs={{0,2},{1,3},{2,0},{3,1},{4,6},{5,7},{6,4},{7,5},{8,10},{9,11},{10,... | collective-permute-start | bytes 393224 | tf_op jit(solution)/shard_map/ppermute | solution.py:21
  62.4 8.9 %stage_up_down.1 = (bf16[924,1024]{1,0:T(8,128)(2,1)S(1)}, bf16[924,1024]{1,0:T(8,128)(2,1)S(1)}, bf16[924,1024]{1,0:T(8,128)(2,1)S(1)}, bf16[924,1024]{1,0:T(8,...) custom-call(s32[2]{0:T(128)S(1)} %pad_add_fusion.place, ...), custom_call_target="tpu_custom_call" | custom-call | bytes 24600576 | tf_op jit(solution)/shard_map/stage_up_down/pallas_call | solution.py:90
  73.3 2.3 %collective-permute-start.22 = (bf16[64,1024]{1,0:T(8,128)(2,1)S(1)}, bf16[64,1024]{1,0:T(8,128)(2,1)S(1)}, u32[]{:S(2)}, u32[]{:S(2)}) collective-permute-start(bf16[64,1024]{1,0:T(8,128)(2,1)S(1)} %state.1.refs_0_), channel_id=1, source_target_pairs={{0,1},{1,0},{2,3},{3,2},{4,5},{5,4},{6,7},{7,6},{8,9},{9,8},{10,11... | collective-permute-start | bytes 393224 | tf_op jit(solution)/shard_map/ppermute | solution.py:21
  78.1 1.8 %collective-permute-start.25 = (bf16[64,1024]{1,0:T(8,128)(2,1)S(1)}, bf16[64,1024]{1,0:T(8,128)(2,1)S(1)}, u32[]{:S(2)}, u32[]{:S(2)}) collective-permute-start(bf16[64,1024]{1,0:T(8,128)(2,1)S(1)} %state.1.refs_0_), channel_id=1, source_target_pairs={{0,16},{4,20},{8,24},{12,28},{16,0},{20,4},{24,8},{28,12},{1,17},{... | collective-permute-start | bytes 393224 | tf_op jit(solution)/shard_map/ppermute | solution.py:21
  79.9 7.7 %collective-permute-done.23.refs_1_ = bf16[64,1024]{1,0:T(8,128)(2,1)S(1)} collective-permute-done((bf16[64,1024]{1,0:T(8,128)(2,1)S(1)}, bf16[64,1024]{1,0:T(8,128)(2,1)S(1)}, u32[]{:S(2)}, u32[]{:S(2)}) %collective-permute-start.23) | collective-permute-done | bytes 131104 | tf_op jit(solution)/shard_map/ppermute | solution.py:21
  90.4 5.0 %collective-permute-done.26.source.refs_1_ = bf16[192,1024]{1,0:T(8,128)(2,1)S(1)} collective-permute-done((bf16[192,1024]{1,0:T(8,128)(2,1)S(1)}, bf16[192,1024]{1,0:T(8,128)(2,1)S(1)}, u32[]{:S(2)}, u32[]{:S(2)}) %collective-permute-start.26) | collective-permute-done | bytes 393248 | tf_op jit(solution)/shard_map/ppermute | solution.py:21
  99.4 3.0 %hidden.4 = (f32[256,924]{1,0:T(8,128)S(1)}, f32[256,924]{1,0:T(8,128)S(1)}, f32[256,128]{1,0:T(8,128)S(1)}) custom-call(s32[2]{0:T(128)S(1)} %pad_add_fusion.place, bf16[64,1024]{1,0:T(8,128)(2,1)S(1)} %state.1.refs_0_, bf16[192,1024]{1,0:T(8,128)(2,1)S(1)} %stack.17.refs_1_, bf16[64,1024]{1,0:T(8,128)(2,1)S(1)} %collective-permute-done.32.refs_2_, ...), custom_call_target="tpu_custom_call" | custom-call | flops 1937768448 | tf_op jit(solution)/shard_map/hidden/pallas_call | solution.py:585
  102.4 3.2 %hidden.5 = (f32[256,924]{1,0:T(8,128)S(1)}, f32[256,924]{1,0:T(8,128)S(1)}, f32[256,128]{1,0:T(8,128)S(1)}) custom-call(s32[2]{0:T(128)S(1)} %pad_add_fusion.place, bf16[64,1024]{1,0:T(8,128)(2,1)S(1)} %collective-permute-done.21.refs_3_.refs_0_, ...), custom_call_target="tpu_custom_call", output_to_operand_aliasing={{0}: (10, {}), {1}: (11, {})} | custom-call | flops 1937768448 | tf_op jit(solution)/shard_map/hidden/pallas_call | solution.py:585
  108.7 3.4 %hidden.6 = (f32[256,924]{1,0:T(8,128)S(1)}, f32[256,924]{1,0:T(8,128)S(1)}, f32[256,128]{1,0:T(8,128)S(1)}) custom-call(s32[2]{0:T(128)S(1)} %pad_add_fusion.place, bf16[64,1024]{1,0:T(8,128)(2,1)S(1)} %collective-permute-done.25.refs_4_.refs_0_, ...), custom_call_target="tpu_custom_call", output_to_operand_aliasing={{0}: (10, {}), {1}: (11, {})} | custom-call | flops 1937768448 | tf_op jit(solution)/shard_map/hidden/pallas_call | solution.py:585
  112.1 3.2 %hidden.7 = bf16[256,924]{1,0:T(8,128)(2,1)S(1)} custom-call(s32[2]{0:T(128)S(1)} %pad_add_fusion.place, bf16[256,1024]{1,0:T(8,128)(2,1)S(1)} %stack.19.refs_0_, bf16[256,1024]{1,0:T(8,128)(2,1)S(1)} %collective-permute-done.34.refs_1_, f32[8,1024]{1,0:T(8,128)S(1)} %gain.1.refs_2_.refs_4_, bf16[924,1024]{1,0:T(8,128)(2,1)S(1)} %get-tuple-element.97.refs_3_, ...), custom_call_target="tpu_custom_call" | custom-call | flops 1937768448 | tf_op jit(solution)/shard_map/hidden/pallas_call | solution.py:585
  123.5 5.9 %collective-permute-done.40.refs_0_ = bf16[128,1024]{1,0:T(8,128)(2,1)S(1)} collective-permute-done((bf16[128,1024]{1,0:T(8,128)(2,1)S(1)}, bf16[128,1024]{1,0:T(8,128)(2,1)S(1)}, u32[]{:S(2)}, u32[]{:S(2)}) %collective-permute-start.40) | collective-permute-done | bytes 262176 | tf_op jit(solution)/shard_map/ppermute | solution.py:21
  133.9 4.9 %collective-permute-done.45.refs_1_ = bf16[128,1024]{1,0:T(8,128)(2,1)S(1)} collective-permute-done((bf16[128,1024]{1,0:T(8,128)(2,1)S(1)}, bf16[128,1024]{1,0:T(8,128)(2,1)S(1)}, u32[]{:S(2)}, u32[]{:S(2)}) %collective-permute-start.45) | collective-permute-done | bytes 262176 | tf_op jit(solution)/shard_map/ppermute | solution.py:21
  140.2 3.5 %collective-permute-start.47 = (bf16[64,1024]{1,0:T(8,128)(2,1)S(1)}, bf16[64,1024]{1,0:T(8,128)(2,1)S(1)}, u32[]{:S(2)}, u32[]{:S(2)}) collective-permute-start(bf16[64,1024]{1,0:T(8,128)(2,1)S(1)} %get-tuple-element.134), channel_id=1, source_target_pairs={{0,3},{1,2},{2,1},{3,0},{4,7},{5,6},{6,5},{7,4},{8,11},{9,10},{10,... | collective-permute-start | bytes 393224 | tf_op jit(solution)/shard_map/ppermute | solution.py:21
  143.7 2.0 %collective-permute-start.48 = (bf16[64,1024]{1,0:T(8,128)(2,1)S(1)}, bf16[64,1024]{1,0:T(8,128)(2,1)S(1)}, u32[]{:S(2)}, u32[]{:S(2)}) collective-permute-start(bf16[64,1024]{1,0:T(8,128)(2,1)S(1)} %get-tuple-element.135), channel_id=1, source_target_pairs={{0,2},{1,3},{2,0},{3,1},{4,6},{5,7},{6,4},{7,5},{8,10},{9,11},{10,... | collective-permute-start | bytes 393224 | tf_op jit(solution)/shard_map/ppermute | solution.py:21
  147.8 4.5 %collective-permute-done.48 = bf16[64,1024]{1,0:T(8,128)(2,1)S(1)} collective-permute-done((bf16[64,1024]{1,0:T(8,128)(2,1)S(1)}, bf16[64,1024]{1,0:T(8,128)(2,1)S(1)}, u32[]{:S(2)}, u32[]{:S(2)}) %collective-permute-start.48) | collective-permute-done | bytes 131104 | tf_op jit(solution)/shard_map/ppermute | solution.py:21
  (120 shorter events, 53.9 us)
Async XLA Ops:
  2.4 9.9 %collective-permute-start = (bf16[544,128]{1,0:T(8,128)(2,1)S(1)}, bf16[544,128]{1,0:T(8,128)(2,1)S(1)}, u32[]{:S(2)}, u32[]{:S(2)}) collective-permute-start(bf16[544,128]{1,0:T(8,128)(2,1)S(1)} %pack.1.refs_1_.refs_0_.queries), channel_id=1, source_target_pairs={{0,8},{4,12},{8,0},{12,4},{16,24},{20,28},{24,16},{28,20},{1,9},{5... | collective-permute-start | bytes 417800 | tf_op jit(solution)/shard_map/ppermute | solution.py:21
  30.6 13.5 %collective-permute-start.5 = (bf16[544,128]{1,0:T(8,128)(2,1)S(1)}, bf16[544,128]{1,0:T(8,128)(2,1)S(1)}, u32[]{:S(2)}, u32[]{:S(2)}) collective-permute-start(bf16[544,128]{1,0:T(8,128)(2,1)S(1)} %get-tuple-element.74), channel_id=1, source_target_pairs={{0,8},{4,12},{8,0},{12,4},{16,24},{20,28},{24,16},{28,20},{1,9},{5... | collective-permute-start | bytes 417800 | tf_op jit(solution)/shard_map/ppermute | solution.py:21
  31.8 12.3 %collective-permute-start.6 = (bf16[544,128]{1,0:T(8,128)(2,1)S(1)}, bf16[544,128]{1,0:T(8,128)(2,1)S(1)}, u32[]{:S(2)}, u32[]{:S(2)}) collective-permute-start(bf16[544,128]{1,0:T(8,128)(2,1)S(1)} %get-tuple-element.75), channel_id=1, source_target_pairs={{0,12},{4,8},{8,4},{12,0},{16,28},{20,24},{24,20},{28,16},{1,13},{... | collective-permute-start | bytes 417800 | tf_op jit(solution)/shard_map/ppermute | solution.py:21
  32.1 12.0 %collective-permute-start.7 = (bf16[544,128]{1,0:T(8,128)(2,1)S(1)}, bf16[544,128]{1,0:T(8,128)(2,1)S(1)}, u32[]{:S(2)}, u32[]{:S(2)}) collective-permute-start(bf16[544,128]{1,0:T(8,128)(2,1)S(1)} %get-tuple-element.76), channel_id=1, source_target_pairs={{0,16},{4,20},{8,24},{12,28},{16,0},{20,4},{24,8},{28,12},{1,17},{... | collective-permute-start | bytes 417800 | tf_op jit(solution)/shard_map/ppermute | solution.py:21
  35.3 8.9 %collective-permute-start.8 = (bf16[544,128]{1,0:T(8,128)(2,1)S(1)}, bf16[544,128]{1,0:T(8,128)(2,1)S(1)}, u32[]{:S(2)}, u32[]{:S(2)}) collective-permute-start(bf16[544,128]{1,0:T(8,128)(2,1)S(1)} %get-tuple-element.77), channel_id=1, source_target_pairs={{0,20},{4,16},{8,28},{12,24},{16,4},{20,0},{24,12},{28,8},{1,21},{... | collective-permute-start | bytes 417800 | tf_op jit(solution)/shard_map/ppermute | solution.py:21
  58.0 13.3 %collective-permute-start.18 = (bf16[64,1024]{1,0:T(8,128)(2,1)S(1)}, bf16[64,1024]{1,0:T(8,128)(2,1)S(1)}, u32[]{:S(2)}, u32[]{:S(2)}) collective-permute-start(bf16[64,1024]{1,0:T(8,128)(2,1)S(1)} %get-tuple-element.83), channel_id=1, source_target_pairs={{0,1},{1,0},{2,3},{3,2},{4,5},{5,4},{6,7},{7,6},{8,9},{9,8},{10,11... | collective-permute-start | bytes 393224 | tf_op jit(solution)/shard_map/ppermute | solution.py:21
  59.6 12.9 %collective-permute-start.19 = (bf16[64,1024]{1,0:T(8,128)(2,1)S(1)}, bf16[64,1024]{1,0:T(8,128)(2,1)S(1)}, u32[]{:S(2)}, u32[]{:S(2)}) collective-permute-start(bf16[64,1024]{1,0:T(8,128)(2,1)S(1)} %get-tuple-element.84), channel_id=1, source_target_pairs={{0,2},{1,3},{2,0},{3,1},{4,6},{5,7},{6,4},{7,5},{8,10},{9,11},{10,... | collective-permute-start | bytes 393224 | tf_op jit(solution)/shard_map/ppermute | solution.py:21
  62.2 10.3 %collective-permute-start.20 = (bf16[64,1024]{1,0:T(8,128)(2,1)S(1)}, bf16[64,1024]{1,0:T(8,128)(2,1)S(1)}, u32[]{:S(2)}, u32[]{:S(2)}) collective-permute-start(bf16[64,1024]{1,0:T(8,128)(2,1)S(1)} %get-tuple-element.85), channel_id=1, source_target_pairs={{0,3},{1,2},{2,1},{3,0},{4,7},{5,6},{6,5},{7,4},{8,11},{9,10},{10,... | collective-permute-start | bytes 393224 | tf_op jit(solution)/shard_map/ppermute | solution.py:21
  75.6 11.9 %collective-permute-start.23 = (bf16[64,1024]{1,0:T(8,128)(2,1)S(1)}, bf16[64,1024]{1,0:T(8,128)(2,1)S(1)}, u32[]{:S(2)}, u32[]{:S(2)}) collective-permute-start(bf16[64,1024]{1,0:T(8,128)(2,1)S(1)} %state.1.refs_0_), channel_id=1, source_target_pairs={{0,2},{1,3},{2,0},{3,1},{4,6},{5,7},{6,4},{7,5},{8,10},{9,11},{10,... | collective-permute-start | bytes 393224 | tf_op jit(solution)/shard_map/ppermute | solution.py:21
  76.6 10.9 %collective-permute-start.24 = (bf16[64,1024]{1,0:T(8,128)(2,1)S(1)}, bf16[64,1024]{1,0:T(8,128)(2,1)S(1)}, u32[]{:S(2)}, u32[]{:S(2)}) collective-permute-start(bf16[64,1024]{1,0:T(8,128)(2,1)S(1)} %state.1.refs_0_), channel_id=1, source_target_pairs={{0,3},{1,2},{2,1},{3,0},{4,7},{5,6},{6,5},{7,4},{8,11},{9,10},{10,... | collective-permute-start | bytes 393224 | tf_op jit(solution)/shard_map/ppermute | solution.py:21
  78.1 9.4 %collective-permute-start.25 = (bf16[64,1024]{1,0:T(8,128)(2,1)S(1)}, bf16[64,1024]{1,0:T(8,128)(2,1)S(1)}, u32[]{:S(2)}, u32[]{:S(2)}) collective-permute-start(bf16[64,1024]{1,0:T(8,128)(2,1)S(1)} %state.1.refs_0_), channel_id=1, source_target_pairs={{0,16},{4,20},{8,24},{12,28},{16,0},{20,4},{24,8},{28,12},{1,17},{... | collective-permute-start | bytes 393224 | tf_op jit(solution)/shard_map/ppermute | solution.py:21
  90.4 9.0 %collective-permute-start.33 = (bf16[192,1024]{1,0:T(8,128)(2,1)S(1)}, bf16[192,1024]{1,0:T(8,128)(2,1)S(1)}, u32[]{:S(2)}, u32[]{:S(2)}) collective-permute-start(bf16[192,1024]{1,0:T(8,128)(2,1)S(1)} %stack.17.refs_1_), channel_id=1, source_target_pairs={{0,4},{4,0},{8,12},{12,8},{16,20},{20,16},{24,28},{28,24},{1,5},{5... | collective-permute-start | bytes 1179656 | tf_op jit(solution)/shard_map/ppermute | solution.py:21
  97.1 8.5 %collective-permute-start.27 = (bf16[128,1024]{1,0:T(8,128)(2,1)S(1)}, bf16[128,1024]{1,0:T(8,128)(2,1)S(1)}, u32[]{:S(2)}, u32[]{:S(2)}) collective-permute-start(bf16[128,1024]{1,0:T(8,128)(2,1)S(1)} %stack.18), channel_id=1, source_target_pairs={{0,16},{4,20},{8,24},{12,28},{16,0},{20,4},{24,8},{28,12},{1,17},{... | collective-permute-start | bytes 786440 | tf_op jit(solution)/shard_map/ppermute | solution.py:21
  98.2 8.2 %collective-permute-start.29 = (bf16[128,1024]{1,0:T(8,128)(2,1)S(1)}, bf16[128,1024]{1,0:T(8,128)(2,1)S(1)}, u32[]{:S(2)}, u32[]{:S(2)}) collective-permute-start(bf16[128,1024]{1,0:T(8,128)(2,1)S(1)} %rows.3), channel_id=1, source_target_pairs={{0,8},{4,12},{8,0},{12,4},{16,24},{20,28},{24,16},{28,20},{1,9},{5... | collective-permute-start | bytes 786440 | tf_op jit(solution)/shard_map/ppermute | solution.py:21
  99.4 9.2 %collective-permute-start.36 = (bf16[192,1024]{1,0:T(8,128)(2,1)S(1)}, bf16[192,1024]{1,0:T(8,128)(2,1)S(1)}, u32[]{:S(2)}, u32[]{:S(2)}) collective-permute-start(bf16[192,1024]{1,0:T(8,128)(2,1)S(1)} %collective-permute-done.28.source.refs_1_), channel_id=1, source_target_pairs={{0,4},{4,0},{8,12},{12,8},{16,20},{20,16},{24,28},{28,24},{1,5},{5... | collective-permute-start | bytes 1179656 | tf_op jit(solution)/shard_map/ppermute | solution.py:21
  119.9 10.7 %collective-permute-start.42 = (bf16[256,1024]{1,0:T(8,128)(2,1)S(1)}, bf16[256,1024]{1,0:T(8,128)(2,1)S(1)}, u32[]{:S(2)}, u32[]{:S(2)}) collective-permute-start(bf16[256,1024]{1,0:T(8,128)(2,1)S(1)} %get-tuple-element.128), channel_id=1, source_target_pairs={{0,4},{4,0},{8,12},{12,8},{16,20},{20,16},{24,28},{28,24},{1,5},{5... | collective-permute-start | bytes 1572872 | tf_op jit(solution)/shard_map/ppermute | solution.py:21
  120.1 10.5 %collective-permute-start.43 = (bf16[128,1024]{1,0:T(8,128)(2,1)S(1)}, bf16[128,1024]{1,0:T(8,128)(2,1)S(1)}, u32[]{:S(2)}, u32[]{:S(2)}) collective-permute-start(bf16[128,1024]{1,0:T(8,128)(2,1)S(1)} %get-tuple-element.115.refs_0_), channel_id=1, source_target_pairs={{0,8},{4,12},{8,0},{12,4},{16,24},{20,28},{24,16},{28,20},{1,9},{5... | collective-permute-start | bytes 786440 | tf_op jit(solution)/shard_map/ppermute | solution.py:21
  121.0 8.3 %collective-permute-start.40 = (bf16[128,1024]{1,0:T(8,128)(2,1)S(1)}, bf16[128,1024]{1,0:T(8,128)(2,1)S(1)}, u32[]{:S(2)}, u32[]{:S(2)}) collective-permute-start(bf16[128,1024]{1,0:T(8,128)(2,1)S(1)} %get-tuple-element.123), channel_id=1, source_target_pairs={{0,16},{4,20},{8,24},{12,28},{16,0},{20,4},{24,8},{28,12},{1,17},{... | collective-permute-start | bytes 786440 | tf_op jit(solution)/shard_map/ppermute | solution.py:21
  123.4 10.4 %collective-permute-start.38 = (bf16[256,1024]{1,0:T(8,128)(2,1)S(1)}, bf16[256,1024]{1,0:T(8,128)(2,1)S(1)}, u32[]{:S(2)}, u32[]{:S(2)}) collective-permute-start(bf16[256,1024]{1,0:T(8,128)(2,1)S(1)} %get-tuple-element.117), channel_id=1, source_target_pairs={{0,4},{4,0},{8,12},{12,8},{16,20},{20,16},{24,28},{28,24},{1,5},{5... | collective-permute-start | bytes 1572872 | tf_op jit(solution)/shard_map/ppermute | solution.py:21
  129.5 9.3 %collective-permute-start.45 = (bf16[128,1024]{1,0:T(8,128)(2,1)S(1)}, bf16[128,1024]{1,0:T(8,128)(2,1)S(1)}, u32[]{:S(2)}, u32[]{:S(2)}) collective-permute-start(bf16[128,1024]{1,0:T(8,128)(2,1)S(1)} %get-tuple-element.132), channel_id=1, source_target_pairs={{0,8},{4,12},{8,0},{12,4},{16,24},{20,28},{24,16},{28,20},{1,9},{5... | collective-permute-start | bytes 786440 | tf_op jit(solution)/shard_map/ppermute | solution.py:21
  130.8 9.3 %collective-permute-start.46 = (bf16[128,1024]{1,0:T(8,128)(2,1)S(1)}, bf16[128,1024]{1,0:T(8,128)(2,1)S(1)}, u32[]{:S(2)}, u32[]{:S(2)}) collective-permute-start(bf16[128,1024]{1,0:T(8,128)(2,1)S(1)} %get-tuple-element.133), channel_id=1, source_target_pairs={{0,16},{4,20},{8,24},{12,28},{16,0},{20,4},{24,8},{28,12},{1,17},{... | collective-permute-start | bytes 786440 | tf_op jit(solution)/shard_map/ppermute | solution.py:21
  132.0 13.8 %collective-permute-start.41 = (bf16[128,1024]{1,0:T(8,128)(2,1)S(1)}, bf16[128,1024]{1,0:T(8,128)(2,1)S(1)}, u32[]{:S(2)}, u32[]{:S(2)}) collective-permute-start(bf16[128,1024]{1,0:T(8,128)(2,1)S(1)} %get-tuple-element.124), channel_id=1, source_target_pairs={{0,8},{4,12},{8,0},{12,4},{16,24},{20,28},{24,16},{28,20},{1,9},{5... | collective-permute-start | bytes 786440 | tf_op jit(solution)/shard_map/ppermute | solution.py:21
  132.9 12.9 %collective-permute-start.44 = (bf16[128,1024]{1,0:T(8,128)(2,1)S(1)}, bf16[128,1024]{1,0:T(8,128)(2,1)S(1)}, u32[]{:S(2)}, u32[]{:S(2)}) collective-permute-start(bf16[128,1024]{1,0:T(8,128)(2,1)S(1)} %get-tuple-element.129), channel_id=1, source_target_pairs={{0,16},{4,20},{8,24},{12,28},{16,0},{20,4},{24,8},{28,12},{1,17},{... | collective-permute-start | bytes 786440 | tf_op jit(solution)/shard_map/ppermute | solution.py:21
  143.7 8.5 %collective-permute-start.48 = (bf16[64,1024]{1,0:T(8,128)(2,1)S(1)}, bf16[64,1024]{1,0:T(8,128)(2,1)S(1)}, u32[]{:S(2)}, u32[]{:S(2)}) collective-permute-start(bf16[64,1024]{1,0:T(8,128)(2,1)S(1)} %get-tuple-element.135), channel_id=1, source_target_pairs={{0,2},{1,3},{2,0},{3,1},{4,6},{5,7},{6,4},{7,5},{8,10},{9,11},{10,... | collective-permute-start | bytes 393224 | tf_op jit(solution)/shard_map/ppermute | solution.py:21
  (32 other events, 197.6 us)

commit v4 on v3

--- a/solution.py
+++ b/solution.py
@@ -288,6 +288,36 @@
         load.wait()
 
 
+def join_kernel(heads, reqs, *refs):
+    count = len(refs) // 3
+    rows = reqs * heads
+    lane = lax.broadcasted_iota(jnp.int32, (reqs, HEAD_DIM), 1)
+    lane3 = lax.broadcasted_iota(jnp.int32, (reqs, heads, HEAD_DIM), 2)
+    head3 = lax.broadcasted_iota(jnp.int32, (reqs, heads, HEAD_DIM), 1)
+
+    def wide(array):
+        return jnp.sum(jnp.where(lane3 == head3, array[:, None, :], 0.0), axis=2, keepdims=True)
+
+    for n in range(count):
+        pair, out = (refs[n], refs[count + n]), refs[2 * count + n]
+        stats = [ref[pl.ds(rows, reqs), :].astype(F32) for ref in pair]
+        best = jnp.maximum(*stats)
+        weight, acc = 0.0, 0.0
+        for stat, ref in zip(stats, pair):
+            factor = jnp.exp(stat - best)
+            weight += factor * (
+                pltpu.roll(stat, HEAD_DIM - heads, 1) + pltpu.roll(stat, HEAD_DIM - 2 * heads, 1)
+            )
+            part = ref[pl.ds(0, rows), :].astype(F32).reshape(reqs, heads, HEAD_DIM)
+            acc += wide(factor) * part
+        high = weight.astype(BF16).astype(F32)
+        low = pltpu.roll(weight - high, 2 * heads, 1)
+        joined = jnp.where(lane < 2 * heads, pltpu.roll(high, heads, 1), low)
+        joined = jnp.where(lane < heads, best, jnp.where(lane < 3 * heads, joined, 0.0))
+        out[pl.ds(0, rows), :] = acc.reshape(rows, HEAD_DIM).astype(BF16)
+        out[pl.ds(rows, reqs), :] = joined.astype(BF16)
+
+
 def combine_kernel(heads, queries, key_new, value_new, *refs):
     parts, out = refs[1:-1], refs[-1]
     reqs = key_new.shape[0]
@@ -366,13 +396,13 @@
     out[...] = gain[...].astype(F32)
 
 
-def hidden_kernel(groups, chip, last, total_width, place, *refs):
+def hidden_kernel(groups, waits, chip, last, total_width, place, *refs):
     pieces, refs = refs[: 2 * groups], refs[2 * groups :]
     gain, w_gate, w_up = refs[0], refs[1:3], refs[3:5]
     before = refs[5:8] if chip else None
-    outs, lines = refs[8 if chip else 5 : -1], refs[-1]
-    width = lines.shape[2]
-    rows, units = outs[0].shape
+    outs, lines = refs[(8 if chip else 5) + waits : -1], refs[-1]
+    rows = lines.shape[1]
+    units = w_gate[0].shape[0]
     contract = (((1,), (1,)), ((), ()))
     square = [None] * groups
     for side in range(2):
@@ -387,23 +417,25 @@
     square = jnp.broadcast_to(jnp.concatenate(square, axis=0), (rows, HEAD_DIM))
     if before is not None:
         square = square + before[2][...]
-    factor = lax.rsqrt(square[:, 0:1] * (1.0 / total_width) + NORM_EPS)
+    if last:
+        factor = lax.rsqrt(square.T[0:1, :] * (1.0 / total_width) + NORM_EPS)
     for first in range(0, units, 512):
         here = slice(first, min(first + 512, units))
         sums = []
         for n, weight in enumerate((w_gate, w_up)):
-            total = None if before is None else before[n][:, here]
+            total = None if before is None else before[n][here, :]
             for side in range(2):
                 part = lax.dot_general(
-                    lines[side], weight[side][here, :], contract, preferred_element_type=F32
+                    weight[side][here, :], lines[side], contract, preferred_element_type=F32
                 )
                 total = part if total is None else total + part
             sums.append(total)
         if last:
             gate = sums[0] * factor
-            outs[0][:, here] = (gate / (1.0 + jnp.exp(-gate)) * (sums[1] * factor)).astype(BF16)
+            hidden = gate / (1.0 + jnp.exp(-gate)) * (sums[1] * factor)
+            outs[0][:, here] = hidden.T.astype(BF16)
         else:
-            outs[0][:, here], outs[1][:, here] = sums
+            outs[0][here, :], outs[1][here, :] = sums
     if not last:
         outs[2][...] = square
 
@@ -510,14 +542,19 @@
     partials, w_out, first_up = (
         attended[:req_devices], attended[req_devices], attended[req_devices + 1 :]
     )
+    joined = pl.pallas_call(
+        functools.partial(join_kernel, heads, reqs),
+        out_shape=[sent] * chips,
+        in_specs=[vmem] * (2 * chips),
+        out_specs=[vmem] * chips,
+        compiler_params=params(6),
+        name="join",
+    )(*partials[:chips], *[swap(part, "req", 1) for part in partials[chips:]])
     w_gate = staged_blocks(
-        place, columns, [partials[0]], [w_gate.T], [(0, t) for t in steps], "stage_gate"
+        place, columns, [joined[0]], [w_gate.T], [(0, t) for t in steps], "stage_gate"
     )
 
-    near_out, far_out = partials[:chips], partials[chips:]
-    parts = [near_out[0], swap(far_out[0], "req", 1)]
-    for c in range(1, chips):
-        parts += [swap(near_out[c], "req", 2 * c), swap(far_out[c], "req", 2 * c + 1)]
+    parts = [joined[0]] + [swap(joined[c], "req", 2 * c) for c in range(1, chips)]
     attention = pl.pallas_call(
         functools.partial(combine_kernel, heads),
         out_shape=jax.ShapeDtypeStruct((reqs, heads * HEAD_DIM), BF16),
@@ -557,41 +594,42 @@
 
     pieces = [state] + [swap(state, "head", a) for a in range(1, head_devices)]
     squares = chips == 4 and head_devices == 4
+    order = [0, 3, 2, 1] if squares else list(range(head_devices))
 
     def spread(array):
         return [array] + [swap(array, "req", 2 * c) for c in range(1, chips)]
 
     if squares:
         own_x, own_y = swap(state, "req", 2), swap(state, "req", 4)
-        late = stacked(pieces[1:], own_x, own_y)
+        own_corner = swap(own_x, "req", 4)
+        late = stacked([pieces[a] for a in order[1:]], own_x, own_y, own_corner)
+        half = late.shape[0] // 2
         late_x, late_y = swap(late, "req", 2), swap(late, "req", 4)
-        across = [
-            swap(stacked([own_x, cut_rows(late_x, 0, block)]), "req", 4),
-            swap(cut_rows(late_y, block, 2 * block), "req", 2),
-        ]
-        near = [[state, late], [own_x, late_x], [own_y, late_y], across]
+        near = [[state, late], [own_x, late_x], [own_y, late_y], []]
     else:
         first = spread(state)
         rest = spread(stacked(pieces[1:], *first[1:]))
         near = [[first[c], rest[c]] for c in range(chips)]
     all_rows = block * head_devices
-    sums = []
+    sums, square = [], []
+    early_far = {c: [swap(near[c][0], "req", 1)] for c in range(chips - 1)} if squares else {}
     for c in range(chips):
         last = c == chips - 1
         if squares and last:
-            near[c] = [stacked(near[c], after)]
-        far = [swap(x, "req", 1) for x in near[c]]
+            near[c] = [stacked(across, square[2])]
+        far = early_far.get(c, []) + [swap(x, "req", 1) for x in near[c][len(early_far.get(c, [])) :]]
         count = len(far)
+        ready = [x for n in sorted(early_far) if n for x in early_far[n]] if c == 0 else []
         sums = pl.pallas_call(
-            functools.partial(hidden_kernel, count, c, last, columns * req_devices),
+            functools.partial(hidden_kernel, count, len(ready), c, last, columns * req_devices),
             out_shape=[jax.ShapeDtypeStruct((all_rows, hidden_width), BF16)]
             if last
             else [
-                jax.ShapeDtypeStruct((all_rows, hidden_width), F32),
-                jax.ShapeDtypeStruct((all_rows, hidden_width), F32),
+                jax.ShapeDtypeStruct((hidden_width, all_rows), F32),
+                jax.ShapeDtypeStruct((hidden_width, all_rows), F32),
                 jax.ShapeDtypeStruct((all_rows, HEAD_DIM), F32),
             ],
-            in_specs=[smem] + [vmem] * (2 * count + 5 + len(sums)),
+            in_specs=[smem] + [vmem] * (2 * count + 5 + len(sums)) + [anywhere] * len(ready),
             out_specs=[vmem] if last else [vmem] * 3,
             scratch_shapes=[pltpu.VMEM((2, all_rows, columns), BF16)],
             input_output_aliases={} if c == 0 or last else {2 * count + 6 + n: n for n in range(2)},
@@ -601,10 +639,18 @@
             ),
             name="hidden",
         )(
-            place, *near[c], *far, gain, *w_gate[2 * c : 2 * c + 2], *w_up[2 * c : 2 * c + 2], *sums
+            place, *near[c], *far, gain, *w_gate[2 * c : 2 * c + 2], *w_up[2 * c : 2 * c + 2], *sums, *ready
         )
-        if c == 1:
-            after = sums[2]
+        if not last:
+            square.append(sums[2])
+        if squares and c == 0:
+            late_x, late_y = stacked([late_x], square[0]), stacked([late_y], square[0])
+            near[1][1], near[2][1] = late_x, late_y
+            across = [
+                own_corner,
+                swap(cut_rows(late_x, 0, half), "req", 4),
+                swap(cut_rows(late_y, half, half), "req", 2),
+            ]
     hidden, = sums
 
 
@@ -618,14 +664,14 @@
             in_specs=[vmem] * 3 + [anywhere] * len(after),
             out_specs=[vmem] * 2,
             compiler_params=params(5),
-            cost_estimate=pl.CostEstimate(
-                flops=4 * all_rows * columns * hidden_width, bytes_accessed=0, transcendentals=0
-            ),
+            cost_estimate=pl.CostEstimate(flops=1, bytes_accessed=1, transcendentals=0),
             name="down",
         )(hidden, w_down[2 * c + 1], w_down[2 * c], *after)
         return near_part, swap(far_part, "req", 1)
 
     def merge(c, layout, halves, passed=(), extra=()):
+        layout = [[order.index(a) for a in blocks] for blocks in layout]
+        passed = [order.index(a) for a in passed]
         return pl.pallas_call(
             functools.partial(merge_kernel, block, layout, passed),
             out_shape=[

time: 153 us -> 147 us (0.961)
  starting transfers between devices: 47.8 us -> 42.3 us
    ppermute x50 -> x51, starting transfers between devices: 47.8 us -> 42.3 us  [swap(): return lax.ppermute(array, axis, [(i, i ^ bits) for i in range(size)])]
    ppermute x50 -> x51, waiting for transfers between devices: 46.8 us -> 47.5 us  [swap(): return lax.ppermute(array, axis, [(i, i ^ bits) for i in range(size)])]
    pallas_call x4 -> x5, Pallas kernels: 12.8 us -> 12.9 us  [the longest x4 12 us: shards(): pl.pallas_call(functools.partial(hidden_kernel, count, len(ready), c, las...]
  transfers between devices with their start and end apart: 50 -> 51, of which waited for: 20 -> 26; matrix products, arithmetic and copies ran while one was open for 0% -> 0% of each run, Pallas kernels for 22% -> 22%
where the time goes in v4:
time: 147 us
  Pallas kernels  54.2 us (37%)
  waiting for transfers between devices  47.5 us (32%)
  starting transfers between devices  42.3 us (29%)
  local copies, waits for them, and re-layouts  1.64 us (1%)
    ppermute x51, waiting for transfers between devices, swap(): return lax.ppermute(array, axis, [(i, i ^ bits) for i in range(size)])  47.5 us
    ppermute x51, starting transfers between devices, swap(): return lax.ppermute(array, axis, [(i, i ^ bits) for i in range(size)])  42.3 us
    pallas_call x2, Pallas kernels, staged_blocks(): pl.pallas_call(functools.partial(split_kernel, len(arrays), wanted), out_...  14.9 us
    pallas_call x4, Pallas kernels, shards(): pl.pallas_call(functools.partial(hidden_kernel, count, len(ready), c, las...  12 us
    pallas_call x1, Pallas kernels, shards(): pl.pallas_call(functools.partial(attend_kernel, req_devices, heads, kv_lo...  11.9 us
    pallas_call x4, Pallas kernels, down(): pl.pallas_call(down_kernel, out_shape=[jax.ShapeDtypeStruct((all_rows, co...  5 us
    pallas_call x1, Pallas kernels, staged(): pl.pallas_call(functools.partial(stage_kernel, len(arrays), pieces), out_...  4.69 us
  transfers between devices with their start and end apart: 51, of which 26 were waited for; matrix products, arithmetic and copies ran while one was open for 0% of the time, Pallas kernels for 22%

profile of v4, /device:TPU:0, one launch (start us, length us, event | category | flops | bytes accessed | tf_op | source)
XLA Modules:
  0.0 146.8 jit_solution(10426627428473998230)
XLA Ops:
  2.4 2.9 %collective-permute-start = (bf16[544,128]{1,0:T(8,128)(2,1)S(1)}, bf16[544,128]{1,0:T(8,128)(2,1)S(1)}, u32[]{:S(2)}, u32[]{:S(2)}) collective-permute-start(bf16[544,128]{1,0:T(8,128)(2,1)S(1)} %pack.1.refs_1_.refs_0_.queries), channel_id=1, source_target_pairs={{0,8},{4,12},{8,0},{12,4},{16,24},{20,28},{24,16},{28,20},{1,9},{5... | collective-permute-start | bytes 417800 | tf_op jit(solution)/shard_map/ppermute | solution.py:21
  7.6 4.7 %stage_keys.1.refs_4_.keys = bf16[192,128,256]{2,1,0:T(8,128)(2,1)S(1)} custom-call(bf16[192,128,256]{2,1,0:T(8,128)(2,1)} %refs_0_.2, bf16[544,128]{1,0:T(8,128)(2,1)S(1)} %pack.1.refs_1_.refs_0_.queries, f32[8,1024]{1,0:T(8,128)S(1)} %gain.1.refs_2_.refs_4_), custom_call_target="tpu_custom_call" | custom-call | bytes 12582912 | tf_op jit(solution)/shard_map/stage_keys/pallas_call | solution.py:62
  13.6 1.9 %collective-permute-done.3.far = bf16[2176,128]{1,0:T(8,128)(2,1)S(1)} collective-permute-done((bf16[2176,128]{1,0:T(8,128)(2,1)S(1)}, bf16[2176,128]{1,0:T(8,128)(2,1)S(1)}, u32[]{:S(2)}, u32[]{:S(2)}) %collective-permute-start.3) | collective-permute-done | bytes 557088 | tf_op jit(solution)/shard_map/ppermute | solution.py:21
  15.5 11.9 %attend.1 = (bf16[544,128]{1,0:T(8,128)(2,1)S(1)}, bf16[544,128]{1,0:T(8,128)(2,1)S(1)}, bf16[544,128]{1,0:T(8,128)(2,1)S(1)}, bf16[544,128]{1,0:T(8,128)(2,1)S(...) custom-call(s32[2]{0:T(128)S(1)} %pad_add_fusion.place, ...), custom_call_target="tpu_custom_call" | custom-call | tf_op jit(solution)/shard_map/attend/pallas_call | solution.py:519
  30.4 1.9 %collective-permute-start.10 = (bf16[544,128]{1,0:T(8,128)(2,1)S(1)}, bf16[544,128]{1,0:T(8,128)(2,1)S(1)}, u32[]{:S(2)}, u32[]{:S(2)}) collective-permute-start(bf16[544,128]{1,0:T(8,128)(2,1)S(1)} %get-tuple-element.87), channel_id=1, source_target_pairs={{0,24},{4,28},{8,16},{12,20},{16,8},{20,12},{24,0},{28,4},{1,25},{... | collective-permute-start | bytes 417800 | tf_op jit(solution)/shard_map/ppermute | solution.py:21
  34.0 6.1 %stage_gate.1 = (bf16[924,1024]{1,0:T(8,128)(2,1)S(1)}, bf16[924,1024]{1,0:T(8,128)(2,1)S(1)}, bf16[924,1024]{1,0:T(8,128)(2,1)S(1)}, bf16[924,1024]{1,0:T(8,128...) custom-call(s32[2]{0:T(128)S(1)} %pad_add_fusion.place, ...), custom_call_target="tpu_custom_call" | custom-call | bytes 15138816 | tf_op jit(solution)/shard_map/stage_gate/pallas_call | solution.py:90
  44.6 2.3 %collective-permute-done.11.refs_1_ = bf16[32,2048]{1,0:T(8,128)(2,1)S(1)} collective-permute-done((bf16[32,2048]{1,0:T(8,128)(2,1)S(1)}, bf16[32,2048]{1,0:T(8,128)(2,1)S(1)}, u32[]{:S(2)}, u32[]{:S(2)}) %collective-permute-start.11) | collective-permute-done | bytes 131104 | tf_op jit(solution)/shard_map/ppermute | solution.py:21
  46.8 2.0 %collective-permute-done.12.refs_2_ = bf16[32,2048]{1,0:T(8,128)(2,1)S(1)} collective-permute-done((bf16[32,2048]{1,0:T(8,128)(2,1)S(1)}, bf16[32,2048]{1,0:T(8,128)(2,1)S(1)}, u32[]{:S(2)}, u32[]{:S(2)}) %collective-permute-start.12) | collective-permute-done | bytes 131104 | tf_op jit(solution)/shard_map/ppermute | solution.py:21
  55.0 2.6 %collective-permute-start.19 = (bf16[64,1024]{1,0:T(8,128)(2,1)S(1)}, bf16[64,1024]{1,0:T(8,128)(2,1)S(1)}, u32[]{:S(2)}, u32[]{:S(2)}) collective-permute-start(bf16[64,1024]{1,0:T(8,128)(2,1)S(1)} %get-tuple-element.92), channel_id=1, source_target_pairs={{0,2},{1,3},{2,0},{3,1},{4,6},{5,7},{6,4},{7,5},{8,10},{9,11},{10,... | collective-permute-start | bytes 393224 | tf_op jit(solution)/shard_map/ppermute | solution.py:21
  57.8 8.9 %stage_up_down.1 = (bf16[924,1024]{1,0:T(8,128)(2,1)S(1)}, bf16[924,1024]{1,0:T(8,128)(2,1)S(1)}, bf16[924,1024]{1,0:T(8,128)(2,1)S(1)}, bf16[924,1024]{1,0:T(8,...) custom-call(s32[2]{0:T(128)S(1)} %pad_add_fusion.place, ...), custom_call_target="tpu_custom_call" | custom-call | bytes 24600576 | tf_op jit(solution)/shard_map/stage_up_down/pallas_call | solution.py:90
  68.9 2.5 %collective-permute-start.23 = (bf16[64,1024]{1,0:T(8,128)(2,1)S(1)}, bf16[64,1024]{1,0:T(8,128)(2,1)S(1)}, u32[]{:S(2)}, u32[]{:S(2)}) collective-permute-start(bf16[64,1024]{1,0:T(8,128)(2,1)S(1)} %state.1.refs_0_), channel_id=1, source_target_pairs={{0,3},{1,2},{2,1},{3,0},{4,7},{5,6},{6,5},{7,4},{8,11},{9,10},{10,... | collective-permute-start | bytes 393224 | tf_op jit(solution)/shard_map/ppermute | solution.py:21
  77.1 5.3 %collective-permute-done.24.refs_1_ = bf16[64,1024]{1,0:T(8,128)(2,1)S(1)} collective-permute-done((bf16[64,1024]{1,0:T(8,128)(2,1)S(1)}, bf16[64,1024]{1,0:T(8,128)(2,1)S(1)}, u32[]{:S(2)}, u32[]{:S(2)}) %collective-permute-start.24) | collective-permute-done | bytes 131104 | tf_op jit(solution)/shard_map/ppermute | solution.py:21
  86.8 2.8 %hidden.4 = (f32[924,256]{1,0:T(8,128)S(1)}, f32[924,256]{1,0:T(8,128)S(1)}, f32[256,128]{1,0:T(8,128)S(1)}) custom-call(s32[2]{0:T(128)S(1)} %pad_add_fusion.place, bf16[64,1024]{1,0:T(8,128)(2,1)S(1)} %state.1.refs_0_, bf16[192,1024]{1,0:T(8,128)(2,1)S(1)} %stack.18.refs_1_, bf16[64,1024]{1,0:T(8,128)(2,1)S(1)} %collective-permute-done.28.refs_2_, ...), custom_call_target="tpu_custom_call" | custom-call | flops 1937768448 | tf_op jit(solution)/shard_map/hidden/pallas_call | solution.py:623
  89.6 4.5 %collective-permute-done.27.refs_0_ = bf16[192,1024]{1,0:T(8,128)(2,1)S(1)} collective-permute-done((bf16[192,1024]{1,0:T(8,128)(2,1)S(1)}, bf16[192,1024]{1,0:T(8,128)(2,1)S(1)}, u32[]{:S(2)}, u32[]{:S(2)}) %collective-permute-start.27) | collective-permute-done | bytes 393248 | tf_op jit(solution)/shard_map/ppermute | solution.py:21
  94.2 2.1 %collective-permute-done.33.refs_0_ = bf16[192,1024]{1,0:T(8,128)(2,1)S(1)} collective-permute-done((bf16[192,1024]{1,0:T(8,128)(2,1)S(1)}, bf16[192,1024]{1,0:T(8,128)(2,1)S(1)}, u32[]{:S(2)}, u32[]{:S(2)}) %collective-permute-start.33) | collective-permute-done | bytes 393248 | tf_op jit(solution)/shard_map/ppermute | solution.py:21
  99.4 3.0 %hidden.5 = (f32[924,256]{1,0:T(8,128)S(1)}, f32[924,256]{1,0:T(8,128)S(1)}, f32[256,128]{1,0:T(8,128)S(1)}) custom-call(s32[2]{0:T(128)S(1)} %pad_add_fusion.place, bf16[64,1024]{1,0:T(8,128)(2,1)S(1)} %collective-permute-done.21.refs_3_.refs_0_, bf16[192,1024]{1,0:T(8,128)(2,1)S(1)} %stack.19.source.refs_1_, ...), custom_call_target="tpu_custom_call", output_to_operand_aliasing={{0}: (10, {}), {1}: (11, {})} | custom-call | flops 1937768448 | tf_op jit(solution)/shard_map/hidden/pallas_call | solution.py:623
  102.3 3.0 %hidden.6 = (f32[924,256]{1,0:T(8,128)S(1)}, f32[924,256]{1,0:T(8,128)S(1)}, f32[256,128]{1,0:T(8,128)S(1)}) custom-call(s32[2]{0:T(128)S(1)} %pad_add_fusion.place, bf16[64,1024]{1,0:T(8,128)(2,1)S(1)} %collective-permute-done.26.refs_4_.refs_0_, bf16[192,1024]{1,0:T(8,128)(2,1)S(1)} %stack.20.source.refs_1_, ...), custom_call_target="tpu_custom_call", output_to_operand_aliasing={{0}: (10, {}), {1}: (11, {})} | custom-call | flops 1937768448 | tf_op jit(solution)/shard_map/hidden/pallas_call | solution.py:623
  105.5 1.9 %collective-permute-done.37.refs_1_ = bf16[256,1024]{1,0:T(8,128)(2,1)S(1)} collective-permute-done((bf16[256,1024]{1,0:T(8,128)(2,1)S(1)}, bf16[256,1024]{1,0:T(8,128)(2,1)S(1)}, u32[]{:S(2)}, u32[]{:S(2)}) %collective-permute-start.37) | collective-permute-done | bytes 524320 | tf_op jit(solution)/shard_map/ppermute | solution.py:21
  107.4 3.3 %hidden.7 = bf16[256,924]{1,0:T(8,128)(2,1)S(1)} custom-call(s32[2]{0:T(128)S(1)} %pad_add_fusion.place, bf16[256,1024]{1,0:T(8,128)(2,1)S(1)} %stack.21.refs_0_, bf16[256,1024]{1,0:T(8,128)(2,1)S(1)} %collective-permute-done.37.refs_1_, f32[8,1024]{1,0:T(8,128)S(1)} %gain.1.refs_2_.refs_4_, bf16[924,1024]{1,0:T(8,128)(2,1)S(1)} %get-tuple-element.112.refs_3_, ...), custom_call_target="tpu_custom_call" | custom-call | flops 1937768448 | tf_op jit(solution)/shard_map/hidden/pallas_call | solution.py:623
  118.7 5.3 %collective-permute-done.41.refs_0_ = bf16[128,1024]{1,0:T(8,128)(2,1)S(1)} collective-permute-done((bf16[128,1024]{1,0:T(8,128)(2,1)S(1)}, bf16[128,1024]{1,0:T(8,128)(2,1)S(1)}, u32[]{:S(2)}, u32[]{:S(2)}) %collective-permute-start.41) | collective-permute-done | bytes 262176 | tf_op jit(solution)/shard_map/ppermute | solution.py:21
  128.6 4.9 %collective-permute-done.46.refs_1_ = bf16[128,1024]{1,0:T(8,128)(2,1)S(1)} collective-permute-done((bf16[128,1024]{1,0:T(8,128)(2,1)S(1)}, bf16[128,1024]{1,0:T(8,128)(2,1)S(1)}, u32[]{:S(2)}, u32[]{:S(2)}) %collective-permute-start.46) | collective-permute-done | bytes 262176 | tf_op jit(solution)/shard_map/ppermute | solution.py:21
  134.7 3.4 %collective-permute-start.48 = (bf16[64,1024]{1,0:T(8,128)(2,1)S(1)}, bf16[64,1024]{1,0:T(8,128)(2,1)S(1)}, u32[]{:S(2)}, u32[]{:S(2)}) collective-permute-start(bf16[64,1024]{1,0:T(8,128)(2,1)S(1)} %get-tuple-element.142), channel_id=1, source_target_pairs={{0,3},{1,2},{2,1},{3,0},{4,7},{5,6},{6,5},{7,4},{8,11},{9,10},{10,... | collective-permute-start | bytes 393224 | tf_op jit(solution)/shard_map/ppermute | solution.py:21
  139.3 2.7 %collective-permute-done.48 = bf16[64,1024]{1,0:T(8,128)(2,1)S(1)} collective-permute-done((bf16[64,1024]{1,0:T(8,128)(2,1)S(1)}, bf16[64,1024]{1,0:T(8,128)(2,1)S(1)}, u32[]{:S(2)}, u32[]{:S(2)}) %collective-permute-start.48) | collective-permute-done | bytes 131104 | tf_op jit(solution)/shard_map/ppermute | solution.py:21
  142.0 3.7 %collective-permute-done.49 = bf16[64,1024]{1,0:T(8,128)(2,1)S(1)} collective-permute-done((bf16[64,1024]{1,0:T(8,128)(2,1)S(1)}, bf16[64,1024]{1,0:T(8,128)(2,1)S(1)}, u32[]{:S(2)}, u32[]{:S(2)}) %collective-permute-start.49) | collective-permute-done | bytes 131104 | tf_op jit(solution)/shard_map/ppermute | solution.py:21
  (120 shorter events, 53.0 us)
Async XLA Ops:
  2.4 9.9 %collective-permute-start = (bf16[544,128]{1,0:T(8,128)(2,1)S(1)}, bf16[544,128]{1,0:T(8,128)(2,1)S(1)}, u32[]{:S(2)}, u32[]{:S(2)}) collective-permute-start(bf16[544,128]{1,0:T(8,128)(2,1)S(1)} %pack.1.refs_1_.refs_0_.queries), channel_id=1, source_target_pairs={{0,8},{4,12},{8,0},{12,4},{16,24},{20,28},{24,16},{28,20},{1,9},{5... | collective-permute-start | bytes 417800 | tf_op jit(solution)/shard_map/ppermute | solution.py:21
  5.3 8.1 %collective-permute-start.1 = (bf16[544,128]{1,0:T(8,128)(2,1)S(1)}, bf16[544,128]{1,0:T(8,128)(2,1)S(1)}, u32[]{:S(2)}, u32[]{:S(2)}) collective-permute-start(bf16[544,128]{1,0:T(8,128)(2,1)S(1)} %pack.1.refs_1_.refs_0_.queries), channel_id=1, source_target_pairs={{0,16},{4,20},{8,24},{12,28},{16,0},{20,4},{24,8},{28,12},{1,17},{... | collective-permute-start | bytes 417800 | tf_op jit(solution)/shard_map/ppermute | solution.py:21
  30.4 9.6 %collective-permute-start.10 = (bf16[544,128]{1,0:T(8,128)(2,1)S(1)}, bf16[544,128]{1,0:T(8,128)(2,1)S(1)}, u32[]{:S(2)}, u32[]{:S(2)}) collective-permute-start(bf16[544,128]{1,0:T(8,128)(2,1)S(1)} %get-tuple-element.87), channel_id=1, source_target_pairs={{0,24},{4,28},{8,16},{12,20},{16,8},{20,12},{24,0},{28,4},{1,25},{... | collective-permute-start | bytes 417800 | tf_op jit(solution)/shard_map/ppermute | solution.py:21
  32.3 8.1 %collective-permute-start.8 = (bf16[544,128]{1,0:T(8,128)(2,1)S(1)}, bf16[544,128]{1,0:T(8,128)(2,1)S(1)}, u32[]{:S(2)}, u32[]{:S(2)}) collective-permute-start(bf16[544,128]{1,0:T(8,128)(2,1)S(1)} %get-tuple-element.85), channel_id=1, source_target_pairs={{0,8},{4,12},{8,0},{12,4},{16,24},{20,28},{24,16},{28,20},{1,9},{5... | collective-permute-start | bytes 417800 | tf_op jit(solution)/shard_map/ppermute | solution.py:21
  53.4 13.3 %collective-permute-start.18 = (bf16[64,1024]{1,0:T(8,128)(2,1)S(1)}, bf16[64,1024]{1,0:T(8,128)(2,1)S(1)}, u32[]{:S(2)}, u32[]{:S(2)}) collective-permute-start(bf16[64,1024]{1,0:T(8,128)(2,1)S(1)} %get-tuple-element.91), channel_id=1, source_target_pairs={{0,1},{1,0},{2,3},{3,2},{4,5},{5,4},{6,7},{7,6},{8,9},{9,8},{10,11... | collective-permute-start | bytes 393224 | tf_op jit(solution)/shard_map/ppermute | solution.py:21
  55.0 12.9 %collective-permute-start.19 = (bf16[64,1024]{1,0:T(8,128)(2,1)S(1)}, bf16[64,1024]{1,0:T(8,128)(2,1)S(1)}, u32[]{:S(2)}, u32[]{:S(2)}) collective-permute-start(bf16[64,1024]{1,0:T(8,128)(2,1)S(1)} %get-tuple-element.92), channel_id=1, source_target_pairs={{0,2},{1,3},{2,0},{3,1},{4,6},{5,7},{6,4},{7,5},{8,10},{9,11},{10,... | collective-permute-start | bytes 393224 | tf_op jit(solution)/shard_map/ppermute | solution.py:21
  57.6 10.3 %collective-permute-start.20 = (bf16[64,1024]{1,0:T(8,128)(2,1)S(1)}, bf16[64,1024]{1,0:T(8,128)(2,1)S(1)}, u32[]{:S(2)}, u32[]{:S(2)}) collective-permute-start(bf16[64,1024]{1,0:T(8,128)(2,1)S(1)} %get-tuple-element.93), channel_id=1, source_target_pairs={{0,3},{1,2},{2,1},{3,0},{4,7},{5,6},{6,5},{7,4},{8,11},{9,10},{10,... | collective-permute-start | bytes 393224 | tf_op jit(solution)/shard_map/ppermute | solution.py:21
  68.9 8.2 %collective-permute-start.23 = (bf16[64,1024]{1,0:T(8,128)(2,1)S(1)}, bf16[64,1024]{1,0:T(8,128)(2,1)S(1)}, u32[]{:S(2)}, u32[]{:S(2)}) collective-permute-start(bf16[64,1024]{1,0:T(8,128)(2,1)S(1)} %state.1.refs_0_), channel_id=1, source_target_pairs={{0,3},{1,2},{2,1},{3,0},{4,7},{5,6},{6,5},{7,4},{8,11},{9,10},{10,... | collective-permute-start | bytes 393224 | tf_op jit(solution)/shard_map/ppermute | solution.py:21
  71.4 11.1 %collective-permute-start.24 = (bf16[64,1024]{1,0:T(8,128)(2,1)S(1)}, bf16[64,1024]{1,0:T(8,128)(2,1)S(1)}, u32[]{:S(2)}, u32[]{:S(2)}) collective-permute-start(bf16[64,1024]{1,0:T(8,128)(2,1)S(1)} %state.1.refs_0_), channel_id=1, source_target_pairs={{0,2},{1,3},{2,0},{3,1},{4,6},{5,7},{6,4},{7,5},{8,10},{9,11},{10,... | collective-permute-start | bytes 393224 | tf_op jit(solution)/shard_map/ppermute | solution.py:21
  72.7 9.8 %collective-permute-start.25 = (bf16[64,1024]{1,0:T(8,128)(2,1)S(1)}, bf16[64,1024]{1,0:T(8,128)(2,1)S(1)}, u32[]{:S(2)}, u32[]{:S(2)}) collective-permute-start(bf16[64,1024]{1,0:T(8,128)(2,1)S(1)} %state.1.refs_0_), channel_id=1, source_target_pairs={{0,1},{1,0},{2,3},{3,2},{4,5},{5,4},{6,7},{7,6},{8,9},{9,8},{10,11... | collective-permute-start | bytes 393224 | tf_op jit(solution)/shard_map/ppermute | solution.py:21
  73.3 9.2 %collective-permute-start.26 = (bf16[64,1024]{1,0:T(8,128)(2,1)S(1)}, bf16[64,1024]{1,0:T(8,128)(2,1)S(1)}, u32[]{:S(2)}, u32[]{:S(2)}) collective-permute-start(bf16[64,1024]{1,0:T(8,128)(2,1)S(1)} %state.1.refs_0_), channel_id=1, source_target_pairs={{0,16},{4,20},{8,24},{12,28},{16,0},{20,4},{24,8},{28,12},{1,17},{... | collective-permute-start | bytes 393224 | tf_op jit(solution)/shard_map/ppermute | solution.py:21
  82.6 11.5 %collective-permute-start.27 = (bf16[192,1024]{1,0:T(8,128)(2,1)S(1)}, bf16[192,1024]{1,0:T(8,128)(2,1)S(1)}, u32[]{:S(2)}, u32[]{:S(2)}) collective-permute-start(bf16[192,1024]{1,0:T(8,128)(2,1)S(1)} %stack.18.refs_1_), channel_id=1, source_target_pairs={{0,8},{4,12},{8,0},{12,4},{16,24},{20,28},{24,16},{28,20},{1,9},{5... | collective-permute-start | bytes 1179656 | tf_op jit(solution)/shard_map/ppermute | solution.py:21
  85.2 11.2 %collective-permute-start.33 = (bf16[192,1024]{1,0:T(8,128)(2,1)S(1)}, bf16[192,1024]{1,0:T(8,128)(2,1)S(1)}, u32[]{:S(2)}, u32[]{:S(2)}) collective-permute-start(bf16[192,1024]{1,0:T(8,128)(2,1)S(1)} %stack.18.refs_1_), channel_id=1, source_target_pairs={{0,16},{4,20},{8,24},{12,28},{16,0},{20,4},{24,8},{28,12},{1,17},{... | collective-permute-start | bytes 1179656 | tf_op jit(solution)/shard_map/ppermute | solution.py:21
  96.5 8.8 %collective-permute-start.34 = (bf16[96,1024]{1,0:T(8,128)(2,1)S(1)}, bf16[96,1024]{1,0:T(8,128)(2,1)S(1)}, u32[]{:S(2)}, u32[]{:S(2)}) collective-permute-start(bf16[96,1024]{1,0:T(8,128)(2,1)S(1)} %rows.3), channel_id=1, source_target_pairs={{0,8},{4,12},{8,0},{12,4},{16,24},{20,28},{24,16},{28,20},{1,9},{5... | collective-permute-start | bytes 589832 | tf_op jit(solution)/shard_map/ppermute | solution.py:21
  97.6 7.7 %collective-permute-start.32 = (bf16[96,1024]{1,0:T(8,128)(2,1)S(1)}, bf16[96,1024]{1,0:T(8,128)(2,1)S(1)}, u32[]{:S(2)}, u32[]{:S(2)}) collective-permute-start(bf16[96,1024]{1,0:T(8,128)(2,1)S(1)} %rows.2), channel_id=1, source_target_pairs={{0,16},{4,20},{8,24},{12,28},{16,0},{20,4},{24,8},{28,12},{1,17},{... | collective-permute-start | bytes 589832 | tf_op jit(solution)/shard_map/ppermute | solution.py:21
  115.3 9.9 %collective-permute-start.43 = (bf16[256,1024]{1,0:T(8,128)(2,1)S(1)}, bf16[256,1024]{1,0:T(8,128)(2,1)S(1)}, u32[]{:S(2)}, u32[]{:S(2)}) collective-permute-start(bf16[256,1024]{1,0:T(8,128)(2,1)S(1)} %get-tuple-element.136), channel_id=1, source_target_pairs={{0,4},{4,0},{8,12},{12,8},{16,20},{20,16},{24,28},{28,24},{1,5},{5... | collective-permute-start | bytes 1572872 | tf_op jit(solution)/shard_map/ppermute | solution.py:21
  115.5 8.6 %collective-permute-start.41 = (bf16[128,1024]{1,0:T(8,128)(2,1)S(1)}, bf16[128,1024]{1,0:T(8,128)(2,1)S(1)}, u32[]{:S(2)}, u32[]{:S(2)}) collective-permute-start(bf16[128,1024]{1,0:T(8,128)(2,1)S(1)} %get-tuple-element.131), channel_id=1, source_target_pairs={{0,16},{4,20},{8,24},{12,28},{16,0},{20,4},{24,8},{28,12},{1,17},{... | collective-permute-start | bytes 786440 | tf_op jit(solution)/shard_map/ppermute | solution.py:21
  116.5 8.6 %collective-permute-start.44 = (bf16[128,1024]{1,0:T(8,128)(2,1)S(1)}, bf16[128,1024]{1,0:T(8,128)(2,1)S(1)}, u32[]{:S(2)}, u32[]{:S(2)}) collective-permute-start(bf16[128,1024]{1,0:T(8,128)(2,1)S(1)} %get-tuple-element.123.refs_0_), channel_id=1, source_target_pairs={{0,8},{4,12},{8,0},{12,4},{16,24},{20,28},{24,16},{28,20},{1,9},{5... | collective-permute-start | bytes 786440 | tf_op jit(solution)/shard_map/ppermute | solution.py:21
  118.6 9.9 %collective-permute-start.39 = (bf16[256,1024]{1,0:T(8,128)(2,1)S(1)}, bf16[256,1024]{1,0:T(8,128)(2,1)S(1)}, u32[]{:S(2)}, u32[]{:S(2)}) collective-permute-start(bf16[256,1024]{1,0:T(8,128)(2,1)S(1)} %get-tuple-element.125), channel_id=1, source_target_pairs={{0,4},{4,0},{8,12},{12,8},{16,20},{20,16},{24,28},{28,24},{1,5},{5... | collective-permute-start | bytes 1572872 | tf_op jit(solution)/shard_map/ppermute | solution.py:21
  124.2 9.3 %collective-permute-start.46 = (bf16[128,1024]{1,0:T(8,128)(2,1)S(1)}, bf16[128,1024]{1,0:T(8,128)(2,1)S(1)}, u32[]{:S(2)}, u32[]{:S(2)}) collective-permute-start(bf16[128,1024]{1,0:T(8,128)(2,1)S(1)} %get-tuple-element.140), channel_id=1, source_target_pairs={{0,8},{4,12},{8,0},{12,4},{16,24},{20,28},{24,16},{28,20},{1,9},{5... | collective-permute-start | bytes 786440 | tf_op jit(solution)/shard_map/ppermute | solution.py:21
  125.3 9.3 %collective-permute-start.47 = (bf16[128,1024]{1,0:T(8,128)(2,1)S(1)}, bf16[128,1024]{1,0:T(8,128)(2,1)S(1)}, u32[]{:S(2)}, u32[]{:S(2)}) collective-permute-start(bf16[128,1024]{1,0:T(8,128)(2,1)S(1)} %get-tuple-element.141), channel_id=1, source_target_pairs={{0,16},{4,20},{8,24},{12,28},{16,0},{20,4},{24,8},{28,12},{1,17},{... | collective-permute-start | bytes 786440 | tf_op jit(solution)/shard_map/ppermute | solution.py:21
  126.3 11.7 %collective-permute-start.42 = (bf16[128,1024]{1,0:T(8,128)(2,1)S(1)}, bf16[128,1024]{1,0:T(8,128)(2,1)S(1)}, u32[]{:S(2)}, u32[]{:S(2)}) collective-permute-start(bf16[128,1024]{1,0:T(8,128)(2,1)S(1)} %get-tuple-element.132), channel_id=1, source_target_pairs={{0,8},{4,12},{8,0},{12,4},{16,24},{20,28},{24,16},{28,20},{1,9},{5... | collective-permute-start | bytes 786440 | tf_op jit(solution)/shard_map/ppermute | solution.py:21
  127.5 10.9 %collective-permute-start.45 = (bf16[128,1024]{1,0:T(8,128)(2,1)S(1)}, bf16[128,1024]{1,0:T(8,128)(2,1)S(1)}, u32[]{:S(2)}, u32[]{:S(2)}) collective-permute-start(bf16[128,1024]{1,0:T(8,128)(2,1)S(1)} %get-tuple-element.137), channel_id=1, source_target_pairs={{0,16},{4,20},{8,24},{12,28},{16,0},{20,4},{24,8},{28,12},{1,17},{... | collective-permute-start | bytes 786440 | tf_op jit(solution)/shard_map/ppermute | solution.py:21
  138.0 7.6 %collective-permute-start.49 = (bf16[64,1024]{1,0:T(8,128)(2,1)S(1)}, bf16[64,1024]{1,0:T(8,128)(2,1)S(1)}, u32[]{:S(2)}, u32[]{:S(2)}) collective-permute-start(bf16[64,1024]{1,0:T(8,128)(2,1)S(1)} %get-tuple-element.143), channel_id=1, source_target_pairs={{0,2},{1,3},{2,0},{3,1},{4,6},{5,7},{6,4},{7,5},{8,10},{9,11},{10,... | collective-permute-start | bytes 393224 | tf_op jit(solution)/shard_map/ppermute | solution.py:21
  (31 other events, 136.4 us)

commit v5 on v4

--- a/solution.py
+++ b/solution.py
@@ -419,8 +419,8 @@
         square = square + before[2][...]
     if last:
         factor = lax.rsqrt(square.T[0:1, :] * (1.0 / total_width) + NORM_EPS)
-    for first in range(0, units, 512):
-        here = slice(first, min(first + 512, units))
+    for first in range(0, units, units):
+        here = slice(first, first + units)
         sums = []
         for n, weight in enumerate((w_gate, w_up)):
             total = None if before is None else before[n][here, :]
@@ -440,9 +440,8 @@
         outs[2][...] = square
 
 
-def down_kernel(hidden, far, near, *refs):
-    far_out, near_out = refs[-2:]
-    for weight, out in ((far, far_out), (near, near_out)):
+def down_kernel(count, hidden, *refs):
+    for weight, out in zip(refs[:count], refs[-count:]):
         out[...] = jnp.dot(hidden[...], weight[...], preferred_element_type=F32).astype(out.dtype)
 
 
@@ -510,12 +509,12 @@
     near = stacked(near, keys)
     far = swap(near, "req", 1)
 
-    step_pages = 16
+    step_pages = 64
     total_rows = rows * req_devices
     anywhere = pl.BlockSpec(memory_space=pl.ANY)
     sent = jax.ShapeDtypeStruct((rows + reqs, HEAD_DIM), BF16)
     copied = jax.ShapeDtypeStruct((hidden_width, columns), BF16)
-    steps, early, w_up = range(req_devices), 3 * req_devices // 8, w_up.T
+    steps, early, w_up = range(req_devices), req_devices // 4, w_up.T
     attended = pl.pallas_call(
         functools.partial(attend_kernel, req_devices, heads, kv_local, reqs, step_pages),
         out_shape=[sent] * req_devices
@@ -582,7 +581,7 @@
     later = [(0, t) for t in steps[early:]] + [(1, t) for t in steps]
     blocks = staged_blocks(place, columns, [summed[0]], [w_up, w_down], later, "stage_up_down")
     w_up, w_down = [*first_up, *blocks[: -len(steps)]], blocks[-len(steps) :]
-    terms = [summed[0]] + [swap(summed[a], "head", a) for a in range(1, head_devices)]
+    terms = [summed[0]] + [swap(summed[a], "head", a) for a in range(head_devices - 1, 0, -1)]
     state = pl.pallas_call(
         state_kernel,
         out_shape=jax.ShapeDtypeStruct((block, columns), BF16),
@@ -616,10 +615,10 @@
     for c in range(chips):
         last = c == chips - 1
         if squares and last:
-            near[c] = [stacked(across, square[2])]
+            near[c] = [stacked(across, square[1])]
         far = early_far.get(c, []) + [swap(x, "req", 1) for x in near[c][len(early_far.get(c, [])) :]]
         count = len(far)
-        ready = [x for n in sorted(early_far) if n for x in early_far[n]] if c == 0 else []
+        ready = early_far.get(2, []) if c == 1 else []
         sums = pl.pallas_call(
             functools.partial(hidden_kernel, count, len(ready), c, last, columns * req_devices),
             out_shape=[jax.ShapeDtypeStruct((all_rows, hidden_width), BF16)]
@@ -633,7 +632,7 @@
             out_specs=[vmem] if last else [vmem] * 3,
             scratch_shapes=[pltpu.VMEM((2, all_rows, columns), BF16)],
             input_output_aliases={} if c == 0 or last else {2 * count + 6 + n: n for n in range(2)},
-            compiler_params=params(5),
+            compiler_params=params(8),
             cost_estimate=pl.CostEstimate(
                 flops=8 * all_rows * columns * hidden_width, bytes_accessed=0, transcendentals=0
             ),
@@ -654,20 +653,20 @@
     hidden, = sums
 
 
-    def down(c, *after):
-        far_part, near_part = pl.pallas_call(
-            down_kernel,
-            out_shape=[
-                jax.ShapeDtypeStruct((all_rows, columns), BF16),
-                jax.ShapeDtypeStruct((all_rows, columns), F32),
-            ],
-            in_specs=[vmem] * 3 + [anywhere] * len(after),
-            out_specs=[vmem] * 2,
+    def down(wanted, *after):
+        weights = [w_down[2 * c + 1] for c in wanted] + [w_down[2 * c] for c in wanted]
+        parts = pl.pallas_call(
+            functools.partial(down_kernel, len(weights)),
+            out_shape=[jax.ShapeDtypeStruct((all_rows, columns), BF16) for _ in wanted]
+            + [jax.ShapeDtypeStruct((all_rows, columns), F32) for _ in wanted],
+            in_specs=[vmem] * (1 + len(weights)) + [anywhere] * len(after),
+            out_specs=[vmem] * len(weights),
             compiler_params=params(5),
             cost_estimate=pl.CostEstimate(flops=1, bytes_accessed=1, transcendentals=0),
             name="down",
-        )(hidden, w_down[2 * c + 1], w_down[2 * c], *after)
-        return near_part, swap(far_part, "req", 1)
+        )(hidden, *weights, *after)
+        far_parts, near_parts = parts[: len(wanted)], parts[len(wanted) :]
+        return [(mine, swap(other, "req", 1)) for mine, other in zip(near_parts, far_parts)]
 
     def merge(c, layout, halves, passed=(), extra=()):
         layout = [[order.index(a) for a in blocks] for blocks in layout]
@@ -698,11 +697,9 @@
 
     totals = {}
     if squares:
-        corner = down(3)
-        halves_x = down(1)
+        (corner,), (halves_x,) = down([3]), down([1])
         by_x, by_y = merge(3, [[2, 0], [3, 1]], corner)
-        halves_y = down(2, by_x)
-        halves_own = down(0, by_x)
+        (halves_y,), (halves_own,) = down([2], by_x), down([0], by_x)
         by_x, by_y = swap(by_x, "req", 2), swap(by_y, "req", 4)
         layout = [[1, 0], [2, 3]]
         own = merge(0, layout, halves_own)
@@ -713,7 +710,7 @@
             totals.update(zip(blocks, total(blocks, parts)))
     else:
         layout = [list(range(1, head_devices)), [0]]
-        merged = [merge(c, layout, down(c)) for c in range(chips)]
+        merged = [merge(c, layout, down([c])[0]) for c in range(chips)]
         for n, blocks in enumerate(layout):
             parts = [merged[0][n]] + [swap(merged[c][n], "req", 2 * c) for c in range(1, chips)]
             totals.update(zip(blocks, total(blocks, parts)))

time: 147 us -> 143 us (0.973)
  Pallas kernels: 54.2 us -> 52.1 us
  waiting for transfers between devices: 47.5 us -> 45.7 us
    pallas_call x1, Pallas kernels: 11.9 us -> 9.58 us  [shards(): pl.pallas_call(functools.partial(attend_kernel, req_devices, heads, kv_lo...]
    ppermute x51, waiting for transfers between devices: 47.5 us -> 45.7 us  [swap(): return lax.ppermute(array, axis, [(i, i ^ bits) for i in range(size)])]
  transfers between devices with their start and end apart: 51 -> 51, of which waited for: 26 -> 27; matrix products, arithmetic and copies ran while one was open for 0% -> 1% of each run, Pallas kernels for 22% -> 23%
where the time goes in v5:
time: 143 us
  Pallas kernels  52.1 us (36%)
  waiting for transfers between devices  45.7 us (32%)
  starting transfers between devices  41.9 us (29%)
  local copies, waits for them, and re-layouts  1.64 us (1%)
    ppermute x51, waiting for transfers between devices, swap(): return lax.ppermute(array, axis, [(i, i ^ bits) for i in range(size)])  45.7 us
    ppermute x51, starting transfers between devices, swap(): return lax.ppermute(array, axis, [(i, i ^ bits) for i in range(size)])  41.9 us
    pallas_call x2, Pallas kernels, staged_blocks(): pl.pallas_call(functools.partial(split_kernel, len(arrays), wanted), out_...  15.5 us
    pallas_call x4, Pallas kernels, shards(): pl.pallas_call(functools.partial(hidden_kernel, count, len(ready), c, las...  11.8 us
    pallas_call x1, Pallas kernels, shards(): pl.pallas_call(functools.partial(attend_kernel, req_devices, heads, kv_lo...  9.58 us
    pallas_call x4, Pallas kernels, down(): pl.pallas_call(functools.partial(down_kernel, len(weights)), out_shape=[j...  5 us
    pallas_call x1, Pallas kernels, staged(): pl.pallas_call(functools.partial(stage_kernel, len(arrays), pieces), out_...  4.69 us
  transfers between devices with their start and end apart: 51, of which 27 were waited for; matrix products, arithmetic and copies ran while one was open for 1% of the time, Pallas kernels for 23%

profile of v5, /device:TPU:0, one launch (start us, length us, event | category | flops | bytes accessed | tf_op | source)
XLA Modules:
  0.0 142.6 jit_solution(15202971221309240225)
XLA Ops:
  2.4 2.9 %collective-permute-start = (bf16[544,128]{1,0:T(8,128)(2,1)S(1)}, bf16[544,128]{1,0:T(8,128)(2,1)S(1)}, u32[]{:S(2)}, u32[]{:S(2)}) collective-permute-start(bf16[544,128]{1,0:T(8,128)(2,1)S(1)} %pack.1.refs_1_.refs_0_.queries), channel_id=1, source_target_pairs={{0,8},{4,12},{8,0},{12,4},{16,24},{20,28},{24,16},{28,20},{1,9},{5... | collective-permute-start | bytes 417800 | tf_op jit(solution)/shard_map/ppermute | solution.py:21
  7.6 4.7 %stage_keys.1.refs_4_.keys = bf16[192,128,256]{2,1,0:T(8,128)(2,1)S(1)} custom-call(bf16[192,128,256]{2,1,0:T(8,128)(2,1)} %refs_0_.2, bf16[544,128]{1,0:T(8,128)(2,1)S(1)} %pack.1.refs_1_.refs_0_.queries, f32[8,1024]{1,0:T(8,128)S(1)} %gain.1.refs_2_.refs_4_), custom_call_target="tpu_custom_call" | custom-call | bytes 12582912 | tf_op jit(solution)/shard_map/stage_keys/pallas_call | solution.py:62
  13.6 1.9 %collective-permute-done.3.far = bf16[2176,128]{1,0:T(8,128)(2,1)S(1)} collective-permute-done((bf16[2176,128]{1,0:T(8,128)(2,1)S(1)}, bf16[2176,128]{1,0:T(8,128)(2,1)S(1)}, u32[]{:S(2)}, u32[]{:S(2)}) %collective-permute-start.3) | collective-permute-done | bytes 557088 | tf_op jit(solution)/shard_map/ppermute | solution.py:21
  15.5 9.6 %attend.1 = (bf16[544,128]{1,0:T(8,128)(2,1)S(1)}, bf16[544,128]{1,0:T(8,128)(2,1)S(1)}, bf16[544,128]{1,0:T(8,128)(2,1)S(1)}, bf16[544,128]{1,0:T(8,128)(2,1)S(...) custom-call(s32[2]{0:T(128)S(1)} %pad_add_fusion.place, ...), custom_call_target="tpu_custom_call" | custom-call | tf_op jit(solution)/shard_map/attend/pallas_call | solution.py:518
  28.1 1.9 %collective-permute-start.10 = (bf16[544,128]{1,0:T(8,128)(2,1)S(1)}, bf16[544,128]{1,0:T(8,128)(2,1)S(1)}, u32[]{:S(2)}, u32[]{:S(2)}) collective-permute-start(bf16[544,128]{1,0:T(8,128)(2,1)S(1)} %get-tuple-element.87), channel_id=1, source_target_pairs={{0,24},{4,28},{8,16},{12,20},{16,8},{20,12},{24,0},{28,4},{1,25},{... | collective-permute-start | bytes 417800 | tf_op jit(solution)/shard_map/ppermute | solution.py:21
  31.7 6.1 %stage_gate.1 = (bf16[924,1024]{1,0:T(8,128)(2,1)S(1)}, bf16[924,1024]{1,0:T(8,128)(2,1)S(1)}, bf16[924,1024]{1,0:T(8,128)(2,1)S(1)}, bf16[924,1024]{1,0:T(8,128...) custom-call(s32[2]{0:T(128)S(1)} %pad_add_fusion.place, ...), custom_call_target="tpu_custom_call" | custom-call | bytes 15138816 | tf_op jit(solution)/shard_map/stage_gate/pallas_call | solution.py:90
  42.2 2.3 %collective-permute-done.11.refs_1_ = bf16[32,2048]{1,0:T(8,128)(2,1)S(1)} collective-permute-done((bf16[32,2048]{1,0:T(8,128)(2,1)S(1)}, bf16[32,2048]{1,0:T(8,128)(2,1)S(1)}, u32[]{:S(2)}, u32[]{:S(2)}) %collective-permute-start.11) | collective-permute-done | bytes 131104 | tf_op jit(solution)/shard_map/ppermute | solution.py:21
  44.5 2.0 %collective-permute-done.12.refs_2_ = bf16[32,2048]{1,0:T(8,128)(2,1)S(1)} collective-permute-done((bf16[32,2048]{1,0:T(8,128)(2,1)S(1)}, bf16[32,2048]{1,0:T(8,128)(2,1)S(1)}, u32[]{:S(2)}, u32[]{:S(2)}) %collective-permute-start.12) | collective-permute-done | bytes 131104 | tf_op jit(solution)/shard_map/ppermute | solution.py:21
  49.1 1.9 %project.1 = (f32[64,1024]{1,0:T(8,128)S(1)}, bf16[64,1024]{1,0:T(8,128)(2,1)S(1)}, bf16[64,1024]{1,0:T(8,128)(2,1)S(1)}, bf16[64,1024]{1,0:T(8,128)(2,1)S(1)}) custom-call(s32[2]{0:T(128)S(1)} %pad_add_fusion.place, bf16[32,2048]{1,0:T(8,128)(2,1)S(1)} %combine.1.refs_0_, bf16[32,2048]{1,0:T(8,128)(2,1)S(1)} %collective-permute-done.11.refs_1_, ...), custom_call_target="tpu_custom_call" | custom-call | tf_op jit(solution)/shard_map/project/pallas_call | solution.py:569
  51.0 3.7 %collective-permute-start.18 = (bf16[64,1024]{1,0:T(8,128)(2,1)S(1)}, bf16[64,1024]{1,0:T(8,128)(2,1)S(1)}, u32[]{:S(2)}, u32[]{:S(2)}) collective-permute-start(bf16[64,1024]{1,0:T(8,128)(2,1)S(1)} %get-tuple-element.91), channel_id=1, source_target_pairs={{0,3},{1,2},{2,1},{3,0},{4,7},{5,6},{6,5},{7,4},{8,11},{9,10},{10,... | collective-permute-start | bytes 393224 | tf_op jit(solution)/shard_map/ppermute | solution.py:21
  55.5 9.4 %stage_up_down.1 = (bf16[924,1024]{1,0:T(8,128)(2,1)S(1)}, bf16[924,1024]{1,0:T(8,128)(2,1)S(1)}, bf16[924,1024]{1,0:T(8,128)(2,1)S(1)}, bf16[924,1024]{1,0:T(8,...) custom-call(s32[2]{0:T(128)S(1)} %pad_add_fusion.place, ...), custom_call_target="tpu_custom_call" | custom-call | bytes 26492928 | tf_op jit(solution)/shard_map/stage_up_down/pallas_call | solution.py:90
  67.1 2.5 %collective-permute-start.23 = (bf16[64,1024]{1,0:T(8,128)(2,1)S(1)}, bf16[64,1024]{1,0:T(8,128)(2,1)S(1)}, u32[]{:S(2)}, u32[]{:S(2)}) collective-permute-start(bf16[64,1024]{1,0:T(8,128)(2,1)S(1)} %state.1.refs_0_), channel_id=1, source_target_pairs={{0,3},{1,2},{2,1},{3,0},{4,7},{5,6},{6,5},{7,4},{8,11},{9,10},{10,... | collective-permute-start | bytes 393224 | tf_op jit(solution)/shard_map/ppermute | solution.py:21
  69.6 1.9 %collective-permute-start.25 = (bf16[64,1024]{1,0:T(8,128)(2,1)S(1)}, bf16[64,1024]{1,0:T(8,128)(2,1)S(1)}, u32[]{:S(2)}, u32[]{:S(2)}) collective-permute-start(bf16[64,1024]{1,0:T(8,128)(2,1)S(1)} %state.1.refs_0_), channel_id=1, source_target_pairs={{0,1},{1,0},{2,3},{3,2},{4,5},{5,4},{6,7},{7,6},{8,9},{9,8},{10,11... | collective-permute-start | bytes 393224 | tf_op jit(solution)/shard_map/ppermute | solution.py:21
  75.3 4.7 %collective-permute-done.24.refs_1_ = bf16[64,1024]{1,0:T(8,128)(2,1)S(1)} collective-permute-done((bf16[64,1024]{1,0:T(8,128)(2,1)S(1)}, bf16[64,1024]{1,0:T(8,128)(2,1)S(1)}, u32[]{:S(2)}, u32[]{:S(2)}) %collective-permute-start.24) | collective-permute-done | bytes 131104 | tf_op jit(solution)/shard_map/ppermute | solution.py:21
  82.9 2.8 %hidden.4 = (f32[924,256]{1,0:T(8,128)S(1)}, f32[924,256]{1,0:T(8,128)S(1)}, f32[256,128]{1,0:T(8,128)S(1)}) custom-call(s32[2]{0:T(128)S(1)} %pad_add_fusion.place, bf16[64,1024]{1,0:T(8,128)(2,1)S(1)} %state.1.refs_0_, bf16[192,1024]{1,0:T(8,128)(2,1)S(1)} %stack.18.refs_1_, bf16[64,1024]{1,0:T(8,128)(2,1)S(1)} %collective-permute-done.28.refs_2_, ...), custom_call_target="tpu_custom_call" | custom-call | flops 1937768448 | tf_op jit(solution)/shard_map/hidden/pallas_call | solution.py:622
  85.7 6.0 %collective-permute-done.27.refs_0_ = bf16[192,1024]{1,0:T(8,128)(2,1)S(1)} collective-permute-done((bf16[192,1024]{1,0:T(8,128)(2,1)S(1)}, bf16[192,1024]{1,0:T(8,128)(2,1)S(1)}, u32[]{:S(2)}, u32[]{:S(2)}) %collective-permute-start.27) | collective-permute-done | bytes 393248 | tf_op jit(solution)/shard_map/ppermute | solution.py:21
  95.5 2.9 %hidden.5 = (f32[924,256]{1,0:T(8,128)S(1)}, f32[924,256]{1,0:T(8,128)S(1)}, f32[256,128]{1,0:T(8,128)S(1)}) custom-call(s32[2]{0:T(128)S(1)} %pad_add_fusion.place, bf16[64,1024]{1,0:T(8,128)(2,1)S(1)} %collective-permute-done.21.refs_3_.refs_0_, bf16[192,1024]{1,0:T(8,128)(2,1)S(1)} %stack.19.source.refs_1_, ...), custom_call_target="tpu_custom_call", output_to_operand_aliasing={{0}: (10, {}), {1}: (11, {})} | custom-call | flops 1937768448 | tf_op jit(solution)/shard_map/hidden/pallas_call | solution.py:622
  100.8 2.9 %hidden.6 = (f32[924,256]{1,0:T(8,128)S(1)}, f32[924,256]{1,0:T(8,128)S(1)}, f32[256,128]{1,0:T(8,128)S(1)}) custom-call(s32[2]{0:T(128)S(1)} %pad_add_fusion.place, bf16[64,1024]{1,0:T(8,128)(2,1)S(1)} %collective-permute-done.26.refs_4_.refs_0_, bf16[192,1024]{1,0:T(8,128)(2,1)S(1)} %stack.20.source.refs_1_, ...), custom_call_target="tpu_custom_call", output_to_operand_aliasing={{0}: (10, {}), {1}: (11, {})} | custom-call | flops 1937768448 | tf_op jit(solution)/shard_map/hidden/pallas_call | solution.py:622
  103.7 3.3 %hidden.7 = bf16[256,924]{1,0:T(8,128)(2,1)S(1)} custom-call(s32[2]{0:T(128)S(1)} %pad_add_fusion.place, bf16[256,1024]{1,0:T(8,128)(2,1)S(1)} %stack.21.refs_0_, bf16[256,1024]{1,0:T(8,128)(2,1)S(1)} %collective-permute-done.36.refs_1_, f32[8,1024]{1,0:T(8,128)S(1)} %gain.1.refs_2_.refs_4_, bf16[924,1024]{1,0:T(8,128)(2,1)S(1)} %get-tuple-element.105.refs_3_, ...), custom_call_target="tpu_custom_call" | custom-call | flops 1937768448 | tf_op jit(solution)/shard_map/hidden/pallas_call | solution.py:622
  116.0 4.5 %collective-permute-done.41.refs_0_ = bf16[128,1024]{1,0:T(8,128)(2,1)S(1)} collective-permute-done((bf16[128,1024]{1,0:T(8,128)(2,1)S(1)}, bf16[128,1024]{1,0:T(8,128)(2,1)S(1)}, u32[]{:S(2)}, u32[]{:S(2)}) %collective-permute-start.41) | collective-permute-done | bytes 262176 | tf_op jit(solution)/shard_map/ppermute | solution.py:21
  125.0 4.9 %collective-permute-done.46.refs_1_ = bf16[128,1024]{1,0:T(8,128)(2,1)S(1)} collective-permute-done((bf16[128,1024]{1,0:T(8,128)(2,1)S(1)}, bf16[128,1024]{1,0:T(8,128)(2,1)S(1)}, u32[]{:S(2)}, u32[]{:S(2)}) %collective-permute-start.46) | collective-permute-done | bytes 262176 | tf_op jit(solution)/shard_map/ppermute | solution.py:21
  131.0 2.4 %collective-permute-start.48 = (bf16[64,1024]{1,0:T(8,128)(2,1)S(1)}, bf16[64,1024]{1,0:T(8,128)(2,1)S(1)}, u32[]{:S(2)}, u32[]{:S(2)}) collective-permute-start(bf16[64,1024]{1,0:T(8,128)(2,1)S(1)} %get-tuple-element.142), channel_id=1, source_target_pairs={{0,3},{1,2},{2,1},{3,0},{4,7},{5,6},{6,5},{7,4},{8,11},{9,10},{10,... | collective-permute-start | bytes 393224 | tf_op jit(solution)/shard_map/ppermute | solution.py:21
  135.6 3.2 %collective-permute-done.48 = bf16[64,1024]{1,0:T(8,128)(2,1)S(1)} collective-permute-done((bf16[64,1024]{1,0:T(8,128)(2,1)S(1)}, bf16[64,1024]{1,0:T(8,128)(2,1)S(1)}, u32[]{:S(2)}, u32[]{:S(2)}) %collective-permute-start.48) | collective-permute-done | bytes 131104 | tf_op jit(solution)/shard_map/ppermute | solution.py:21
  138.9 2.6 %collective-permute-done.49 = bf16[64,1024]{1,0:T(8,128)(2,1)S(1)} collective-permute-done((bf16[64,1024]{1,0:T(8,128)(2,1)S(1)}, bf16[64,1024]{1,0:T(8,128)(2,1)S(1)}, u32[]{:S(2)}, u32[]{:S(2)}) %collective-permute-start.49) | collective-permute-done | bytes 131104 | tf_op jit(solution)/shard_map/ppermute | solution.py:21
  (120 shorter events, 51.4 us)
Async XLA Ops:
  2.4 9.9 %collective-permute-start = (bf16[544,128]{1,0:T(8,128)(2,1)S(1)}, bf16[544,128]{1,0:T(8,128)(2,1)S(1)}, u32[]{:S(2)}, u32[]{:S(2)}) collective-permute-start(bf16[544,128]{1,0:T(8,128)(2,1)S(1)} %pack.1.refs_1_.refs_0_.queries), channel_id=1, source_target_pairs={{0,8},{4,12},{8,0},{12,4},{16,24},{20,28},{24,16},{28,20},{1,9},{5... | collective-permute-start | bytes 417800 | tf_op jit(solution)/shard_map/ppermute | solution.py:21
  5.3 8.1 %collective-permute-start.1 = (bf16[544,128]{1,0:T(8,128)(2,1)S(1)}, bf16[544,128]{1,0:T(8,128)(2,1)S(1)}, u32[]{:S(2)}, u32[]{:S(2)}) collective-permute-start(bf16[544,128]{1,0:T(8,128)(2,1)S(1)} %pack.1.refs_1_.refs_0_.queries), channel_id=1, source_target_pairs={{0,16},{4,20},{8,24},{12,28},{16,0},{20,4},{24,8},{28,12},{1,17},{... | collective-permute-start | bytes 417800 | tf_op jit(solution)/shard_map/ppermute | solution.py:21
  28.1 9.6 %collective-permute-start.10 = (bf16[544,128]{1,0:T(8,128)(2,1)S(1)}, bf16[544,128]{1,0:T(8,128)(2,1)S(1)}, u32[]{:S(2)}, u32[]{:S(2)}) collective-permute-start(bf16[544,128]{1,0:T(8,128)(2,1)S(1)} %get-tuple-element.87), channel_id=1, source_target_pairs={{0,24},{4,28},{8,16},{12,20},{16,8},{20,12},{24,0},{28,4},{1,25},{... | collective-permute-start | bytes 417800 | tf_op jit(solution)/shard_map/ppermute | solution.py:21
  30.0 8.1 %collective-permute-start.8 = (bf16[544,128]{1,0:T(8,128)(2,1)S(1)}, bf16[544,128]{1,0:T(8,128)(2,1)S(1)}, u32[]{:S(2)}, u32[]{:S(2)}) collective-permute-start(bf16[544,128]{1,0:T(8,128)(2,1)S(1)} %get-tuple-element.85), channel_id=1, source_target_pairs={{0,8},{4,12},{8,0},{12,4},{16,24},{20,28},{24,16},{28,20},{1,9},{5... | collective-permute-start | bytes 417800 | tf_op jit(solution)/shard_map/ppermute | solution.py:21
  51.0 13.9 %collective-permute-start.18 = (bf16[64,1024]{1,0:T(8,128)(2,1)S(1)}, bf16[64,1024]{1,0:T(8,128)(2,1)S(1)}, u32[]{:S(2)}, u32[]{:S(2)}) collective-permute-start(bf16[64,1024]{1,0:T(8,128)(2,1)S(1)} %get-tuple-element.91), channel_id=1, source_target_pairs={{0,3},{1,2},{2,1},{3,0},{4,7},{5,6},{6,5},{7,4},{8,11},{9,10},{10,... | collective-permute-start | bytes 393224 | tf_op jit(solution)/shard_map/ppermute | solution.py:21
  54.7 11.4 %collective-permute-start.19 = (bf16[64,1024]{1,0:T(8,128)(2,1)S(1)}, bf16[64,1024]{1,0:T(8,128)(2,1)S(1)}, u32[]{:S(2)}, u32[]{:S(2)}) collective-permute-start(bf16[64,1024]{1,0:T(8,128)(2,1)S(1)} %get-tuple-element.92), channel_id=1, source_target_pairs={{0,2},{1,3},{2,0},{3,1},{4,6},{5,7},{6,4},{7,5},{8,10},{9,11},{10,... | collective-permute-start | bytes 393224 | tf_op jit(solution)/shard_map/ppermute | solution.py:21
  54.7 11.4 %collective-permute-start.20 = (bf16[64,1024]{1,0:T(8,128)(2,1)S(1)}, bf16[64,1024]{1,0:T(8,128)(2,1)S(1)}, u32[]{:S(2)}, u32[]{:S(2)}) collective-permute-start(bf16[64,1024]{1,0:T(8,128)(2,1)S(1)} %get-tuple-element.93), channel_id=1, source_target_pairs={{0,1},{1,0},{2,3},{3,2},{4,5},{5,4},{6,7},{7,6},{8,9},{9,8},{10,11... | collective-permute-start | bytes 393224 | tf_op jit(solution)/shard_map/ppermute | solution.py:21
  67.1 8.2 %collective-permute-start.23 = (bf16[64,1024]{1,0:T(8,128)(2,1)S(1)}, bf16[64,1024]{1,0:T(8,128)(2,1)S(1)}, u32[]{:S(2)}, u32[]{:S(2)}) collective-permute-start(bf16[64,1024]{1,0:T(8,128)(2,1)S(1)} %state.1.refs_0_), channel_id=1, source_target_pairs={{0,3},{1,2},{2,1},{3,0},{4,7},{5,6},{6,5},{7,4},{8,11},{9,10},{10,... | collective-permute-start | bytes 393224 | tf_op jit(solution)/shard_map/ppermute | solution.py:21
  69.6 10.4 %collective-permute-start.24 = (bf16[64,1024]{1,0:T(8,128)(2,1)S(1)}, bf16[64,1024]{1,0:T(8,128)(2,1)S(1)}, u32[]{:S(2)}, u32[]{:S(2)}) collective-permute-start(bf16[64,1024]{1,0:T(8,128)(2,1)S(1)} %state.1.refs_0_), channel_id=1, source_target_pairs={{0,2},{1,3},{2,0},{3,1},{4,6},{5,7},{6,4},{7,5},{8,10},{9,11},{10,... | collective-permute-start | bytes 393224 | tf_op jit(solution)/shard_map/ppermute | solution.py:21
  69.6 10.4 %collective-permute-start.25 = (bf16[64,1024]{1,0:T(8,128)(2,1)S(1)}, bf16[64,1024]{1,0:T(8,128)(2,1)S(1)}, u32[]{:S(2)}, u32[]{:S(2)}) collective-permute-start(bf16[64,1024]{1,0:T(8,128)(2,1)S(1)} %state.1.refs_0_), channel_id=1, source_target_pairs={{0,1},{1,0},{2,3},{3,2},{4,5},{5,4},{6,7},{7,6},{8,9},{9,8},{10,11... | collective-permute-start | bytes 393224 | tf_op jit(solution)/shard_map/ppermute | solution.py:21
  71.5 8.6 %collective-permute-start.26 = (bf16[64,1024]{1,0:T(8,128)(2,1)S(1)}, bf16[64,1024]{1,0:T(8,128)(2,1)S(1)}, u32[]{:S(2)}, u32[]{:S(2)}) collective-permute-start(bf16[64,1024]{1,0:T(8,128)(2,1)S(1)} %state.1.refs_0_), channel_id=1, source_target_pairs={{0,16},{4,20},{8,24},{12,28},{16,0},{20,4},{24,8},{28,12},{1,17},{... | collective-permute-start | bytes 393224 | tf_op jit(solution)/shard_map/ppermute | solution.py:21
  80.1 11.5 %collective-permute-start.27 = (bf16[192,1024]{1,0:T(8,128)(2,1)S(1)}, bf16[192,1024]{1,0:T(8,128)(2,1)S(1)}, u32[]{:S(2)}, u32[]{:S(2)}) collective-permute-start(bf16[192,1024]{1,0:T(8,128)(2,1)S(1)} %stack.18.refs_1_), channel_id=1, source_target_pairs={{0,8},{4,12},{8,0},{12,4},{16,24},{20,28},{24,16},{28,20},{1,9},{5... | collective-permute-start | bytes 1179656 | tf_op jit(solution)/shard_map/ppermute | solution.py:21
  81.5 11.4 %collective-permute-start.31 = (bf16[192,1024]{1,0:T(8,128)(2,1)S(1)}, bf16[192,1024]{1,0:T(8,128)(2,1)S(1)}, u32[]{:S(2)}, u32[]{:S(2)}) collective-permute-start(bf16[192,1024]{1,0:T(8,128)(2,1)S(1)} %stack.18.refs_1_), channel_id=1, source_target_pairs={{0,16},{4,20},{8,24},{12,28},{16,0},{20,4},{24,8},{28,12},{1,17},{... | collective-permute-start | bytes 1179656 | tf_op jit(solution)/shard_map/ppermute | solution.py:21
  111.6 9.9 %collective-permute-start.43 = (bf16[256,1024]{1,0:T(8,128)(2,1)S(1)}, bf16[256,1024]{1,0:T(8,128)(2,1)S(1)}, u32[]{:S(2)}, u32[]{:S(2)}) collective-permute-start(bf16[256,1024]{1,0:T(8,128)(2,1)S(1)} %get-tuple-element.136), channel_id=1, source_target_pairs={{0,4},{4,0},{8,12},{12,8},{16,20},{20,16},{24,28},{28,24},{1,5},{5... | collective-permute-start | bytes 1572872 | tf_op jit(solution)/shard_map/ppermute | solution.py:21
  112.1 8.3 %collective-permute-start.41 = (bf16[128,1024]{1,0:T(8,128)(2,1)S(1)}, bf16[128,1024]{1,0:T(8,128)(2,1)S(1)}, u32[]{:S(2)}, u32[]{:S(2)}) collective-permute-start(bf16[128,1024]{1,0:T(8,128)(2,1)S(1)} %get-tuple-element.131), channel_id=1, source_target_pairs={{0,16},{4,20},{8,24},{12,28},{16,0},{20,4},{24,8},{28,12},{1,17},{... | collective-permute-start | bytes 786440 | tf_op jit(solution)/shard_map/ppermute | solution.py:21
  113.4 8.1 %collective-permute-start.44 = (bf16[128,1024]{1,0:T(8,128)(2,1)S(1)}, bf16[128,1024]{1,0:T(8,128)(2,1)S(1)}, u32[]{:S(2)}, u32[]{:S(2)}) collective-permute-start(bf16[128,1024]{1,0:T(8,128)(2,1)S(1)} %get-tuple-element.123.refs_2_), channel_id=1, source_target_pairs={{0,8},{4,12},{8,0},{12,4},{16,24},{20,28},{24,16},{28,20},{1,9},{5... | collective-permute-start | bytes 786440 | tf_op jit(solution)/shard_map/ppermute | solution.py:21
  115.9 9.0 %collective-permute-start.39 = (bf16[256,1024]{1,0:T(8,128)(2,1)S(1)}, bf16[256,1024]{1,0:T(8,128)(2,1)S(1)}, u32[]{:S(2)}, u32[]{:S(2)}) collective-permute-start(bf16[256,1024]{1,0:T(8,128)(2,1)S(1)} %get-tuple-element.125), channel_id=1, source_target_pairs={{0,4},{4,0},{8,12},{12,8},{16,20},{20,16},{24,28},{28,24},{1,5},{5... | collective-permute-start | bytes 1572872 | tf_op jit(solution)/shard_map/ppermute | solution.py:21
  120.6 9.3 %collective-permute-start.46 = (bf16[128,1024]{1,0:T(8,128)(2,1)S(1)}, bf16[128,1024]{1,0:T(8,128)(2,1)S(1)}, u32[]{:S(2)}, u32[]{:S(2)}) collective-permute-start(bf16[128,1024]{1,0:T(8,128)(2,1)S(1)} %get-tuple-element.140), channel_id=1, source_target_pairs={{0,8},{4,12},{8,0},{12,4},{16,24},{20,28},{24,16},{28,20},{1,9},{5... | collective-permute-start | bytes 786440 | tf_op jit(solution)/shard_map/ppermute | solution.py:21
  121.6 9.3 %collective-permute-start.47 = (bf16[128,1024]{1,0:T(8,128)(2,1)S(1)}, bf16[128,1024]{1,0:T(8,128)(2,1)S(1)}, u32[]{:S(2)}, u32[]{:S(2)}) collective-permute-start(bf16[128,1024]{1,0:T(8,128)(2,1)S(1)} %get-tuple-element.141), channel_id=1, source_target_pairs={{0,16},{4,20},{8,24},{12,28},{16,0},{20,4},{24,8},{28,12},{1,17},{... | collective-permute-start | bytes 786440 | tf_op jit(solution)/shard_map/ppermute | solution.py:21
  123.3 10.4 %collective-permute-start.42 = (bf16[128,1024]{1,0:T(8,128)(2,1)S(1)}, bf16[128,1024]{1,0:T(8,128)(2,1)S(1)}, u32[]{:S(2)}, u32[]{:S(2)}) collective-permute-start(bf16[128,1024]{1,0:T(8,128)(2,1)S(1)} %get-tuple-element.132), channel_id=1, source_target_pairs={{0,8},{4,12},{8,0},{12,4},{16,24},{20,28},{24,16},{28,20},{1,9},{5... | collective-permute-start | bytes 786440 | tf_op jit(solution)/shard_map/ppermute | solution.py:21
  124.2 10.3 %collective-permute-start.45 = (bf16[128,1024]{1,0:T(8,128)(2,1)S(1)}, bf16[128,1024]{1,0:T(8,128)(2,1)S(1)}, u32[]{:S(2)}, u32[]{:S(2)}) collective-permute-start(bf16[128,1024]{1,0:T(8,128)(2,1)S(1)} %get-tuple-element.137), channel_id=1, source_target_pairs={{0,16},{4,20},{8,24},{12,28},{16,0},{20,4},{24,8},{28,12},{1,17},{... | collective-permute-start | bytes 786440 | tf_op jit(solution)/shard_map/ppermute | solution.py:21
  131.0 7.9 %collective-permute-start.48 = (bf16[64,1024]{1,0:T(8,128)(2,1)S(1)}, bf16[64,1024]{1,0:T(8,128)(2,1)S(1)}, u32[]{:S(2)}, u32[]{:S(2)}) collective-permute-start(bf16[64,1024]{1,0:T(8,128)(2,1)S(1)} %get-tuple-element.142), channel_id=1, source_target_pairs={{0,3},{1,2},{2,1},{3,0},{4,7},{5,6},{6,5},{7,4},{8,11},{9,10},{10,... | collective-permute-start | bytes 393224 | tf_op jit(solution)/shard_map/ppermute | solution.py:21
  133.5 8.0 %collective-permute-start.49 = (bf16[64,1024]{1,0:T(8,128)(2,1)S(1)}, bf16[64,1024]{1,0:T(8,128)(2,1)S(1)}, u32[]{:S(2)}, u32[]{:S(2)}) collective-permute-start(bf16[64,1024]{1,0:T(8,128)(2,1)S(1)} %get-tuple-element.143), channel_id=1, source_target_pairs={{0,2},{1,3},{2,0},{3,1},{4,6},{5,7},{6,4},{7,5},{8,10},{9,11},{10,... | collective-permute-start | bytes 393224 | tf_op jit(solution)/shard_map/ppermute | solution.py:21
  134.6 7.2 %collective-permute-start.50 = (bf16[64,1024]{1,0:T(8,128)(2,1)S(1)}, bf16[64,1024]{1,0:T(8,128)(2,1)S(1)}, u32[]{:S(2)}, u32[]{:S(2)}) collective-permute-start(bf16[64,1024]{1,0:T(8,128)(2,1)S(1)} %get-tuple-element.144), channel_id=1, source_target_pairs={{0,1},{1,0},{2,3},{3,2},{4,5},{5,4},{6,7},{7,6},{8,9},{9,8},{10,11... | collective-permute-start | bytes 393224 | tf_op jit(solution)/shard_map/ppermute | solution.py:21
  (31 other events, 135.1 us)

commit v6 on v5

--- a/solution.py
+++ b/solution.py
@@ -19,10 +19,6 @@
 def swap(array, axis, bits):
     size = lax.axis_size(axis)
     return lax.ppermute(array, axis, [(i, i ^ bits) for i in range(size)])
-
-
-def whole(shape):
-    return pl.BlockSpec(shape, lambda *_: (0,) * len(shape))
 
 
 def in_vmem(array):
@@ -84,6 +80,24 @@
         copy.wait()
 
 
+def keys_kernel(pieces, keys, *refs):
+    keys_copy, top, weight, acc, sems = refs[-5:]
+    cut = keys.shape[0] // pieces
+    copies = [
+        pltpu.make_async_copy(
+            keys.at[pl.ds(n * cut, cut)], keys_copy.at[pl.ds(n * cut, cut)], sems.at[n]
+        )
+        for n in range(pieces)
+    ]
+    for copy in copies:
+        copy.start()
+    top[...] = jnp.full(top.shape, NEGATIVE_FILL, F32)
+    weight[...] = jnp.zeros(weight.shape, F32)
+    acc[...] = jnp.zeros(acc.shape, F32)
+    for copy in copies:
+        copy.wait()
+
+
 def staged_blocks(place, width, after, arrays, wanted, name):
     anywhere = pl.BlockSpec(memory_space=pl.ANY)
     shapes = [jax.ShapeDtypeStruct((arrays[n].shape[0], width), arrays[n].dtype) for n, _ in wanted]
@@ -103,8 +117,10 @@
     )(place, *[in_hbm(array) for array in arrays], *after)
 
 
-def pack_kernel(page_len, place, lengths, table, queries, out):
+def pack_kernel(page_len, place, lengths, table, queries, out, held_queries, sem):
     del place
+    copy = pltpu.make_async_copy(queries, held_queries, sem)
+    copy.start()
     reqs, slots = table.shape
     query_rows = queries.shape[0] * queries.shape[1] // HEAD_DIM
     inverse_rows = out.shape[0] - query_rows
@@ -121,7 +137,8 @@
         total += lax.dot_general(
             row_hit, lane_hit, (((1,), (1,)), ((), ())), preferred_element_type=F32
         )
-    own = queries[...].astype(F32).reshape(query_rows, HEAD_DIM)
+    copy.wait()
+    own = held_queries[...].astype(F32).reshape(query_rows, HEAD_DIM)
     out[pl.ds(0, query_rows), :] = own.astype(BF16)
     out[pl.ds(query_rows, inverse_rows), :] = total.astype(BF16)
 
@@ -164,18 +181,18 @@
 
 
 def attend_kernel(
-    devices, heads, kv_local, reqs, step_pages, place, near, far, keys, value_pool, *refs
+    devices, heads, kv_local, reqs, step_pages, place, *refs
 ):
-    w_out, w_up, refs = refs[0], refs[1], refs[2:]
-    outs, refs = refs[:-11], refs[-11:]
+    sources, refs = refs[:devices], refs[devices:]
+    (keys, value_pool, w_out, w_up), refs = refs[:4], refs[7:]
+    outs, (top, weight, acc), refs = refs[:-11], refs[-11:-8], refs[-8:]
     outs, w_out_copy, w_up_copies = outs[:devices], outs[devices], outs[devices + 1 :]
-    query, score, top, weight, acc, found, index, values, sem, value_sem, out_sem = refs
+    query, score, found, index, values, sem, value_sem, out_sem = refs
     chips = len(outs) // 2
     pages = keys.shape[0]
     steps = pages // step_pages
     rows = reqs * heads
-    stride = near.shape[0] // chips
-    inverse_rows = stride - rows
+    inverse_rows = sources[0].shape[0] - rows
     group = heads // kv_local
     scale = 1.0 / math.sqrt(HEAD_DIM)
     lane = lax.broadcasted_iota(jnp.int32, (heads, HEAD_DIM), 1)
@@ -195,23 +212,15 @@
     pick = jnp.where(lax.broadcasted_iota(jnp.int32, (8, inverse_rows), 1) == wanted, 1.0, 0.0)
     half = lax.broadcasted_iota(jnp.int32, (8, 2 * LO), 1)
     total = jnp.zeros((8, 2 * LO), F32)
-    for side, ref in enumerate((near, far)):
-        for chip in range(chips):
-            at = (side * chips + chip) * rows
-            query[pl.ds(at, rows), :] = ref[pl.ds(chip * stride, rows), :].astype(F32)
-            part = jnp.dot(
-                pick.astype(BF16),
-                ref[pl.ds(chip * stride + rows, inverse_rows), :],
-                preferred_element_type=F32,
-            )
-            base = (side * chips + chip) * reqs - 1
-            total += jnp.where((half < LO) & (part > 0.0), part + base, part)
+    for n, source in enumerate(sources):
+        query[pl.ds(n * rows, rows), :] = source[pl.ds(0, rows), :].astype(F32)
+        part = jnp.dot(
+            pick.astype(BF16), source[pl.ds(rows, inverse_rows), :], preferred_element_type=F32
+        )
+        total += jnp.where((half < LO) & (part > 0.0), part + (n * reqs - 1), part)
     found[...] = total.astype(jnp.int32)
     copy = pltpu.make_async_copy(found, index, sem)
     copy.start()
-    top[...] = jnp.full(top.shape, NEGATIVE_FILL, F32)
-    weight[...] = jnp.zeros(weight.shape, F32)
-    acc[...] = jnp.zeros(acc.shape, F32)
     copy.wait()
 
     def rows_of(page):
@@ -233,14 +242,13 @@
                 q, keys[first + p], (((1,), (1,)), ((), ())), preferred_element_type=F32
             ) * scale
             scores.append(jnp.where(lane < tokens_of(first + p), s, NEGATIVE_FILL))
-        best = [jnp.max(s, axis=1, keepdims=True) for s in scores]
+        best = [jnp.max(s, axis=1, keepdims=True).astype(BF16).astype(F32) for s in scores]
         for p in range(step_pages):
             score[first + p] = scores[p]
         for p in range(step_pages):
             at = rows_of(first + p)
             top[at, :] = jnp.maximum(top[at, :], best[p])
 
-    top[...] = top[...].astype(BF16).astype(F32)
     for load in loads:
         load.wait()
     weight_loads = [pltpu.make_async_copy(w_out, w_out_copy, out_sem.at[len(w_up_copies)])]
@@ -419,8 +427,8 @@
         square = square + before[2][...]
     if last:
         factor = lax.rsqrt(square.T[0:1, :] * (1.0 / total_width) + NORM_EPS)
-    for first in range(0, units, units):
-        here = slice(first, first + units)
+    for first in range(0, units, 512):
+        here = slice(first, min(first + 512, units))
         sums = []
         for n, weight in enumerate((w_gate, w_up)):
             total = None if before is None else before[n][here, :]
@@ -438,6 +446,9 @@
             outs[0][here, :], outs[1][here, :] = sums
     if not last:
         outs[2][...] = square
+    elif waits:
+        product = jnp.dot(outs[0][...], refs[8][...], preferred_element_type=F32)
+        outs[1][...] = product.astype(BF16)
 
 
 def down_kernel(count, hidden, *refs):
@@ -485,16 +496,18 @@
     place = jnp.stack([me, lax.axis_index("head")]).astype(jnp.int32)
     vmem = pl.BlockSpec(memory_space=pltpu.VMEM)
     smem = pl.BlockSpec(memory_space=pltpu.SMEM)
+    anywhere = pl.BlockSpec(memory_space=pl.ANY)
 
     inverse_rows = -(-(pages * req_devices // LO) // 16) * 16
     payload = pl.pallas_call(
         functools.partial(pack_kernel, page_len),
         out_shape=jax.ShapeDtypeStruct((rows + inverse_rows, HEAD_DIM), BF16),
-        in_specs=[smem, smem, vmem, vmem],
+        in_specs=[smem, smem, vmem, anywhere],
         out_specs=vmem,
+        scratch_shapes=[pltpu.VMEM(queries.shape, BF16), pltpu.SemaphoreType.DMA],
         compiler_params=params(),
         name="pack",
-    )(place, in_hbm(lengths), in_hbm(page_table), queries)
+    )(place, in_hbm(lengths), in_hbm(page_table), in_hbm(queries))
     near = [payload] + [swap(payload, "req", 2 * c) for c in range(1, chips)]
     columns = w_out.shape[1]
     gain = pl.pallas_call(
@@ -505,13 +518,24 @@
         compiler_params=params(1),
         name="gain",
     )(norm_gain.reshape(req_devices, columns))
-    keys, = staged([payload, gain], key_pool, name="stage_keys")
-    near = stacked(near, keys)
-    far = swap(near, "req", 1)
+    total_rows = rows * req_devices
+    running = jax.ShapeDtypeStruct((total_rows, HEAD_DIM), F32)
+    keys, *terms = pl.pallas_call(
+        functools.partial(keys_kernel, 4),
+        out_shape=[jax.ShapeDtypeStruct(key_pool.shape, BF16)] + [running] * 3,
+        in_specs=[anywhere] * 3,
+        out_specs=[anywhere] + [vmem] * 3,
+        scratch_shapes=[pltpu.SemaphoreType.DMA((4,))],
+        compiler_params=params(1),
+        cost_estimate=pl.CostEstimate(
+            flops=0, bytes_accessed=2 * math.prod(key_pool.shape), transcendentals=0
+        ),
+        name="stage_keys",
+    )(in_hbm(key_pool), payload, gain)
+    near = [payload] + [stacked([x], keys) for x in near[1:]]
+    far = [swap(x, "req", 1) for x in near]
 
     step_pages = 64
-    total_rows = rows * req_devices
-    anywhere = pl.BlockSpec(memory_space=pl.ANY)
     sent = jax.ShapeDtypeStruct((rows + reqs, HEAD_DIM), BF16)
     copied = jax.ShapeDtypeStruct((hidden_width, columns), BF16)
     steps, early, w_up = range(req_devices), req_devices // 4, w_up.T
@@ -519,15 +543,16 @@
         functools.partial(attend_kernel, req_devices, heads, kv_local, reqs, step_pages),
         out_shape=[sent] * req_devices
         + [jax.ShapeDtypeStruct(w_out.shape, BF16)]
-        + [copied] * early,
-        in_specs=[smem, vmem, vmem, vmem] + [anywhere] * 3,
-        out_specs=[vmem] * req_devices + [anywhere] * (1 + early),
+        + [copied] * early
+        + [running] * 3,
+        in_specs=[smem] + [vmem] * (req_devices + 1) + [anywhere] * 3 + [vmem] * 3,
+        out_specs=[vmem] * req_devices + [anywhere] * (1 + early) + [vmem] * 3,
+        input_output_aliases={
+            req_devices + 5 + n: req_devices + 1 + early + n for n in range(3)
+        },
         scratch_shapes=[
             pltpu.VMEM((total_rows, HEAD_DIM), F32),
             pltpu.VMEM((pages, heads, HEAD_DIM), F32),
-            pltpu.VMEM((total_rows, HEAD_DIM), F32),
-            pltpu.VMEM((total_rows, HEAD_DIM), F32),
-            pltpu.VMEM((total_rows, HEAD_DIM), F32),
             pltpu.VMEM((8, 2 * LO), jnp.int32),
             pltpu.SMEM((8, 2 * LO), jnp.int32),
             pltpu.VMEM(value_pool.shape, BF16),
@@ -535,11 +560,11 @@
             pltpu.SemaphoreType.DMA((4,)),
             pltpu.SemaphoreType.DMA((early + 1,)),
         ],
-        compiler_params=params(24),
+        compiler_params=params(20),
         name="attend",
-    )(place, near, far, keys, in_hbm(value_pool), in_hbm(w_out), in_hbm(w_up))
+    )(place, *near, *far, keys, in_hbm(value_pool), in_hbm(w_out), in_hbm(w_up), *terms)
     partials, w_out, first_up = (
-        attended[:req_devices], attended[req_devices], attended[req_devices + 1 :]
+        attended[:req_devices], attended[req_devices], attended[req_devices + 1 : -3]
     )
     joined = pl.pallas_call(
         functools.partial(join_kernel, heads, reqs),
@@ -615,24 +640,29 @@
     for c in range(chips):
         last = c == chips - 1
         if squares and last:
-            near[c] = [stacked(across, square[1])]
+            near[c] = [across[0]] + [stacked([x], square[2]) for x in across[1:]]
         far = early_far.get(c, []) + [swap(x, "req", 1) for x in near[c][len(early_far.get(c, [])) :]]
         count = len(far)
         ready = early_far.get(2, []) if c == 1 else []
+        if squares and last:
+            ready = [w_down[2 * c + 1]]
         sums = pl.pallas_call(
             functools.partial(hidden_kernel, count, len(ready), c, last, columns * req_devices),
             out_shape=[jax.ShapeDtypeStruct((all_rows, hidden_width), BF16)]
+            + [jax.ShapeDtypeStruct((all_rows, columns), BF16)] * len(ready)
             if last
             else [
                 jax.ShapeDtypeStruct((hidden_width, all_rows), F32),
                 jax.ShapeDtypeStruct((hidden_width, all_rows), F32),
                 jax.ShapeDtypeStruct((all_rows, HEAD_DIM), F32),
             ],
-            in_specs=[smem] + [vmem] * (2 * count + 5 + len(sums)) + [anywhere] * len(ready),
-            out_specs=[vmem] if last else [vmem] * 3,
+            in_specs=[smem]
+            + [vmem] * (2 * count + 5 + len(sums))
+            + [vmem if last else anywhere] * len(ready),
+            out_specs=[vmem] * (1 + len(ready) if last else 3),
             scratch_shapes=[pltpu.VMEM((2, all_rows, columns), BF16)],
             input_output_aliases={} if c == 0 or last else {2 * count + 6 + n: n for n in range(2)},
-            compiler_params=params(8),
+            compiler_params=params(5),
             cost_estimate=pl.CostEstimate(
                 flops=8 * all_rows * columns * hidden_width, bytes_accessed=0, transcendentals=0
             ),
@@ -650,15 +680,15 @@
                 swap(cut_rows(late_x, 0, half), "req", 4),
                 swap(cut_rows(late_y, half, half), "req", 2),
             ]
-    hidden, = sums
-
-
-    def down(wanted, *after):
-        weights = [w_down[2 * c + 1] for c in wanted] + [w_down[2 * c] for c in wanted]
+    hidden = sums[0]
+
+    def down(wanted, *after, near_only=()):
+        weights = [w_down[2 * c + 1] for c in wanted]
+        weights += [w_down[2 * c] for c in (*wanted, *near_only)]
         parts = pl.pallas_call(
             functools.partial(down_kernel, len(weights)),
             out_shape=[jax.ShapeDtypeStruct((all_rows, columns), BF16) for _ in wanted]
-            + [jax.ShapeDtypeStruct((all_rows, columns), F32) for _ in wanted],
+            + [jax.ShapeDtypeStruct((all_rows, columns), F32) for _ in (*wanted, *near_only)],
             in_specs=[vmem] * (1 + len(weights)) + [anywhere] * len(after),
             out_specs=[vmem] * len(weights),
             compiler_params=params(5),
@@ -666,7 +696,8 @@
             name="down",
         )(hidden, *weights, *after)
         far_parts, near_parts = parts[: len(wanted)], parts[len(wanted) :]
-        return [(mine, swap(other, "req", 1)) for mine, other in zip(near_parts, far_parts)]
+        pairs = [(mine, swap(other, "req", 1)) for mine, other in zip(near_parts, far_parts)]
+        return pairs + list(near_parts[len(wanted) :])
 
     def merge(c, layout, halves, passed=(), extra=()):
         layout = [[order.index(a) for a in blocks] for blocks in layout]
@@ -697,7 +728,9 @@
 
     totals = {}
     if squares:
-        (corner,), (halves_x,) = down([3]), down([1])
+        other = swap(sums[1], "req", 1)
+        halves_x, corner = down([1], near_only=[3])
+        corner = (corner, other)
         by_x, by_y = merge(3, [[2, 0], [3, 1]], corner)
         (halves_y,), (halves_own,) = down([2], by_x), down([0], by_x)
         by_x, by_y = swap(by_x, "req", 2), swap(by_y, "req", 4)

time: 143 us -> 142 us (level)
    pallas_call x4 -> x3, Pallas kernels: 5 us -> 4.3 us  [down(): pl.pallas_call(functools.partial(down_kernel, len(weights)), out_shape=[j...]
    ppermute x51 -> x56, waiting for transfers between devices: 45.7 us -> 45.9 us  [swap(): return lax.ppermute(array, axis, [(i, i ^ bits) for i in range(size)])]
    ppermute x51 -> x56, starting transfers between devices: 41.9 us -> 41.8 us  [swap(): return lax.ppermute(array, axis, [(i, i ^ bits) for i in range(size)])]
  transfers between devices with their start and end apart: 51 -> 56, of which waited for: 27 -> 29; matrix products, arithmetic and copies ran while one was open for 1% -> 1% of each run, Pallas kernels for 23% -> 24%
where the time goes in v6:
time: 142 us
  Pallas kernels  52.2 us (37%)
  waiting for transfers between devices  45.9 us (32%)
  starting transfers between devices  41.8 us (29%)
    ppermute x56, waiting for transfers between devices, swap(): return lax.ppermute(array, axis, [(i, i ^ bits) for i in range(size)])  45.9 us
    ppermute x56, starting transfers between devices, swap(): return lax.ppermute(array, axis, [(i, i ^ bits) for i in range(size)])  41.8 us
    pallas_call x2, Pallas kernels, staged_blocks(): pl.pallas_call(functools.partial(split_kernel, len(arrays), wanted), out_...  15.5 us
    pallas_call x4, Pallas kernels, shards(): pl.pallas_call(functools.partial(hidden_kernel, count, len(ready), c, las...  12.6 us
    pallas_call x1, Pallas kernels, shards(): pl.pallas_call(functools.partial(attend_kernel, req_devices, heads, kv_lo...  9.16 us
    pallas_call x1, Pallas kernels, shards(): pl.pallas_call(functools.partial(keys_kernel, 4), out_shape=[jax.ShapeDty...  4.69 us
    pallas_call x3, Pallas kernels, down(): pl.pallas_call(functools.partial(down_kernel, len(weights)), out_shape=[j...  4.3 us
  transfers between devices with their start and end apart: 56, of which 29 were waited for; matrix products, arithmetic and copies ran while one was open for 1% of the time, Pallas kernels for 24%

profile of v6, /device:TPU:0, one launch (start us, length us, event | category | flops | bytes accessed | tf_op | source)
XLA Modules:
  0.0 141.8 jit_solution(2843557204307318697)
XLA Ops:
  1.8 3.0 %collective-permute-start.1 = (bf16[544,128]{1,0:T(8,128)(2,1)S(1)}, bf16[544,128]{1,0:T(8,128)(2,1)S(1)}, u32[]{:S(2)}, u32[]{:S(2)}) collective-permute-start(bf16[544,128]{1,0:T(8,128)(2,1)S(1)} %pack.1.refs_0_.queries), channel_id=1, source_target_pairs={{0,16},{4,20},{8,24},{12,28},{16,0},{20,4},{24,8},{28,12},{1,17},{... | collective-permute-start | bytes 417800 | tf_op jit(solution)/shard_map/ppermute | solution.py:21
  7.1 4.7 %stage_keys.1 = (bf16[192,128,256]{2,1,0:T(8,128)(2,1)S(1)}, f32[4096,128]{1,0:T(8,128)S(1)}, f32[4096,128]{1,0:T(8,128)S(1)}, f32[4096,128]{1,0:T(8,128)S(1)}) custom-call(bf16[192,128,256]{2,1,0:T(8,128)(2,1)} %keys.1, bf16[544,128]{1,0:T(8,128)(2,1)S(1)} %pack.1.refs_0_.queries, f32[8,1024]{1,0:T(8,128)S(1)} %gain.1.refs_1_.refs_4_.refs_6_), custom_call_target="tpu_custom_call" | custom-call | bytes 12582912 | tf_op jit(solution)/shard_map/stage_keys/pallas_call | solution.py:523
  14.3 9.2 %attend.1 = (bf16[544,128]{1,0:T(8,128)(2,1)S(1)}, bf16[544,128]{1,0:T(8,128)(2,1)S(1)}, bf16[544,128]{1,0:T(8,128)(2,1)S(1)}, bf16[544,128]{1,0:T(8,128)(2,1)S(...) custom-call(s32[2]{0:T(128)S(1)} %pad_add_fusion.place, ...), custom_call_target="tpu_custom_call", output_to_operand_aliasing={{11}: (13, {}), {12}: (14, {}), {13}: (15, {})} | custom-call | tf_op jit(solution)/shard_map/attend/pallas_call | solution.py:542
  26.4 2.0 %collective-permute-start.11 = (bf16[544,128]{1,0:T(8,128)(2,1)S(1)}, bf16[544,128]{1,0:T(8,128)(2,1)S(1)}, u32[]{:S(2)}, u32[]{:S(2)}) collective-permute-start(bf16[544,128]{1,0:T(8,128)(2,1)S(1)} %get-tuple-element.94), channel_id=1, source_target_pairs={{0,8},{4,12},{8,0},{12,4},{16,24},{20,28},{24,16},{28,20},{1,9},{5... | collective-permute-start | bytes 417800 | tf_op jit(solution)/shard_map/ppermute | solution.py:21
  30.0 6.1 %stage_gate.1 = (bf16[924,1024]{1,0:T(8,128)(2,1)S(1)}, bf16[924,1024]{1,0:T(8,128)(2,1)S(1)}, bf16[924,1024]{1,0:T(8,128)(2,1)S(1)}, bf16[924,1024]{1,0:T(8,128...) custom-call(s32[2]{0:T(128)S(1)} %pad_add_fusion.place, ...), custom_call_target="tpu_custom_call" | custom-call | bytes 15138816 | tf_op jit(solution)/shard_map/stage_gate/pallas_call | solution.py:104
  41.1 2.4 %collective-permute-done.14.refs_1_ = bf16[32,2048]{1,0:T(8,128)(2,1)S(1)} collective-permute-done((bf16[32,2048]{1,0:T(8,128)(2,1)S(1)}, bf16[32,2048]{1,0:T(8,128)(2,1)S(1)}, u32[]{:S(2)}, u32[]{:S(2)}) %collective-permute-start.14) | collective-permute-done | bytes 131104 | tf_op jit(solution)/shard_map/ppermute | solution.py:21
  43.5 3.1 %collective-permute-done.15.refs_2_ = bf16[32,2048]{1,0:T(8,128)(2,1)S(1)} collective-permute-done((bf16[32,2048]{1,0:T(8,128)(2,1)S(1)}, bf16[32,2048]{1,0:T(8,128)(2,1)S(1)}, u32[]{:S(2)}, u32[]{:S(2)}) %collective-permute-start.15) | collective-permute-done | bytes 131104 | tf_op jit(solution)/shard_map/ppermute | solution.py:21
  48.2 1.9 %project.1 = (f32[64,1024]{1,0:T(8,128)S(1)}, bf16[64,1024]{1,0:T(8,128)(2,1)S(1)}, bf16[64,1024]{1,0:T(8,128)(2,1)S(1)}, bf16[64,1024]{1,0:T(8,128)(2,1)S(1)}) custom-call(s32[2]{0:T(128)S(1)} %pad_add_fusion.place, bf16[32,2048]{1,0:T(8,128)(2,1)S(1)} %combine.1.refs_0_, bf16[32,2048]{1,0:T(8,128)(2,1)S(1)} %collective-permute-done.14.refs_1_, ...), custom_call_target="tpu_custom_call" | custom-call | tf_op jit(solution)/shard_map/project/pallas_call | solution.py:594
  50.0 3.7 %collective-permute-start.21 = (bf16[64,1024]{1,0:T(8,128)(2,1)S(1)}, bf16[64,1024]{1,0:T(8,128)(2,1)S(1)}, u32[]{:S(2)}, u32[]{:S(2)}) collective-permute-start(bf16[64,1024]{1,0:T(8,128)(2,1)S(1)} %get-tuple-element.100), channel_id=1, source_target_pairs={{0,3},{1,2},{2,1},{3,0},{4,7},{5,6},{6,5},{7,4},{8,11},{9,10},{10,... | collective-permute-start | bytes 393224 | tf_op jit(solution)/shard_map/ppermute | solution.py:21
  54.5 9.4 %stage_up_down.1 = (bf16[924,1024]{1,0:T(8,128)(2,1)S(1)}, bf16[924,1024]{1,0:T(8,128)(2,1)S(1)}, bf16[924,1024]{1,0:T(8,128)(2,1)S(1)}, bf16[924,1024]{1,0:T(8,...) custom-call(s32[2]{0:T(128)S(1)} %pad_add_fusion.place, ...), custom_call_target="tpu_custom_call" | custom-call | bytes 26492928 | tf_op jit(solution)/shard_map/stage_up_down/pallas_call | solution.py:104
  65.8 2.5 %collective-permute-start.26 = (bf16[64,1024]{1,0:T(8,128)(2,1)S(1)}, bf16[64,1024]{1,0:T(8,128)(2,1)S(1)}, u32[]{:S(2)}, u32[]{:S(2)}) collective-permute-start(bf16[64,1024]{1,0:T(8,128)(2,1)S(1)} %state.1.refs_0_), channel_id=1, source_target_pairs={{0,3},{1,2},{2,1},{3,0},{4,7},{5,6},{6,5},{7,4},{8,11},{9,10},{10,... | collective-permute-start | bytes 393224 | tf_op jit(solution)/shard_map/ppermute | solution.py:21
  68.3 1.9 %collective-permute-start.28 = (bf16[64,1024]{1,0:T(8,128)(2,1)S(1)}, bf16[64,1024]{1,0:T(8,128)(2,1)S(1)}, u32[]{:S(2)}, u32[]{:S(2)}) collective-permute-start(bf16[64,1024]{1,0:T(8,128)(2,1)S(1)} %state.1.refs_0_), channel_id=1, source_target_pairs={{0,1},{1,0},{2,3},{3,2},{4,5},{5,4},{6,7},{7,6},{8,9},{9,8},{10,11... | collective-permute-start | bytes 393224 | tf_op jit(solution)/shard_map/ppermute | solution.py:21
  72.2 1.8 %collective-permute-done.26.refs_0_ = bf16[64,1024]{1,0:T(8,128)(2,1)S(1)} collective-permute-done((bf16[64,1024]{1,0:T(8,128)(2,1)S(1)}, bf16[64,1024]{1,0:T(8,128)(2,1)S(1)}, u32[]{:S(2)}, u32[]{:S(2)}) %collective-permute-start.26) | collective-permute-done | bytes 131104 | tf_op jit(solution)/shard_map/ppermute | solution.py:21
  74.0 4.7 %collective-permute-done.27.refs_1_ = bf16[64,1024]{1,0:T(8,128)(2,1)S(1)} collective-permute-done((bf16[64,1024]{1,0:T(8,128)(2,1)S(1)}, bf16[64,1024]{1,0:T(8,128)(2,1)S(1)}, u32[]{:S(2)}, u32[]{:S(2)}) %collective-permute-start.27) | collective-permute-done | bytes 131104 | tf_op jit(solution)/shard_map/ppermute | solution.py:21
  81.7 2.8 %hidden.4 = (f32[924,256]{1,0:T(8,128)S(1)}, f32[924,256]{1,0:T(8,128)S(1)}, f32[256,128]{1,0:T(8,128)S(1)}) custom-call(s32[2]{0:T(128)S(1)} %pad_add_fusion.place, bf16[64,1024]{1,0:T(8,128)(2,1)S(1)} %state.1.refs_0_, bf16[192,1024]{1,0:T(8,128)(2,1)S(1)} %stack.23.refs_1_, bf16[64,1024]{1,0:T(8,128)(2,1)S(1)} %collective-permute-done.31.refs_2_, ...), custom_call_target="tpu_custom_call" | custom-call | flops 1937768448 | tf_op jit(solution)/shard_map/hidden/pallas_call | solution.py:649
  84.6 5.8 %collective-permute-done.30.refs_0_ = bf16[192,1024]{1,0:T(8,128)(2,1)S(1)} collective-permute-done((bf16[192,1024]{1,0:T(8,128)(2,1)S(1)}, bf16[192,1024]{1,0:T(8,128)(2,1)S(1)}, u32[]{:S(2)}, u32[]{:S(2)}) %collective-permute-start.30) | collective-permute-done | bytes 393248 | tf_op jit(solution)/shard_map/ppermute | solution.py:21
  95.0 3.0 %hidden.5 = (f32[924,256]{1,0:T(8,128)S(1)}, f32[924,256]{1,0:T(8,128)S(1)}, f32[256,128]{1,0:T(8,128)S(1)}) custom-call(s32[2]{0:T(128)S(1)} %pad_add_fusion.place, bf16[64,1024]{1,0:T(8,128)(2,1)S(1)} %collective-permute-done.24.refs_3_.refs_0_, bf16[192,1024]{1,0:T(8,128)(2,1)S(1)} %stack.24.source.refs_1_, ...), custom_call_target="tpu_custom_call", output_to_operand_aliasing={{0}: (10, {}), {1}: (11, {})} | custom-call | flops 1937768448 | tf_op jit(solution)/shard_map/hidden/pallas_call | solution.py:649
  98.0 3.0 %hidden.6 = (f32[924,256]{1,0:T(8,128)S(1)}, f32[924,256]{1,0:T(8,128)S(1)}, f32[256,128]{1,0:T(8,128)S(1)}) custom-call(s32[2]{0:T(128)S(1)} %pad_add_fusion.place, bf16[64,1024]{1,0:T(8,128)(2,1)S(1)} %collective-permute-done.29.refs_4_.refs_0_, bf16[192,1024]{1,0:T(8,128)(2,1)S(1)} %stack.25.refs_1_.source, ...), custom_call_target="tpu_custom_call", output_to_operand_aliasing={{0}: (10, {}), {1}: (11, {})} | custom-call | flops 1937768448 | tf_op jit(solution)/shard_map/hidden/pallas_call | solution.py:649
  103.0 3.9 %hidden.7 = (bf16[256,924]{1,0:T(8,128)(2,1)S(1)}, bf16[256,1024]{1,0:T(8,128)(2,1)S(1)}) custom-call(s32[2]{0:T(128)S(1)} %pad_add_fusion.place, bf16[64,1024]{1,0:T(8,128)(2,1)S(1)} %collective-permute-done.25.refs_5_.refs_0_, bf16[96,1024]{1,0:T(8,128)(2,1)S(1)} %stack.26.refs_1_, bf16[96,1024]{1,0:T(8,128)(2,1)S(1)} %stack.27.refs_2_, ...), custom_call_target="tpu_custom_call" | custom-call | flops 1937768448 | tf_op jit(solution)/shard_map/hidden/pallas_call | solution.py:649
  114.1 5.3 %collective-permute-done.46.refs_0_ = bf16[128,1024]{1,0:T(8,128)(2,1)S(1)} collective-permute-done((bf16[128,1024]{1,0:T(8,128)(2,1)S(1)}, bf16[128,1024]{1,0:T(8,128)(2,1)S(1)}, u32[]{:S(2)}, u32[]{:S(2)}) %collective-permute-start.46) | collective-permute-done | bytes 262176 | tf_op jit(solution)/shard_map/ppermute | solution.py:21
  124.0 4.9 %collective-permute-done.51.refs_1_ = bf16[128,1024]{1,0:T(8,128)(2,1)S(1)} collective-permute-done((bf16[128,1024]{1,0:T(8,128)(2,1)S(1)}, bf16[128,1024]{1,0:T(8,128)(2,1)S(1)}, u32[]{:S(2)}, u32[]{:S(2)}) %collective-permute-start.51) | collective-permute-done | bytes 262176 | tf_op jit(solution)/shard_map/ppermute | solution.py:21
  130.0 2.4 %collective-permute-start.53 = (bf16[64,1024]{1,0:T(8,128)(2,1)S(1)}, bf16[64,1024]{1,0:T(8,128)(2,1)S(1)}, u32[]{:S(2)}, u32[]{:S(2)}) collective-permute-start(bf16[64,1024]{1,0:T(8,128)(2,1)S(1)} %get-tuple-element.152), channel_id=1, source_target_pairs={{0,3},{1,2},{2,1},{3,0},{4,7},{5,6},{6,5},{7,4},{8,11},{9,10},{10,... | collective-permute-start | bytes 393224 | tf_op jit(solution)/shard_map/ppermute | solution.py:21
  134.6 3.6 %collective-permute-done.53 = bf16[64,1024]{1,0:T(8,128)(2,1)S(1)} collective-permute-done((bf16[64,1024]{1,0:T(8,128)(2,1)S(1)}, bf16[64,1024]{1,0:T(8,128)(2,1)S(1)}, u32[]{:S(2)}, u32[]{:S(2)}) %collective-permute-start.53) | collective-permute-done | bytes 131104 | tf_op jit(solution)/shard_map/ppermute | solution.py:21
  138.2 2.5 %collective-permute-done.54 = bf16[64,1024]{1,0:T(8,128)(2,1)S(1)} collective-permute-done((bf16[64,1024]{1,0:T(8,128)(2,1)S(1)}, bf16[64,1024]{1,0:T(8,128)(2,1)S(1)}, u32[]{:S(2)}, u32[]{:S(2)}) %collective-permute-start.54) | collective-permute-done | bytes 131104 | tf_op jit(solution)/shard_map/ppermute | solution.py:21
  (130 shorter events, 48.1 us)
Async XLA Ops:
  1.8 10.0 %collective-permute-start.1 = (bf16[544,128]{1,0:T(8,128)(2,1)S(1)}, bf16[544,128]{1,0:T(8,128)(2,1)S(1)}, u32[]{:S(2)}, u32[]{:S(2)}) collective-permute-start(bf16[544,128]{1,0:T(8,128)(2,1)S(1)} %pack.1.refs_0_.queries), channel_id=1, source_target_pairs={{0,16},{4,20},{8,24},{12,28},{16,0},{20,4},{24,8},{28,12},{1,17},{... | collective-permute-start | bytes 417800 | tf_op jit(solution)/shard_map/ppermute | solution.py:21
  26.4 9.6 %collective-permute-start.11 = (bf16[544,128]{1,0:T(8,128)(2,1)S(1)}, bf16[544,128]{1,0:T(8,128)(2,1)S(1)}, u32[]{:S(2)}, u32[]{:S(2)}) collective-permute-start(bf16[544,128]{1,0:T(8,128)(2,1)S(1)} %get-tuple-element.94), channel_id=1, source_target_pairs={{0,8},{4,12},{8,0},{12,4},{16,24},{20,28},{24,16},{28,20},{1,9},{5... | collective-permute-start | bytes 417800 | tf_op jit(solution)/shard_map/ppermute | solution.py:21
  28.4 8.5 %collective-permute-start.12 = (bf16[544,128]{1,0:T(8,128)(2,1)S(1)}, bf16[544,128]{1,0:T(8,128)(2,1)S(1)}, u32[]{:S(2)}, u32[]{:S(2)}) collective-permute-start(bf16[544,128]{1,0:T(8,128)(2,1)S(1)} %get-tuple-element.95), channel_id=1, source_target_pairs={{0,16},{4,20},{8,24},{12,28},{16,0},{20,4},{24,8},{28,12},{1,17},{... | collective-permute-start | bytes 417800 | tf_op jit(solution)/shard_map/ppermute | solution.py:21
  38.8 7.8 %collective-permute-start.15 = (bf16[32,2048]{1,0:T(8,128)(2,1)S(1)}, bf16[32,2048]{1,0:T(8,128)(2,1)S(1)}, u32[]{:S(2)}, u32[]{:S(2)}) collective-permute-start(bf16[32,2048]{1,0:T(8,128)(2,1)S(1)} %combine.1.refs_0_), channel_id=1, source_target_pairs={{0,16},{4,20},{8,24},{12,28},{16,0},{20,4},{24,8},{28,12},{1,17},{... | collective-permute-start | bytes 393224 | tf_op jit(solution)/shard_map/ppermute | solution.py:21
  50.0 13.9 %collective-permute-start.21 = (bf16[64,1024]{1,0:T(8,128)(2,1)S(1)}, bf16[64,1024]{1,0:T(8,128)(2,1)S(1)}, u32[]{:S(2)}, u32[]{:S(2)}) collective-permute-start(bf16[64,1024]{1,0:T(8,128)(2,1)S(1)} %get-tuple-element.100), channel_id=1, source_target_pairs={{0,3},{1,2},{2,1},{3,0},{4,7},{5,6},{6,5},{7,4},{8,11},{9,10},{10,... | collective-permute-start | bytes 393224 | tf_op jit(solution)/shard_map/ppermute | solution.py:21
  53.7 11.6 %collective-permute-start.22 = (bf16[64,1024]{1,0:T(8,128)(2,1)S(1)}, bf16[64,1024]{1,0:T(8,128)(2,1)S(1)}, u32[]{:S(2)}, u32[]{:S(2)}) collective-permute-start(bf16[64,1024]{1,0:T(8,128)(2,1)S(1)} %get-tuple-element.101), channel_id=1, source_target_pairs={{0,2},{1,3},{2,0},{3,1},{4,6},{5,7},{6,4},{7,5},{8,10},{9,11},{10,... | collective-permute-start | bytes 393224 | tf_op jit(solution)/shard_map/ppermute | solution.py:21
  53.7 11.6 %collective-permute-start.23 = (bf16[64,1024]{1,0:T(8,128)(2,1)S(1)}, bf16[64,1024]{1,0:T(8,128)(2,1)S(1)}, u32[]{:S(2)}, u32[]{:S(2)}) collective-permute-start(bf16[64,1024]{1,0:T(8,128)(2,1)S(1)} %get-tuple-element.102), channel_id=1, source_target_pairs={{0,1},{1,0},{2,3},{3,2},{4,5},{5,4},{6,7},{7,6},{8,9},{9,8},{10,11... | collective-permute-start | bytes 393224 | tf_op jit(solution)/shard_map/ppermute | solution.py:21
  65.8 8.2 %collective-permute-start.26 = (bf16[64,1024]{1,0:T(8,128)(2,1)S(1)}, bf16[64,1024]{1,0:T(8,128)(2,1)S(1)}, u32[]{:S(2)}, u32[]{:S(2)}) collective-permute-start(bf16[64,1024]{1,0:T(8,128)(2,1)S(1)} %state.1.refs_0_), channel_id=1, source_target_pairs={{0,3},{1,2},{2,1},{3,0},{4,7},{5,6},{6,5},{7,4},{8,11},{9,10},{10,... | collective-permute-start | bytes 393224 | tf_op jit(solution)/shard_map/ppermute | solution.py:21
  68.3 10.4 %collective-permute-start.27 = (bf16[64,1024]{1,0:T(8,128)(2,1)S(1)}, bf16[64,1024]{1,0:T(8,128)(2,1)S(1)}, u32[]{:S(2)}, u32[]{:S(2)}) collective-permute-start(bf16[64,1024]{1,0:T(8,128)(2,1)S(1)} %state.1.refs_0_), channel_id=1, source_target_pairs={{0,2},{1,3},{2,0},{3,1},{4,6},{5,7},{6,4},{7,5},{8,10},{9,11},{10,... | collective-permute-start | bytes 393224 | tf_op jit(solution)/shard_map/ppermute | solution.py:21
  68.3 10.4 %collective-permute-start.28 = (bf16[64,1024]{1,0:T(8,128)(2,1)S(1)}, bf16[64,1024]{1,0:T(8,128)(2,1)S(1)}, u32[]{:S(2)}, u32[]{:S(2)}) collective-permute-start(bf16[64,1024]{1,0:T(8,128)(2,1)S(1)} %state.1.refs_0_), channel_id=1, source_target_pairs={{0,1},{1,0},{2,3},{3,2},{4,5},{5,4},{6,7},{7,6},{8,9},{9,8},{10,11... | collective-permute-start | bytes 393224 | tf_op jit(solution)/shard_map/ppermute | solution.py:21
  70.2 8.5 %collective-permute-start.29 = (bf16[64,1024]{1,0:T(8,128)(2,1)S(1)}, bf16[64,1024]{1,0:T(8,128)(2,1)S(1)}, u32[]{:S(2)}, u32[]{:S(2)}) collective-permute-start(bf16[64,1024]{1,0:T(8,128)(2,1)S(1)} %state.1.refs_0_), channel_id=1, source_target_pairs={{0,16},{4,20},{8,24},{12,28},{16,0},{20,4},{24,8},{28,12},{1,17},{... | collective-permute-start | bytes 393224 | tf_op jit(solution)/shard_map/ppermute | solution.py:21
  78.9 11.5 %collective-permute-start.30 = (bf16[192,1024]{1,0:T(8,128)(2,1)S(1)}, bf16[192,1024]{1,0:T(8,128)(2,1)S(1)}, u32[]{:S(2)}, u32[]{:S(2)}) collective-permute-start(bf16[192,1024]{1,0:T(8,128)(2,1)S(1)} %stack.23.refs_1_), channel_id=1, source_target_pairs={{0,8},{4,12},{8,0},{12,4},{16,24},{20,28},{24,16},{28,20},{1,9},{5... | collective-permute-start | bytes 1179656 | tf_op jit(solution)/shard_map/ppermute | solution.py:21
  80.6 11.4 %collective-permute-start.34 = (bf16[192,1024]{1,0:T(8,128)(2,1)S(1)}, bf16[192,1024]{1,0:T(8,128)(2,1)S(1)}, u32[]{:S(2)}, u32[]{:S(2)}) collective-permute-start(bf16[192,1024]{1,0:T(8,128)(2,1)S(1)} %stack.23.refs_1_), channel_id=1, source_target_pairs={{0,16},{4,20},{8,24},{12,28},{16,0},{20,4},{24,8},{28,12},{1,17},{... | collective-permute-start | bytes 1179656 | tf_op jit(solution)/shard_map/ppermute | solution.py:21
  92.7 8.3 %collective-permute-start.39 = (bf16[96,1024]{1,0:T(8,128)(2,1)S(1)}, bf16[96,1024]{1,0:T(8,128)(2,1)S(1)}, u32[]{:S(2)}, u32[]{:S(2)}) collective-permute-start(bf16[96,1024]{1,0:T(8,128)(2,1)S(1)} %rows.3), channel_id=1, source_target_pairs={{0,8},{4,12},{8,0},{12,4},{16,24},{20,28},{24,16},{28,20},{1,9},{5... | collective-permute-start | bytes 589832 | tf_op jit(solution)/shard_map/ppermute | solution.py:21
  110.7 9.8 %collective-permute-start.48 = (bf16[256,1024]{1,0:T(8,128)(2,1)S(1)}, bf16[256,1024]{1,0:T(8,128)(2,1)S(1)}, u32[]{:S(2)}, u32[]{:S(2)}) collective-permute-start(bf16[256,1024]{1,0:T(8,128)(2,1)S(1)} %get-tuple-element.146), channel_id=1, source_target_pairs={{0,4},{4,0},{8,12},{12,8},{16,20},{20,16},{24,28},{28,24},{1,5},{5... | collective-permute-start | bytes 1572872 | tf_op jit(solution)/shard_map/ppermute | solution.py:21
  111.0 8.4 %collective-permute-start.46 = (bf16[128,1024]{1,0:T(8,128)(2,1)S(1)}, bf16[128,1024]{1,0:T(8,128)(2,1)S(1)}, u32[]{:S(2)}, u32[]{:S(2)}) collective-permute-start(bf16[128,1024]{1,0:T(8,128)(2,1)S(1)} %get-tuple-element.141), channel_id=1, source_target_pairs={{0,16},{4,20},{8,24},{12,28},{16,0},{20,4},{24,8},{28,12},{1,17},{... | collective-permute-start | bytes 786440 | tf_op jit(solution)/shard_map/ppermute | solution.py:21
  112.0 8.5 %collective-permute-start.49 = (bf16[128,1024]{1,0:T(8,128)(2,1)S(1)}, bf16[128,1024]{1,0:T(8,128)(2,1)S(1)}, u32[]{:S(2)}, u32[]{:S(2)}) collective-permute-start(bf16[128,1024]{1,0:T(8,128)(2,1)S(1)} %get-tuple-element.135.refs_2_), channel_id=1, source_target_pairs={{0,8},{4,12},{8,0},{12,4},{16,24},{20,28},{24,16},{28,20},{1,9},{5... | collective-permute-start | bytes 786440 | tf_op jit(solution)/shard_map/ppermute | solution.py:21
  114.0 9.9 %collective-permute-start.44 = (bf16[256,1024]{1,0:T(8,128)(2,1)S(1)}, bf16[256,1024]{1,0:T(8,128)(2,1)S(1)}, u32[]{:S(2)}, u32[]{:S(2)}) collective-permute-start(bf16[256,1024]{1,0:T(8,128)(2,1)S(1)} %get-tuple-element.137), channel_id=1, source_target_pairs={{0,4},{4,0},{8,12},{12,8},{16,20},{20,16},{24,28},{28,24},{1,5},{5... | collective-permute-start | bytes 1572872 | tf_op jit(solution)/shard_map/ppermute | solution.py:21
  119.6 9.3 %collective-permute-start.51 = (bf16[128,1024]{1,0:T(8,128)(2,1)S(1)}, bf16[128,1024]{1,0:T(8,128)(2,1)S(1)}, u32[]{:S(2)}, u32[]{:S(2)}) collective-permute-start(bf16[128,1024]{1,0:T(8,128)(2,1)S(1)} %get-tuple-element.150), channel_id=1, source_target_pairs={{0,8},{4,12},{8,0},{12,4},{16,24},{20,28},{24,16},{28,20},{1,9},{5... | collective-permute-start | bytes 786440 | tf_op jit(solution)/shard_map/ppermute | solution.py:21
  120.6 9.3 %collective-permute-start.52 = (bf16[128,1024]{1,0:T(8,128)(2,1)S(1)}, bf16[128,1024]{1,0:T(8,128)(2,1)S(1)}, u32[]{:S(2)}, u32[]{:S(2)}) collective-permute-start(bf16[128,1024]{1,0:T(8,128)(2,1)S(1)} %get-tuple-element.151), channel_id=1, source_target_pairs={{0,16},{4,20},{8,24},{12,28},{16,0},{20,4},{24,8},{28,12},{1,17},{... | collective-permute-start | bytes 786440 | tf_op jit(solution)/shard_map/ppermute | solution.py:21
  121.7 11.2 %collective-permute-start.47 = (bf16[128,1024]{1,0:T(8,128)(2,1)S(1)}, bf16[128,1024]{1,0:T(8,128)(2,1)S(1)}, u32[]{:S(2)}, u32[]{:S(2)}) collective-permute-start(bf16[128,1024]{1,0:T(8,128)(2,1)S(1)} %get-tuple-element.142), channel_id=1, source_target_pairs={{0,8},{4,12},{8,0},{12,4},{16,24},{20,28},{24,16},{28,20},{1,9},{5... | collective-permute-start | bytes 786440 | tf_op jit(solution)/shard_map/ppermute | solution.py:21
  122.9 10.8 %collective-permute-start.50 = (bf16[128,1024]{1,0:T(8,128)(2,1)S(1)}, bf16[128,1024]{1,0:T(8,128)(2,1)S(1)}, u32[]{:S(2)}, u32[]{:S(2)}) collective-permute-start(bf16[128,1024]{1,0:T(8,128)(2,1)S(1)} %get-tuple-element.147), channel_id=1, source_target_pairs={{0,16},{4,20},{8,24},{12,28},{16,0},{20,4},{24,8},{28,12},{1,17},{... | collective-permute-start | bytes 786440 | tf_op jit(solution)/shard_map/ppermute | solution.py:21
  130.0 8.2 %collective-permute-start.53 = (bf16[64,1024]{1,0:T(8,128)(2,1)S(1)}, bf16[64,1024]{1,0:T(8,128)(2,1)S(1)}, u32[]{:S(2)}, u32[]{:S(2)}) collective-permute-start(bf16[64,1024]{1,0:T(8,128)(2,1)S(1)} %get-tuple-element.152), channel_id=1, source_target_pairs={{0,3},{1,2},{2,1},{3,0},{4,7},{5,6},{6,5},{7,4},{8,11},{9,10},{10,... | collective-permute-start | bytes 393224 | tf_op jit(solution)/shard_map/ppermute | solution.py:21
  132.5 8.3 %collective-permute-start.54 = (bf16[64,1024]{1,0:T(8,128)(2,1)S(1)}, bf16[64,1024]{1,0:T(8,128)(2,1)S(1)}, u32[]{:S(2)}, u32[]{:S(2)}) collective-permute-start(bf16[64,1024]{1,0:T(8,128)(2,1)S(1)} %get-tuple-element.153), channel_id=1, source_target_pairs={{0,2},{1,3},{2,0},{3,1},{4,6},{5,7},{6,4},{7,5},{8,10},{9,11},{10,... | collective-permute-start | bytes 393224 | tf_op jit(solution)/shard_map/ppermute | solution.py:21
  (35 other events, 147.2 us)

commit v7 on v6

--- a/solution.py
+++ b/solution.py
@@ -213,7 +213,7 @@
     half = lax.broadcasted_iota(jnp.int32, (8, 2 * LO), 1)
     total = jnp.zeros((8, 2 * LO), F32)
     for n, source in enumerate(sources):
-        query[pl.ds(n * rows, rows), :] = source[pl.ds(0, rows), :].astype(F32)
+        query[pl.ds(n * rows, rows), :] = source[pl.ds(0, rows), :].astype(query.dtype)
         part = jnp.dot(
             pick.astype(BF16), source[pl.ds(rows, inverse_rows), :], preferred_element_type=F32
         )
@@ -234,7 +234,7 @@
         first = step * step_pages
         scores = []
         for p in range(step_pages):
-            q = query[rows_of(first + p), :]
+            q = query[rows_of(first + p), :].astype(F32)
             q = jnp.concatenate(
                 [jnp.where(head // group == kv, q, 0.0) for kv in range(kv_local)], axis=1
             ).astype(BF16)
@@ -535,7 +535,7 @@
     near = [payload] + [stacked([x], keys) for x in near[1:]]
     far = [swap(x, "req", 1) for x in near]
 
-    step_pages = 64
+    step_pages = 96
     sent = jax.ShapeDtypeStruct((rows + reqs, HEAD_DIM), BF16)
     copied = jax.ShapeDtypeStruct((hidden_width, columns), BF16)
     steps, early, w_up = range(req_devices), req_devices // 4, w_up.T
@@ -551,7 +551,7 @@
             req_devices + 5 + n: req_devices + 1 + early + n for n in range(3)
         },
         scratch_shapes=[
-            pltpu.VMEM((total_rows, HEAD_DIM), F32),
+            pltpu.VMEM((total_rows, HEAD_DIM), F32 if heads % 16 else BF16),
             pltpu.VMEM((pages, heads, HEAD_DIM), F32),
             pltpu.VMEM((8, 2 * LO), jnp.int32),
             pltpu.SMEM((8, 2 * LO), jnp.int32),

time: 142 us -> 142 us (level)
  no operation moved by 1% of the time
where the time goes in v7:
time: 142 us
  Pallas kernels  52.1 us (37%)
  waiting for transfers between devices  45.8 us (32%)
  starting transfers between devices  41.9 us (30%)
    ppermute x56, waiting for transfers between devices, swap(): return lax.ppermute(array, axis, [(i, i ^ bits) for i in range(size)])  45.8 us
    ppermute x56, starting transfers between devices, swap(): return lax.ppermute(array, axis, [(i, i ^ bits) for i in range(size)])  41.9 us
    pallas_call x2, Pallas kernels, staged_blocks(): pl.pallas_call(functools.partial(split_kernel, len(arrays), wanted), out_...  15.5 us
    pallas_call x4, Pallas kernels, shards(): pl.pallas_call(functools.partial(hidden_kernel, count, len(ready), c, las...  12.6 us
    pallas_call x1, Pallas kernels, shards(): pl.pallas_call(functools.partial(attend_kernel, req_devices, heads, kv_lo...  9.09 us
    pallas_call x1, Pallas kernels, shards(): pl.pallas_call(functools.partial(keys_kernel, 4), out_shape=[jax.ShapeDty...  4.69 us
    pallas_call x3, Pallas kernels, down(): pl.pallas_call(functools.partial(down_kernel, len(weights)), out_shape=[j...  4.3 us
  transfers between devices with their start and end apart: 56, of which 29 were waited for; matrix products, arithmetic and copies ran while one was open for 1% of the time, Pallas kernels for 24%

profile of v7, /device:TPU:0, one launch (start us, length us, event | category | flops | bytes accessed | tf_op | source)
XLA Modules:
  0.0 141.7 jit_solution(8555877439329790689)
XLA Ops:
  1.8 3.0 %collective-permute-start.1 = (bf16[544,128]{1,0:T(8,128)(2,1)S(1)}, bf16[544,128]{1,0:T(8,128)(2,1)S(1)}, u32[]{:S(2)}, u32[]{:S(2)}) collective-permute-start(bf16[544,128]{1,0:T(8,128)(2,1)S(1)} %pack.1.refs_0_.queries), channel_id=1, source_target_pairs={{0,16},{4,20},{8,24},{12,28},{16,0},{20,4},{24,8},{28,12},{1,17},{... | collective-permute-start | bytes 417800 | tf_op jit(solution)/shard_map/ppermute | solution.py:21
  7.1 4.7 %stage_keys.1 = (bf16[192,128,256]{2,1,0:T(8,128)(2,1)S(1)}, f32[4096,128]{1,0:T(8,128)S(1)}, f32[4096,128]{1,0:T(8,128)S(1)}, f32[4096,128]{1,0:T(8,128)S(1)}) custom-call(bf16[192,128,256]{2,1,0:T(8,128)(2,1)} %keys.1, bf16[544,128]{1,0:T(8,128)(2,1)S(1)} %pack.1.refs_0_.queries, f32[8,1024]{1,0:T(8,128)S(1)} %gain.1.refs_1_.refs_4_.refs_6_), custom_call_target="tpu_custom_call" | custom-call | bytes 12582912 | tf_op jit(solution)/shard_map/stage_keys/pallas_call | solution.py:523
  14.3 9.1 %attend.1 = (bf16[544,128]{1,0:T(8,128)(2,1)S(1)}, bf16[544,128]{1,0:T(8,128)(2,1)S(1)}, bf16[544,128]{1,0:T(8,128)(2,1)S(1)}, bf16[544,128]{1,0:T(8,128)(2,1)S(...) custom-call(s32[2]{0:T(128)S(1)} %pad_add_fusion.place, ...), custom_call_target="tpu_custom_call", output_to_operand_aliasing={{11}: (13, {}), {12}: (14, {}), {13}: (15, {})} | custom-call | tf_op jit(solution)/shard_map/attend/pallas_call | solution.py:542
  26.4 2.0 %collective-permute-start.11 = (bf16[544,128]{1,0:T(8,128)(2,1)S(1)}, bf16[544,128]{1,0:T(8,128)(2,1)S(1)}, u32[]{:S(2)}, u32[]{:S(2)}) collective-permute-start(bf16[544,128]{1,0:T(8,128)(2,1)S(1)} %get-tuple-element.94), channel_id=1, source_target_pairs={{0,8},{4,12},{8,0},{12,4},{16,24},{20,28},{24,16},{28,20},{1,9},{5... | collective-permute-start | bytes 417800 | tf_op jit(solution)/shard_map/ppermute | solution.py:21
  29.9 6.1 %stage_gate.1 = (bf16[924,1024]{1,0:T(8,128)(2,1)S(1)}, bf16[924,1024]{1,0:T(8,128)(2,1)S(1)}, bf16[924,1024]{1,0:T(8,128)(2,1)S(1)}, bf16[924,1024]{1,0:T(8,128...) custom-call(s32[2]{0:T(128)S(1)} %pad_add_fusion.place, ...), custom_call_target="tpu_custom_call" | custom-call | bytes 15138816 | tf_op jit(solution)/shard_map/stage_gate/pallas_call | solution.py:104
  41.0 2.4 %collective-permute-done.14.refs_1_ = bf16[32,2048]{1,0:T(8,128)(2,1)S(1)} collective-permute-done((bf16[32,2048]{1,0:T(8,128)(2,1)S(1)}, bf16[32,2048]{1,0:T(8,128)(2,1)S(1)}, u32[]{:S(2)}, u32[]{:S(2)}) %collective-permute-start.14) | collective-permute-done | bytes 131104 | tf_op jit(solution)/shard_map/ppermute | solution.py:21
  43.5 3.1 %collective-permute-done.15.refs_2_ = bf16[32,2048]{1,0:T(8,128)(2,1)S(1)} collective-permute-done((bf16[32,2048]{1,0:T(8,128)(2,1)S(1)}, bf16[32,2048]{1,0:T(8,128)(2,1)S(1)}, u32[]{:S(2)}, u32[]{:S(2)}) %collective-permute-start.15) | collective-permute-done | bytes 131104 | tf_op jit(solution)/shard_map/ppermute | solution.py:21
  48.1 1.9 %project.1 = (f32[64,1024]{1,0:T(8,128)S(1)}, bf16[64,1024]{1,0:T(8,128)(2,1)S(1)}, bf16[64,1024]{1,0:T(8,128)(2,1)S(1)}, bf16[64,1024]{1,0:T(8,128)(2,1)S(1)}) custom-call(s32[2]{0:T(128)S(1)} %pad_add_fusion.place, bf16[32,2048]{1,0:T(8,128)(2,1)S(1)} %combine.1.refs_0_, bf16[32,2048]{1,0:T(8,128)(2,1)S(1)} %collective-permute-done.14.refs_1_, ...), custom_call_target="tpu_custom_call" | custom-call | tf_op jit(solution)/shard_map/project/pallas_call | solution.py:594
  49.9 3.7 %collective-permute-start.21 = (bf16[64,1024]{1,0:T(8,128)(2,1)S(1)}, bf16[64,1024]{1,0:T(8,128)(2,1)S(1)}, u32[]{:S(2)}, u32[]{:S(2)}) collective-permute-start(bf16[64,1024]{1,0:T(8,128)(2,1)S(1)} %get-tuple-element.100), channel_id=1, source_target_pairs={{0,3},{1,2},{2,1},{3,0},{4,7},{5,6},{6,5},{7,4},{8,11},{9,10},{10,... | collective-permute-start | bytes 393224 | tf_op jit(solution)/shard_map/ppermute | solution.py:21
  54.4 9.4 %stage_up_down.1 = (bf16[924,1024]{1,0:T(8,128)(2,1)S(1)}, bf16[924,1024]{1,0:T(8,128)(2,1)S(1)}, bf16[924,1024]{1,0:T(8,128)(2,1)S(1)}, bf16[924,1024]{1,0:T(8,...) custom-call(s32[2]{0:T(128)S(1)} %pad_add_fusion.place, ...), custom_call_target="tpu_custom_call" | custom-call | bytes 26492928 | tf_op jit(solution)/shard_map/stage_up_down/pallas_call | solution.py:104
  65.7 2.5 %collective-permute-start.26 = (bf16[64,1024]{1,0:T(8,128)(2,1)S(1)}, bf16[64,1024]{1,0:T(8,128)(2,1)S(1)}, u32[]{:S(2)}, u32[]{:S(2)}) collective-permute-start(bf16[64,1024]{1,0:T(8,128)(2,1)S(1)} %state.1.refs_0_), channel_id=1, source_target_pairs={{0,3},{1,2},{2,1},{3,0},{4,7},{5,6},{6,5},{7,4},{8,11},{9,10},{10,... | collective-permute-start | bytes 393224 | tf_op jit(solution)/shard_map/ppermute | solution.py:21
  68.2 1.9 %collective-permute-start.28 = (bf16[64,1024]{1,0:T(8,128)(2,1)S(1)}, bf16[64,1024]{1,0:T(8,128)(2,1)S(1)}, u32[]{:S(2)}, u32[]{:S(2)}) collective-permute-start(bf16[64,1024]{1,0:T(8,128)(2,1)S(1)} %state.1.refs_0_), channel_id=1, source_target_pairs={{0,1},{1,0},{2,3},{3,2},{4,5},{5,4},{6,7},{7,6},{8,9},{9,8},{10,11... | collective-permute-start | bytes 393224 | tf_op jit(solution)/shard_map/ppermute | solution.py:21
  72.1 1.8 %collective-permute-done.26.refs_0_ = bf16[64,1024]{1,0:T(8,128)(2,1)S(1)} collective-permute-done((bf16[64,1024]{1,0:T(8,128)(2,1)S(1)}, bf16[64,1024]{1,0:T(8,128)(2,1)S(1)}, u32[]{:S(2)}, u32[]{:S(2)}) %collective-permute-start.26) | collective-permute-done | bytes 131104 | tf_op jit(solution)/shard_map/ppermute | solution.py:21
  74.0 4.7 %collective-permute-done.27.refs_1_ = bf16[64,1024]{1,0:T(8,128)(2,1)S(1)} collective-permute-done((bf16[64,1024]{1,0:T(8,128)(2,1)S(1)}, bf16[64,1024]{1,0:T(8,128)(2,1)S(1)}, u32[]{:S(2)}, u32[]{:S(2)}) %collective-permute-start.27) | collective-permute-done | bytes 131104 | tf_op jit(solution)/shard_map/ppermute | solution.py:21
  81.7 2.8 %hidden.4 = (f32[924,256]{1,0:T(8,128)S(1)}, f32[924,256]{1,0:T(8,128)S(1)}, f32[256,128]{1,0:T(8,128)S(1)}) custom-call(s32[2]{0:T(128)S(1)} %pad_add_fusion.place, bf16[64,1024]{1,0:T(8,128)(2,1)S(1)} %state.1.refs_0_, bf16[192,1024]{1,0:T(8,128)(2,1)S(1)} %stack.23.refs_1_, bf16[64,1024]{1,0:T(8,128)(2,1)S(1)} %collective-permute-done.31.refs_2_, ...), custom_call_target="tpu_custom_call" | custom-call | flops 1937768448 | tf_op jit(solution)/shard_map/hidden/pallas_call | solution.py:649
  84.5 5.8 %collective-permute-done.30.refs_0_ = bf16[192,1024]{1,0:T(8,128)(2,1)S(1)} collective-permute-done((bf16[192,1024]{1,0:T(8,128)(2,1)S(1)}, bf16[192,1024]{1,0:T(8,128)(2,1)S(1)}, u32[]{:S(2)}, u32[]{:S(2)}) %collective-permute-start.30) | collective-permute-done | bytes 393248 | tf_op jit(solution)/shard_map/ppermute | solution.py:21
  94.9 3.0 %hidden.5 = (f32[924,256]{1,0:T(8,128)S(1)}, f32[924,256]{1,0:T(8,128)S(1)}, f32[256,128]{1,0:T(8,128)S(1)}) custom-call(s32[2]{0:T(128)S(1)} %pad_add_fusion.place, bf16[64,1024]{1,0:T(8,128)(2,1)S(1)} %collective-permute-done.24.refs_3_.refs_0_, bf16[192,1024]{1,0:T(8,128)(2,1)S(1)} %stack.24.source.refs_1_, ...), custom_call_target="tpu_custom_call", output_to_operand_aliasing={{0}: (10, {}), {1}: (11, {})} | custom-call | flops 1937768448 | tf_op jit(solution)/shard_map/hidden/pallas_call | solution.py:649
  97.9 3.0 %hidden.6 = (f32[924,256]{1,0:T(8,128)S(1)}, f32[924,256]{1,0:T(8,128)S(1)}, f32[256,128]{1,0:T(8,128)S(1)}) custom-call(s32[2]{0:T(128)S(1)} %pad_add_fusion.place, bf16[64,1024]{1,0:T(8,128)(2,1)S(1)} %collective-permute-done.29.refs_4_.refs_0_, bf16[192,1024]{1,0:T(8,128)(2,1)S(1)} %stack.25.refs_1_.source, ...), custom_call_target="tpu_custom_call", output_to_operand_aliasing={{0}: (10, {}), {1}: (11, {})} | custom-call | flops 1937768448 | tf_op jit(solution)/shard_map/hidden/pallas_call | solution.py:649
  102.9 3.9 %hidden.7 = (bf16[256,924]{1,0:T(8,128)(2,1)S(1)}, bf16[256,1024]{1,0:T(8,128)(2,1)S(1)}) custom-call(s32[2]{0:T(128)S(1)} %pad_add_fusion.place, bf16[64,1024]{1,0:T(8,128)(2,1)S(1)} %collective-permute-done.25.refs_5_.refs_0_, bf16[96,1024]{1,0:T(8,128)(2,1)S(1)} %stack.26.refs_1_, bf16[96,1024]{1,0:T(8,128)(2,1)S(1)} %stack.27.refs_2_, ...), custom_call_target="tpu_custom_call" | custom-call | flops 1937768448 | tf_op jit(solution)/shard_map/hidden/pallas_call | solution.py:649
  114.1 5.3 %collective-permute-done.46.refs_0_ = bf16[128,1024]{1,0:T(8,128)(2,1)S(1)} collective-permute-done((bf16[128,1024]{1,0:T(8,128)(2,1)S(1)}, bf16[128,1024]{1,0:T(8,128)(2,1)S(1)}, u32[]{:S(2)}, u32[]{:S(2)}) %collective-permute-start.46) | collective-permute-done | bytes 262176 | tf_op jit(solution)/shard_map/ppermute | solution.py:21
  124.0 4.9 %collective-permute-done.51.refs_1_ = bf16[128,1024]{1,0:T(8,128)(2,1)S(1)} collective-permute-done((bf16[128,1024]{1,0:T(8,128)(2,1)S(1)}, bf16[128,1024]{1,0:T(8,128)(2,1)S(1)}, u32[]{:S(2)}, u32[]{:S(2)}) %collective-permute-start.51) | collective-permute-done | bytes 262176 | tf_op jit(solution)/shard_map/ppermute | solution.py:21
  129.9 2.4 %collective-permute-start.53 = (bf16[64,1024]{1,0:T(8,128)(2,1)S(1)}, bf16[64,1024]{1,0:T(8,128)(2,1)S(1)}, u32[]{:S(2)}, u32[]{:S(2)}) collective-permute-start(bf16[64,1024]{1,0:T(8,128)(2,1)S(1)} %get-tuple-element.152), channel_id=1, source_target_pairs={{0,3},{1,2},{2,1},{3,0},{4,7},{5,6},{6,5},{7,4},{8,11},{9,10},{10,... | collective-permute-start | bytes 393224 | tf_op jit(solution)/shard_map/ppermute | solution.py:21
  134.5 3.6 %collective-permute-done.53 = bf16[64,1024]{1,0:T(8,128)(2,1)S(1)} collective-permute-done((bf16[64,1024]{1,0:T(8,128)(2,1)S(1)}, bf16[64,1024]{1,0:T(8,128)(2,1)S(1)}, u32[]{:S(2)}, u32[]{:S(2)}) %collective-permute-start.53) | collective-permute-done | bytes 131104 | tf_op jit(solution)/shard_map/ppermute | solution.py:21
  138.1 2.5 %collective-permute-done.54 = bf16[64,1024]{1,0:T(8,128)(2,1)S(1)} collective-permute-done((bf16[64,1024]{1,0:T(8,128)(2,1)S(1)}, bf16[64,1024]{1,0:T(8,128)(2,1)S(1)}, u32[]{:S(2)}, u32[]{:S(2)}) %collective-permute-start.54) | collective-permute-done | bytes 131104 | tf_op jit(solution)/shard_map/ppermute | solution.py:21
  (130 shorter events, 48.1 us)
Async XLA Ops:
  1.8 10.0 %collective-permute-start.1 = (bf16[544,128]{1,0:T(8,128)(2,1)S(1)}, bf16[544,128]{1,0:T(8,128)(2,1)S(1)}, u32[]{:S(2)}, u32[]{:S(2)}) collective-permute-start(bf16[544,128]{1,0:T(8,128)(2,1)S(1)} %pack.1.refs_0_.queries), channel_id=1, source_target_pairs={{0,16},{4,20},{8,24},{12,28},{16,0},{20,4},{24,8},{28,12},{1,17},{... | collective-permute-start | bytes 417800 | tf_op jit(solution)/shard_map/ppermute | solution.py:21
  26.4 9.6 %collective-permute-start.11 = (bf16[544,128]{1,0:T(8,128)(2,1)S(1)}, bf16[544,128]{1,0:T(8,128)(2,1)S(1)}, u32[]{:S(2)}, u32[]{:S(2)}) collective-permute-start(bf16[544,128]{1,0:T(8,128)(2,1)S(1)} %get-tuple-element.94), channel_id=1, source_target_pairs={{0,8},{4,12},{8,0},{12,4},{16,24},{20,28},{24,16},{28,20},{1,9},{5... | collective-permute-start | bytes 417800 | tf_op jit(solution)/shard_map/ppermute | solution.py:21
  28.4 8.5 %collective-permute-start.12 = (bf16[544,128]{1,0:T(8,128)(2,1)S(1)}, bf16[544,128]{1,0:T(8,128)(2,1)S(1)}, u32[]{:S(2)}, u32[]{:S(2)}) collective-permute-start(bf16[544,128]{1,0:T(8,128)(2,1)S(1)} %get-tuple-element.95), channel_id=1, source_target_pairs={{0,16},{4,20},{8,24},{12,28},{16,0},{20,4},{24,8},{28,12},{1,17},{... | collective-permute-start | bytes 417800 | tf_op jit(solution)/shard_map/ppermute | solution.py:21
  38.8 7.8 %collective-permute-start.15 = (bf16[32,2048]{1,0:T(8,128)(2,1)S(1)}, bf16[32,2048]{1,0:T(8,128)(2,1)S(1)}, u32[]{:S(2)}, u32[]{:S(2)}) collective-permute-start(bf16[32,2048]{1,0:T(8,128)(2,1)S(1)} %combine.1.refs_0_), channel_id=1, source_target_pairs={{0,16},{4,20},{8,24},{12,28},{16,0},{20,4},{24,8},{28,12},{1,17},{... | collective-permute-start | bytes 393224 | tf_op jit(solution)/shard_map/ppermute | solution.py:21
  49.9 13.9 %collective-permute-start.21 = (bf16[64,1024]{1,0:T(8,128)(2,1)S(1)}, bf16[64,1024]{1,0:T(8,128)(2,1)S(1)}, u32[]{:S(2)}, u32[]{:S(2)}) collective-permute-start(bf16[64,1024]{1,0:T(8,128)(2,1)S(1)} %get-tuple-element.100), channel_id=1, source_target_pairs={{0,3},{1,2},{2,1},{3,0},{4,7},{5,6},{6,5},{7,4},{8,11},{9,10},{10,... | collective-permute-start | bytes 393224 | tf_op jit(solution)/shard_map/ppermute | solution.py:21
  53.6 11.6 %collective-permute-start.22 = (bf16[64,1024]{1,0:T(8,128)(2,1)S(1)}, bf16[64,1024]{1,0:T(8,128)(2,1)S(1)}, u32[]{:S(2)}, u32[]{:S(2)}) collective-permute-start(bf16[64,1024]{1,0:T(8,128)(2,1)S(1)} %get-tuple-element.101), channel_id=1, source_target_pairs={{0,2},{1,3},{2,0},{3,1},{4,6},{5,7},{6,4},{7,5},{8,10},{9,11},{10,... | collective-permute-start | bytes 393224 | tf_op jit(solution)/shard_map/ppermute | solution.py:21
  53.6 11.6 %collective-permute-start.23 = (bf16[64,1024]{1,0:T(8,128)(2,1)S(1)}, bf16[64,1024]{1,0:T(8,128)(2,1)S(1)}, u32[]{:S(2)}, u32[]{:S(2)}) collective-permute-start(bf16[64,1024]{1,0:T(8,128)(2,1)S(1)} %get-tuple-element.102), channel_id=1, source_target_pairs={{0,1},{1,0},{2,3},{3,2},{4,5},{5,4},{6,7},{7,6},{8,9},{9,8},{10,11... | collective-permute-start | bytes 393224 | tf_op jit(solution)/shard_map/ppermute | solution.py:21
  65.7 8.2 %collective-permute-start.26 = (bf16[64,1024]{1,0:T(8,128)(2,1)S(1)}, bf16[64,1024]{1,0:T(8,128)(2,1)S(1)}, u32[]{:S(2)}, u32[]{:S(2)}) collective-permute-start(bf16[64,1024]{1,0:T(8,128)(2,1)S(1)} %state.1.refs_0_), channel_id=1, source_target_pairs={{0,3},{1,2},{2,1},{3,0},{4,7},{5,6},{6,5},{7,4},{8,11},{9,10},{10,... | collective-permute-start | bytes 393224 | tf_op jit(solution)/shard_map/ppermute | solution.py:21
  68.2 10.4 %collective-permute-start.27 = (bf16[64,1024]{1,0:T(8,128)(2,1)S(1)}, bf16[64,1024]{1,0:T(8,128)(2,1)S(1)}, u32[]{:S(2)}, u32[]{:S(2)}) collective-permute-start(bf16[64,1024]{1,0:T(8,128)(2,1)S(1)} %state.1.refs_0_), channel_id=1, source_target_pairs={{0,2},{1,3},{2,0},{3,1},{4,6},{5,7},{6,4},{7,5},{8,10},{9,11},{10,... | collective-permute-start | bytes 393224 | tf_op jit(solution)/shard_map/ppermute | solution.py:21
  68.2 10.4 %collective-permute-start.28 = (bf16[64,1024]{1,0:T(8,128)(2,1)S(1)}, bf16[64,1024]{1,0:T(8,128)(2,1)S(1)}, u32[]{:S(2)}, u32[]{:S(2)}) collective-permute-start(bf16[64,1024]{1,0:T(8,128)(2,1)S(1)} %state.1.refs_0_), channel_id=1, source_target_pairs={{0,1},{1,0},{2,3},{3,2},{4,5},{5,4},{6,7},{7,6},{8,9},{9,8},{10,11... | collective-permute-start | bytes 393224 | tf_op jit(solution)/shard_map/ppermute | solution.py:21
  70.1 8.5 %collective-permute-start.29 = (bf16[64,1024]{1,0:T(8,128)(2,1)S(1)}, bf16[64,1024]{1,0:T(8,128)(2,1)S(1)}, u32[]{:S(2)}, u32[]{:S(2)}) collective-permute-start(bf16[64,1024]{1,0:T(8,128)(2,1)S(1)} %state.1.refs_0_), channel_id=1, source_target_pairs={{0,16},{4,20},{8,24},{12,28},{16,0},{20,4},{24,8},{28,12},{1,17},{... | collective-permute-start | bytes 393224 | tf_op jit(solution)/shard_map/ppermute | solution.py:21
  78.8 11.5 %collective-permute-start.30 = (bf16[192,1024]{1,0:T(8,128)(2,1)S(1)}, bf16[192,1024]{1,0:T(8,128)(2,1)S(1)}, u32[]{:S(2)}, u32[]{:S(2)}) collective-permute-start(bf16[192,1024]{1,0:T(8,128)(2,1)S(1)} %stack.23.refs_1_), channel_id=1, source_target_pairs={{0,8},{4,12},{8,0},{12,4},{16,24},{20,28},{24,16},{28,20},{1,9},{5... | collective-permute-start | bytes 1179656 | tf_op jit(solution)/shard_map/ppermute | solution.py:21
  80.5 11.4 %collective-permute-start.34 = (bf16[192,1024]{1,0:T(8,128)(2,1)S(1)}, bf16[192,1024]{1,0:T(8,128)(2,1)S(1)}, u32[]{:S(2)}, u32[]{:S(2)}) collective-permute-start(bf16[192,1024]{1,0:T(8,128)(2,1)S(1)} %stack.23.refs_1_), channel_id=1, source_target_pairs={{0,16},{4,20},{8,24},{12,28},{16,0},{20,4},{24,8},{28,12},{1,17},{... | collective-permute-start | bytes 1179656 | tf_op jit(solution)/shard_map/ppermute | solution.py:21
  92.6 8.3 %collective-permute-start.39 = (bf16[96,1024]{1,0:T(8,128)(2,1)S(1)}, bf16[96,1024]{1,0:T(8,128)(2,1)S(1)}, u32[]{:S(2)}, u32[]{:S(2)}) collective-permute-start(bf16[96,1024]{1,0:T(8,128)(2,1)S(1)} %rows.3), channel_id=1, source_target_pairs={{0,8},{4,12},{8,0},{12,4},{16,24},{20,28},{24,16},{28,20},{1,9},{5... | collective-permute-start | bytes 589832 | tf_op jit(solution)/shard_map/ppermute | solution.py:21
  110.6 9.8 %collective-permute-start.48 = (bf16[256,1024]{1,0:T(8,128)(2,1)S(1)}, bf16[256,1024]{1,0:T(8,128)(2,1)S(1)}, u32[]{:S(2)}, u32[]{:S(2)}) collective-permute-start(bf16[256,1024]{1,0:T(8,128)(2,1)S(1)} %get-tuple-element.146), channel_id=1, source_target_pairs={{0,4},{4,0},{8,12},{12,8},{16,20},{20,16},{24,28},{28,24},{1,5},{5... | collective-permute-start | bytes 1572872 | tf_op jit(solution)/shard_map/ppermute | solution.py:21
  110.9 8.4 %collective-permute-start.46 = (bf16[128,1024]{1,0:T(8,128)(2,1)S(1)}, bf16[128,1024]{1,0:T(8,128)(2,1)S(1)}, u32[]{:S(2)}, u32[]{:S(2)}) collective-permute-start(bf16[128,1024]{1,0:T(8,128)(2,1)S(1)} %get-tuple-element.141), channel_id=1, source_target_pairs={{0,16},{4,20},{8,24},{12,28},{16,0},{20,4},{24,8},{28,12},{1,17},{... | collective-permute-start | bytes 786440 | tf_op jit(solution)/shard_map/ppermute | solution.py:21
  111.9 8.5 %collective-permute-start.49 = (bf16[128,1024]{1,0:T(8,128)(2,1)S(1)}, bf16[128,1024]{1,0:T(8,128)(2,1)S(1)}, u32[]{:S(2)}, u32[]{:S(2)}) collective-permute-start(bf16[128,1024]{1,0:T(8,128)(2,1)S(1)} %get-tuple-element.135.refs_2_), channel_id=1, source_target_pairs={{0,8},{4,12},{8,0},{12,4},{16,24},{20,28},{24,16},{28,20},{1,9},{5... | collective-permute-start | bytes 786440 | tf_op jit(solution)/shard_map/ppermute | solution.py:21
  114.0 9.9 %collective-permute-start.44 = (bf16[256,1024]{1,0:T(8,128)(2,1)S(1)}, bf16[256,1024]{1,0:T(8,128)(2,1)S(1)}, u32[]{:S(2)}, u32[]{:S(2)}) collective-permute-start(bf16[256,1024]{1,0:T(8,128)(2,1)S(1)} %get-tuple-element.137), channel_id=1, source_target_pairs={{0,4},{4,0},{8,12},{12,8},{16,20},{20,16},{24,28},{28,24},{1,5},{5... | collective-permute-start | bytes 1572872 | tf_op jit(solution)/shard_map/ppermute | solution.py:21
  119.5 9.3 %collective-permute-start.51 = (bf16[128,1024]{1,0:T(8,128)(2,1)S(1)}, bf16[128,1024]{1,0:T(8,128)(2,1)S(1)}, u32[]{:S(2)}, u32[]{:S(2)}) collective-permute-start(bf16[128,1024]{1,0:T(8,128)(2,1)S(1)} %get-tuple-element.150), channel_id=1, source_target_pairs={{0,8},{4,12},{8,0},{12,4},{16,24},{20,28},{24,16},{28,20},{1,9},{5... | collective-permute-start | bytes 786440 | tf_op jit(solution)/shard_map/ppermute | solution.py:21
  120.6 9.3 %collective-permute-start.52 = (bf16[128,1024]{1,0:T(8,128)(2,1)S(1)}, bf16[128,1024]{1,0:T(8,128)(2,1)S(1)}, u32[]{:S(2)}, u32[]{:S(2)}) collective-permute-start(bf16[128,1024]{1,0:T(8,128)(2,1)S(1)} %get-tuple-element.151), channel_id=1, source_target_pairs={{0,16},{4,20},{8,24},{12,28},{16,0},{20,4},{24,8},{28,12},{1,17},{... | collective-permute-start | bytes 786440 | tf_op jit(solution)/shard_map/ppermute | solution.py:21
  121.6 11.2 %collective-permute-start.47 = (bf16[128,1024]{1,0:T(8,128)(2,1)S(1)}, bf16[128,1024]{1,0:T(8,128)(2,1)S(1)}, u32[]{:S(2)}, u32[]{:S(2)}) collective-permute-start(bf16[128,1024]{1,0:T(8,128)(2,1)S(1)} %get-tuple-element.142), channel_id=1, source_target_pairs={{0,8},{4,12},{8,0},{12,4},{16,24},{20,28},{24,16},{28,20},{1,9},{5... | collective-permute-start | bytes 786440 | tf_op jit(solution)/shard_map/ppermute | solution.py:21
  122.8 10.8 %collective-permute-start.50 = (bf16[128,1024]{1,0:T(8,128)(2,1)S(1)}, bf16[128,1024]{1,0:T(8,128)(2,1)S(1)}, u32[]{:S(2)}, u32[]{:S(2)}) collective-permute-start(bf16[128,1024]{1,0:T(8,128)(2,1)S(1)} %get-tuple-element.147), channel_id=1, source_target_pairs={{0,16},{4,20},{8,24},{12,28},{16,0},{20,4},{24,8},{28,12},{1,17},{... | collective-permute-start | bytes 786440 | tf_op jit(solution)/shard_map/ppermute | solution.py:21
  129.9 8.2 %collective-permute-start.53 = (bf16[64,1024]{1,0:T(8,128)(2,1)S(1)}, bf16[64,1024]{1,0:T(8,128)(2,1)S(1)}, u32[]{:S(2)}, u32[]{:S(2)}) collective-permute-start(bf16[64,1024]{1,0:T(8,128)(2,1)S(1)} %get-tuple-element.152), channel_id=1, source_target_pairs={{0,3},{1,2},{2,1},{3,0},{4,7},{5,6},{6,5},{7,4},{8,11},{9,10},{10,... | collective-permute-start | bytes 393224 | tf_op jit(solution)/shard_map/ppermute | solution.py:21
  132.4 8.3 %collective-permute-start.54 = (bf16[64,1024]{1,0:T(8,128)(2,1)S(1)}, bf16[64,1024]{1,0:T(8,128)(2,1)S(1)}, u32[]{:S(2)}, u32[]{:S(2)}) collective-permute-start(bf16[64,1024]{1,0:T(8,128)(2,1)S(1)} %get-tuple-element.153), channel_id=1, source_target_pairs={{0,2},{1,3},{2,0},{3,1},{4,6},{5,7},{6,4},{7,5},{8,10},{9,11},{10,... | collective-permute-start | bytes 393224 | tf_op jit(solution)/shard_map/ppermute | solution.py:21
  (35 other events, 147.1 us)
